TPU v7x, 32 devices: a whole 2x2x4 slice. The times are simulated.
32 devices in a mesh: dp: 16 (over z, y, x), mp: 2 (over core).
Axes of the slice: x: 2, y: 2, z: 4, core: 2. Of those that a mesh axis runs over, the one named last changes fastest.
Arguments:
- tokens: bfloat16 [32768, 1472], P('dp', 'mp'), may hold values from -6 to 6
- cotangent: bfloat16 [32768, 1472], P('dp', 'mp'), may hold values from -6 to 6
- lengths: int32 [32], P('dp'), may hold values from 512 to 1024, as said below
- keep_mask: int32 [32768], P('dp'), may hold values from 0 to 1, as said below
- ln_attn: float32 [1472], replicated, may hold values from 0.1 to 1.9
- w_query: bfloat16 [1472, 384], P(None, 'mp'), may hold values from -0.15625 to 0.15625
- w_key: bfloat16 [1472, 384], P(None, 'mp'), may hold values from -0.15625 to 0.15625
- w_value: bfloat16 [1472, 384], P(None, 'mp'), may hold values from -0.15625 to 0.15625
- w_attn_out: bfloat16 [384, 1472], P('mp'), may hold values from -1.75 to 1.75
- rel_table: float32 [32, 6], P(None, 'mp'), may hold values from -4 to 4
- w_delete: bfloat16 [1472], replicated, may hold values from -0.15625 to 0.15625
- ln_ffn: float32 [1472], replicated, may hold values from 0.1 to 1.9
- w_gate: bfloat16 [1472, 3584], P(None, 'mp'), may hold values from -0.15625 to 0.15625
- w_up: bfloat16 [1472, 3584], P(None, 'mp'), may hold values from -0.15625 to 0.15625
- w_ffn_out: bfloat16 [3584, 1472], P('mp'), may hold values from -0.09375 to 0.09375
Outputs:
- mixed: bfloat16 [32768, 1472], P('dp', 'mp')
- grad_tokens: bfloat16 [32768, 1472], P('dp', 'mp')
- grad_ln_attn: float32 [1472], P('mp')
- grad_w_query: float32 [1472, 384], P(None, 'mp')
- grad_w_key: float32 [1472, 384], P(None, 'mp')
- grad_w_value: float32 [1472, 384], P(None, 'mp')
- grad_w_attn_out: float32 [384, 1472], P('mp')
- grad_rel_table: float32 [32, 6], P(None, 'mp')
- grad_w_delete: float32 [1472], replicated
- grad_ln_ffn: float32 [1472], P('mp')
- grad_w_gate: float32 [1472, 3584], P(None, ('mp', 'dp'))
- grad_w_up: float32 [1472, 3584], P(None, ('mp', 'dp'))
- grad_w_ffn_out: float32 [3584, 1472], P(('mp', 'dp'))
Inputs may be any that keep to these rules, and one draw needn't show every extreme that they name: `lengths`: on one index of dp every item has length 1024. `keep_mask`: zero on every padding row; exactly 16384 ones in all; on one index of dp every one of its 2048 rows is kept.
All inputs are finite; a program needn't handle non-finite values.
Results may differ from a plain program's by a relative error of at most 0.015.
Values may be sent and summed in bfloat16 or wider, within the bound.
A program may use at most 448 MiB of HBM per device.

v0:
```python
import functools

import jax
import jax.numpy as jnp
import numpy as np
from jax import lax
from jax.experimental import pallas as pl
from jax.experimental.pallas import tpu as pltpu
from jax.sharding import PartitionSpec as P

D = 1472
HDIM = 64
BUCKETS = 32
LMAX = 1024
ROWS_DEV = 2048

EPSILON = 1e-06
DELETE_DEPTH = 4.0
NEG_LARGE = -1e30
NEAR_STEPS = (1, 2, 3, 4, 5, 6, 7, 8, 12, 16, 23, 32, 46, 64, 91)
TILE = 128
QBLOCK = 256
AUG = 16
F32 = jnp.float32
BF16 = jnp.bfloat16
GELU_C = float(np.sqrt(2.0 / np.pi))

NN = (((1,), (0,)), ((), ()))
TN = (((0,), (0,)), ((), ()))
NT = (((1,), (1,)), ((), ()))


def dot(a, b, dims):
    return lax.dot_general(a, b, dims, preferred_element_type=F32)


def call(kernel, name, flops, nbytes, **kw):
    return pl.pallas_call(
        kernel,
        name=name,
        cost_estimate=pl.CostEstimate(
            flops=int(flops), bytes_accessed=int(nbytes), transcendentals=0
        ),
        compiler_params=pltpu.CompilerParams(vmem_limit_bytes=56 << 20),
        **kw,
    )


VMEM = pl.BlockSpec(memory_space=pltpu.VMEM)
SMEM = pl.BlockSpec(memory_space=pltpu.SMEM)


def compact_kernel(part_ref, slot_ref, x_ref, own_ref, peer_ref):
    part = part_ref[0]
    for which, out_ref in ((0, own_ref), (1, peer_ref)):
        item = part if which == 0 else 1 - part
        for block in range(LMAX // QBLOCK):
            width = ROWS_DEV - 512 - block * QBLOCK
            start = pl.multiple_of(item * 512 + block * QBLOCK, 128)
            ids = item * LMAX + block * QBLOCK + lax.broadcasted_iota(jnp.int32, (QBLOCK, 1), 0)
            hot = (slot_ref[:, pl.ds(start, width)] == ids).astype(F32).astype(BF16)
            rows = dot(x_ref[:, pl.ds(start, width)], hot, NT)
            out_ref[:, block * QBLOCK : (block + 1) * QBLOCK] = rows.astype(BF16)


def compact(part, slot, columns):
    width = columns.shape[0]
    shape = jax.ShapeDtypeStruct((width, LMAX), BF16)
    return call(
        compact_kernel,
        "compact",
        2 * width * 2 * 4608 * 256,
        width * 2048 * 4,
        in_specs=[SMEM, VMEM, VMEM],
        out_specs=[VMEM, VMEM],
        out_shape=[shape, shape],
    )(part, slot, columns)


def spread_kernel(part_ref, slot_ref, own_ref, peer_ref, out_ref):
    first = part_ref[0] == 0
    items = (
        jnp.where(first, own_ref[...], peer_ref[...]),
        jnp.where(first, peer_ref[...], own_ref[...]),
    )
    for block in range(ROWS_DEV // QBLOCK):
        end = (block + 1) * QBLOCK
        slots = slot_ref[:, end - QBLOCK : end]
        total = None
        for item in range(2):
            reach = min(end - 512 * item, LMAX)
            if reach <= 0 or (item == 0 and end > LMAX):
                continue
            ids = item * LMAX + lax.broadcasted_iota(jnp.int32, (reach, 1), 0)
            hot = (slots == ids).astype(F32).astype(BF16)
            part = dot(items[item][:, :reach], hot, NN)
            total = part if total is None else total + part
        out_ref[:, end - QBLOCK : end] = total.astype(BF16)


def spread(part, slot, own, peer):
    width = own.shape[0]
    return call(
        spread_kernel,
        "spread",
        2 * width * 7168 * 256,
        width * 2048 * 4,
        in_specs=[SMEM, VMEM, VMEM, VMEM],
        out_specs=VMEM,
        out_shape=jax.ShapeDtypeStruct((width, ROWS_DEV), BF16),
    )(part, slot, own, peer)


STRIP = LMAX + LMAX - TILE


def offsets(shift):
    keys = lax.broadcasted_iota(jnp.int32, (TILE, TILE), 0)
    queries = lax.broadcasted_iota(jnp.int32, (TILE, TILE), 1)
    return shift * TILE + keys - queries


def strip_kernel(table_ref, strip_ref):
    head = pl.program_id(0)
    middle = LMAX - TILE

    def value(bucket):
        return table_ref[bucket, head]

    def side(distance, base, start):
        tile = jnp.full((TILE, TILE), start, F32)
        for count, step in enumerate(NEAR_STEPS):
            tile = jnp.where(distance >= step, value(base + count + 1), tile)
        return tile

    strip_ref[0, : middle - TILE, :] = jnp.full((middle - TILE, TILE), value(15), F32)
    strip_ref[0, middle + 2 * TILE :, :] = jnp.full((STRIP - middle - 2 * TILE, TILE), value(31), F32)
    before = offsets(-1)
    strip_ref[0, middle - TILE : middle, :] = side(-before, 0, value(0))
    relative = offsets(0)
    strip_ref[0, middle : middle + TILE, :] = jnp.where(
        relative > 0, side(relative, 16, value(0)), side(-relative, 0, value(0))
    )
    after = offsets(1)
    strip_ref[0, middle + TILE : middle + 2 * TILE, :] = side(after, 16, value(0))


def bias_strip(table, heads):
    return call(
        strip_kernel,
        "bias_strip",
        heads * 3e6,
        heads * STRIP * TILE * 4,
        grid=(heads,),
        in_specs=[SMEM],
        out_specs=pl.BlockSpec((1, STRIP, TILE), lambda h: (h, 0, 0)),
        out_shape=jax.ShapeDtypeStruct((heads, STRIP, TILE), F32),
    )(table)


def attend_kernel(q_ref, k_ref, v_ref, gate_ref, strip_ref, prob_ref, out_ref):
    ones = (lax.broadcasted_iota(jnp.int32, (AUG, LMAX), 0) == 0).astype(F32).astype(BF16)
    scale = HDIM ** (-0.5)
    queries = jnp.concatenate([(q_ref[...].astype(F32) * scale).astype(BF16), ones], axis=0)
    keys = jnp.concatenate([k_ref[...], gate_ref[...]], axis=0)
    for block in range(LMAX // QBLOCK):
        low = block * QBLOCK
        scores = dot(keys, queries[:, low : low + QBLOCK], TN)
        bias = []
        for sub in range(QBLOCK // TILE):
            start = LMAX - TILE - (low + sub * TILE)
            bias.append(strip_ref[0, start : start + LMAX, :])
        scores = scores + jnp.concatenate(bias, axis=1)
        top = jnp.max(scores, axis=0, keepdims=True)
        weights = jnp.exp(scores - top)
        total = jnp.sum(weights, axis=0, keepdims=True)
        prob = (weights * (1.0 / total)).astype(BF16)
        prob_ref[0, :, low : low + QBLOCK] = prob
        out_ref[:, low : low + QBLOCK] = dot(v_ref[...], prob, NN).astype(BF16)


def attend(qkv, gate, strip, heads):
    return call(
        attend_kernel,
        "attend",
        heads * 4 * LMAX * LMAX * HDIM * 4,
        heads * LMAX * LMAX * 2,
        grid=(heads,),
        in_specs=[
            pl.BlockSpec((HDIM, LMAX), lambda h: (h, 0)),
            pl.BlockSpec((HDIM, LMAX), lambda h: (heads + h, 0)),
            pl.BlockSpec((HDIM, LMAX), lambda h: (2 * heads + h, 0)),
            pl.BlockSpec((AUG, LMAX), lambda h: (0, 0)),
            pl.BlockSpec((1, STRIP, TILE), lambda h: (h, 0, 0)),
        ],
        out_specs=[
            pl.BlockSpec((1, LMAX, LMAX), lambda h: (h, 0, 0)),
            pl.BlockSpec((HDIM, LMAX), lambda h: (h, 0)),
        ],
        out_shape=[
            jax.ShapeDtypeStruct((heads, LMAX, LMAX), BF16),
            jax.ShapeDtypeStruct((heads * HDIM, LMAX), BF16),
        ],
    )(qkv, qkv, qkv, gate, strip)


def attend_back_kernel(
    q_ref, k_ref, v_ref, prob_ref, go_ref, gq_ref, gk_ref, gv_ref, sums_ref, near_ref
):
    scale = HDIM ** (-0.5)
    blocks = LMAX // TILE
    member = (
        lax.broadcasted_iota(jnp.int32, (AUG, LMAX), 0)
        == lax.broadcasted_iota(jnp.int32, (AUG, LMAX), 1) // TILE
    )
    queries = jnp.concatenate([q_ref[...], member.astype(F32).astype(BF16)], axis=0)
    near = [jnp.zeros((TILE, TILE), F32) for _ in range(3)]
    key_total = jnp.zeros((HDIM + AUG, LMAX), F32)
    val_total = jnp.zeros((HDIM, LMAX), F32)
    for block in range(LMAX // QBLOCK):
        low = block * QBLOCK
        prob = prob_ref[0, :, low : low + QBLOCK]
        grad_out = go_ref[:, low : low + QBLOCK]
        soft = prob.astype(F32)
        grad_prob = dot(v_ref[...], grad_out, TN)
        inner = jnp.sum(soft * grad_prob, axis=0, keepdims=True)
        grad_scores = (soft * (grad_prob - inner)).astype(BF16)
        gq_ref[:, low : low + QBLOCK] = (dot(k_ref[...], grad_scores, NN) * scale).astype(BF16)
        key_total = key_total + dot(queries[:, low : low + QBLOCK], grad_scores, NT)
        val_total = val_total + dot(grad_out, prob, NT)
        for sub in range(QBLOCK // TILE):
            place = block * (QBLOCK // TILE) + sub
            for shift in (-1, 0, 1):
                at = place + shift
                if 0 <= at < blocks:
                    piece = grad_scores[at * TILE : (at + 1) * TILE, sub * TILE : (sub + 1) * TILE]
                    near[shift + 1] = near[shift + 1] + piece.astype(F32)
    gk_ref[...] = (key_total[:HDIM] * scale).astype(BF16)
    gv_ref[...] = val_total.astype(BF16)
    sums_ref[0] = key_total[HDIM : HDIM + blocks]

    def fold(tile):
        return jnp.sum(tile.reshape(TILE // 8, 8, TILE), axis=0)

    before, same, after = near
    for sign, base, other, shift in ((-1, 0, before, -1), (1, 16, after, 1)):
        near_offset = sign * offsets(0)
        far_offset = sign * offsets(shift)
        floor = 0 if sign < 0 else 1
        last = fold(jnp.where(near_offset >= floor, same, 0.0)) + fold(
            jnp.where(far_offset >= floor, other, 0.0)
        )
        for count, step in enumerate(NEAR_STEPS):
            following = fold(jnp.where(near_offset >= step, same, 0.0)) + fold(
                jnp.where(far_offset >= step, other, 0.0)
            )
            near_ref[0, base + count] = last - following
            last = following
        near_ref[0, base + 15] = last


def attend_back(qkv, prob, grad_attended, heads):
    blocks = LMAX // TILE
    rows = jax.ShapeDtypeStruct((heads * HDIM, LMAX), BF16)
    spec = pl.BlockSpec((HDIM, LMAX), lambda h: (h, 0))
    return call(
        attend_back_kernel,
        "attend_back",
        heads * 8 * LMAX * LMAX * HDIM * 4,
        heads * LMAX * LMAX * 2,
        grid=(heads,),
        in_specs=[
            spec,
            pl.BlockSpec((HDIM, LMAX), lambda h: (heads + h, 0)),
            pl.BlockSpec((HDIM, LMAX), lambda h: (2 * heads + h, 0)),
            pl.BlockSpec((1, LMAX, LMAX), lambda h: (h, 0, 0)),
            spec,
        ],
        out_specs=[
            spec,
            spec,
            spec,
            pl.BlockSpec((1, blocks, LMAX), lambda h: (h, 0, 0)),
            pl.BlockSpec((1, BUCKETS, 8, TILE), lambda h: (h, 0, 0, 0)),
        ],
        out_shape=[
            rows,
            rows,
            rows,
            jax.ShapeDtypeStruct((heads, blocks, LMAX), F32),
            jax.ShapeDtypeStruct((heads, BUCKETS, 8, TILE), F32),
        ],
    )(qkv, qkv, qkv, prob, grad_attended)


def ffn_kernel(gate_ref, up_ref, down_ref, x_ref, cot_ref, hid_ref, gg_ref, gu_ref):
    gate = dot(gate_ref[...], x_ref[...], TN)
    up = dot(up_ref[...], x_ref[...], TN)
    grad = dot(down_ref[...], cot_ref[...], TN)
    square = gate * gate
    bend = jnp.tanh(GELU_C * gate * (1.0 + 0.044715 * square))
    half = 0.5 * (1.0 + bend)
    gelu = gate * half
    slope = half + 0.5 * gate * (1.0 - bend * bend) * (GELU_C * (1.0 + 3 * 0.044715 * square))
    hid_ref[...] = (gelu * up).astype(BF16)
    gg_ref[...] = (grad * up * slope).astype(BF16)
    gu_ref[...] = (grad * gelu).astype(BF16)


def ffn(w_gate, w_up, w_down_t, normed, cot):
    units = w_gate.shape[1]
    width = 256
    weight = pl.BlockSpec((D, width), lambda i: (0, i))
    whole = pl.BlockSpec((D, LMAX), lambda i: (0, 0))
    out = pl.BlockSpec((width, LMAX), lambda i: (i, 0))
    shape = jax.ShapeDtypeStruct((units, LMAX), BF16)
    return call(
        ffn_kernel,
        "ffn",
        6 * D * units * LMAX,
        3 * D * units * 2 + 2 * D * LMAX * 2 + 3 * units * LMAX * 2,
        grid=(units // width,),
        in_specs=[weight, weight, weight, whole, whole],
        out_specs=[out, out, out],
        out_shape=[shape, shape, shape],
    )(w_gate, w_up, w_down_t, normed, cot)


def weight_grad_kernel(a_own, a_peer, b_own, b_peer, out_ref):
    total = dot(a_own[...], b_own[...], NT) + dot(a_peer[...], b_peer[...], NT)
    out_ref[...] = total.astype(BF16)


def weight_grad(a_own, a_peer, b_own, b_peer):
    units = a_own.shape[0]
    width = 256
    left = pl.BlockSpec((width, LMAX), lambda i: (i, 0))
    whole = pl.BlockSpec((D, LMAX), lambda i: (0, 0))
    return call(
        weight_grad_kernel,
        "weight_grad",
        4 * D * units * LMAX,
        4 * D * LMAX + 4 * units * LMAX + 2 * units * D,
        grid=(units // width,),
        in_specs=[left, left, whole, whole],
        out_specs=pl.BlockSpec((width, D), lambda i: (i, 0)),
        out_shape=jax.ShapeDtypeStruct((units, D), BF16),
    )(a_own, a_peer, b_own, b_peer)


def project_kernel(count, *refs):
    total = dot(refs[0][...], refs[count][...], NN)
    for i in range(1, count):
        total = total + dot(refs[i][...], refs[count + i][...], NN)
    refs[-1][...] = total.astype(refs[-1].dtype)


def project(weights, values, dtype):
    count = len(weights)
    units = weights[0].shape[1]
    width = D // 4
    weight = pl.BlockSpec((width, units), lambda i: (i, 0))
    whole = pl.BlockSpec((units, LMAX), lambda i: (0, 0))
    return call(
        functools.partial(project_kernel, count),
        "project",
        2 * count * D * units * LMAX,
        2 * count * (D * units + units * LMAX) + 4 * D * LMAX,
        grid=(D // width,),
        in_specs=[weight] * count + [whole] * count,
        out_specs=pl.BlockSpec((width, LMAX), lambda i: (i, 0)),
        out_shape=jax.ShapeDtypeStruct((D, LMAX), dtype),
    )(*weights, *values)


def halve(values, order):
    size = lax.axis_size("dp")
    bits = size.bit_length() - 1
    index = lax.axis_index("dp")
    rows = values.shape[0] // size
    values = values.reshape((2,) * bits + (rows, values.shape[1]))
    left = list(range(bits - 1, -1, -1))
    for step, bit in enumerate(order):
        axis = left.index(bit)
        left.pop(axis)
        mine = (index >> bit) & 1
        keep = lax.dynamic_index_in_dim(values, mine, axis, keepdims=False)
        give = lax.dynamic_index_in_dim(values, 1 - mine, axis, keepdims=False)
        came = lax.ppermute(give, "dp", [(i, i ^ (1 << bit)) for i in range(size)])
        total = keep.astype(F32) + came.astype(F32)
        values = total if step == bits - 1 else total.astype(BF16)
    return values


def regather(values, order):
    size = lax.axis_size("dp")
    bits = size.bit_length() - 1
    index = lax.axis_index("dp")
    rows, width = values.shape
    have = []
    for bit in order[::-1]:
        came = lax.ppermute(values, "dp", [(i, i ^ (1 << bit)) for i in range(size)])
        axis = sum(1 for b in have if b > bit)
        have.append(bit)
        mine = (index >> bit) & 1
        values = jnp.where(
            mine == 0, jnp.stack([values, came], axis), jnp.stack([came, values], axis)
        )
    return values.reshape(size * rows, width)


def swap(values):
    return lax.ppermute(values, "mp", [(0, 1), (1, 0)])


def body(
    tokens,
    cotangent,
    lengths,
    keep_mask,
    ln_attn,
    w_query,
    w_key,
    w_value,
    w_attn_out,
    rel_table,
    w_delete,
    ln_ffn,
    w_gate,
    w_up,
    w_ffn_out,
):
    dev_count = lax.axis_size("dp")
    bits = dev_count.bit_length() - 1
    part = lax.axis_index("mp")
    inner = 2 * w_query.shape[1]
    heads = inner // HDIM
    half = tokens.shape[1]
    first = part == 0
    part_ref = part.reshape(1).astype(jnp.int32)
    order_one = tuple(range(bits))
    order_two = (1, 0) + tuple(range(2, bits))

    def in_parts(own, peer, axis):
        return jnp.where(
            first, jnp.concatenate([own, peer], axis), jnp.concatenate([peer, own], axis)
        )

    row_ids = jnp.arange(ROWS_DEV, dtype=jnp.int32)
    kept_total = jnp.cumsum(keep_mask)
    in_first = row_ids < lengths[0]
    kept_first = jnp.sum(jnp.where(in_first, keep_mask, 0))
    kept_count = jnp.where(first, kept_first, kept_total[-1] - kept_first)
    rank = kept_total - 1 + jnp.where(in_first, 0, LMAX - kept_first)
    slot = jnp.where(keep_mask > 0, rank, -1).reshape(1, ROWS_DEV)

    own_tokens, peer_tokens = compact(part_ref, slot, tokens.T)
    state_t = in_parts(own_tokens, swap(peer_tokens), 0)
    own_cot, peer_cot = compact(part_ref, slot, cotangent.T)
    cot_own = in_parts(own_cot, swap(peer_cot), 0)
    cot_peer = in_parts(peer_cot, swap(own_cot), 0)

    own_weights = jnp.stack([w_query.T, w_key.T, w_value.T, w_attn_out])
    weights = in_parts(own_weights, swap(own_weights), 1)
    w_qkv = weights[:3].reshape(3 * inner, D)
    w_out = weights[3]
    table = in_parts(rel_table, swap(rel_table), 1)
    strip = bias_strip(table, heads)

    state = state_t.astype(F32)
    scale_one = lax.rsqrt(jnp.mean(state * state, axis=0, keepdims=True) + EPSILON)
    gain_one = ln_attn[:, None]
    normed_one = (state * scale_one * gain_one).astype(BF16)
    qkv = dot(w_qkv, normed_one, NN).astype(BF16)
    del_logit = dot(w_delete.reshape(1, D), normed_one, NN)
    del_gate = (-DELETE_DEPTH * jax.nn.sigmoid(-del_logit)).astype(BF16)
    valid = jnp.arange(LMAX, dtype=jnp.int32)[None, :] < kept_count
    gate_row = jnp.where(valid, del_gate, jnp.asarray(NEG_LARGE, BF16))
    gate_rows = jnp.concatenate([gate_row, jnp.zeros((AUG - 1, LMAX), BF16)], axis=0)
    prob, attended = attend(qkv, gate_rows, strip, heads)

    mid = state + dot(w_out, attended, TN)
    scale_two = lax.rsqrt(jnp.mean(mid * mid, axis=0, keepdims=True) + EPSILON)
    gain_two = ln_ffn[:, None]
    normed_two = (mid * scale_two * gain_two).astype(BF16)
    normed_two_peer = swap(normed_two)
    w_down_t = w_ffn_out.T
    hid_own, gg_own, gu_own = ffn(w_gate, w_up, w_down_t, normed_two, cot_own)
    hid_peer, gg_peer, gu_peer = ffn(w_gate, w_up, w_down_t, normed_two_peer, cot_peer)

    part_down = weight_grad(hid_own, hid_peer, cot_own, cot_peer)
    part_gate = weight_grad(gg_own, gg_peer, normed_two, normed_two_peer)
    part_up = weight_grad(gu_own, gu_peer, normed_two, normed_two_peer)
    grad_down = halve(part_down, order_one)
    grad_gate = halve(part_gate, order_two)
    share = part_up.shape[0] // dev_count
    cut = (share // 2 + 15) // 16 * 16 if share % 16 == 0 else share // 2
    pieces = part_up.reshape(dev_count, share, D)
    grad_up = jnp.concatenate(
        [
            halve(pieces[:, :cut].reshape(-1, D), order_one),
            halve(pieces[:, cut:].reshape(-1, D), order_two),
        ],
        axis=0,
    )

    back_peer = project((w_gate, w_up), (gg_peer, gu_peer), BF16)
    back_own = project((w_gate, w_up), (gg_own, gu_own), F32)
    grad_normed_two = back_own + swap(back_peer).astype(F32)
    weighted_two = grad_normed_two * gain_two
    inner_two = jnp.sum(weighted_two * mid, axis=0, keepdims=True)
    grad_mid = (
        cot_own.astype(F32) + scale_two * weighted_two - mid * (scale_two**3 * inner_two / D)
    )
    grad_ln_ffn = jnp.sum(grad_normed_two * (mid * scale_two), axis=1)
    grad_attn = grad_mid.astype(BF16)
    grad_attended = dot(w_out, grad_attn, NN).astype(BF16)
    grad_w_out = dot(attended, grad_attn, NT)

    grad_q, grad_k, grad_v, sums, near = attend_back(qkv, prob, grad_attended, heads)
    grad_gate_own = jnp.sum(sums, axis=(0, 1))[None, :]
    grad_logit = (
        grad_gate_own * DELETE_DEPTH * jax.nn.sigmoid(del_logit) * jax.nn.sigmoid(-del_logit)
    )
    grad_qkv = jnp.concatenate([grad_q, grad_k, grad_v], axis=0)
    grad_w_qkv = dot(grad_qkv, normed_one, NT)
    grad_w_delete = jnp.sum(normed_one.astype(F32) * grad_logit, axis=1)
    grad_normed_one = dot(w_qkv, grad_qkv, TN) + w_delete.astype(F32)[:, None] * grad_logit
    weighted_one = grad_normed_one * gain_one
    inner_one = jnp.sum(weighted_one * state, axis=0, keepdims=True)
    grad_state = (
        grad_mid + scale_one * weighted_one - state * (scale_one**3 * inner_one / D)
    ).astype(BF16)
    grad_ln_attn = jnp.sum(grad_normed_one * (state * scale_one), axis=1)

    blocks = LMAX // TILE
    tile_sums = jnp.sum(sums.reshape(heads, blocks, blocks, TILE), axis=3)
    block_ids = jnp.arange(blocks)
    shift = block_ids[None, :] - block_ids[:, None]
    far_before = jnp.sum(jnp.where(shift <= -2, tile_sums, 0.0), axis=(1, 2))
    far_after = jnp.sum(jnp.where(shift >= 2, tile_sums, 0.0), axis=(1, 2))
    grad_table = jnp.sum(near, axis=(2, 3)).T
    bucket_ids = jnp.arange(BUCKETS)[:, None]
    grad_table = (
        grad_table
        + jnp.where(bucket_ids == 15, far_before[None, :], 0.0)
        + jnp.where(bucket_ids == 31, far_after[None, :], 0.0)
    )

    small = jnp.concatenate([grad_table.reshape(-1), grad_ln_ffn, grad_ln_attn, grad_w_delete])
    small = lax.psum(small, ("dp", "mp"))
    table_size = BUCKETS * heads
    grad_table = small[:table_size].reshape(BUCKETS, heads)
    grad_ln_ffn = small[table_size : table_size + D]
    grad_ln_attn = small[table_size + D : table_size + 2 * D]
    grad_w_delete = small[table_size + 2 * D :]

    own_rows = inner // 2
    grads = jnp.concatenate([grad_w_qkv, grad_w_out], axis=0).reshape(4, 2, own_rows, D)
    keep = lax.dynamic_index_in_dim(grads, part, 1, keepdims=False)
    give = lax.dynamic_index_in_dim(grads, 1 - part, 1, keepdims=False).astype(BF16)
    both = (keep + swap(give).astype(F32)).astype(BF16).reshape(4 * own_rows, D)
    total = regather(halve(both, order_one).astype(BF16), order_one).astype(F32)
    total = total.reshape(4, own_rows, D)

    mixed_peer = project((w_down_t,), (hid_peer,), BF16)
    mixed_own = project((w_down_t,), (hid_own,), F32)
    mixed = (mid + mixed_own + swap(mixed_peer).astype(F32)).astype(BF16)

    def home(values):
        mine = lax.dynamic_slice_in_dim(values, part * half, half, 0)
        other = lax.dynamic_slice_in_dim(values, (1 - part) * half, half, 0)
        return spread(part_ref, slot, mine, swap(other)).T

    def own_half(values):
        return lax.dynamic_slice_in_dim(values, part * half, half, 0)

    return (
        home(mixed),
        home(grad_state),
        own_half(grad_ln_attn),
        total[0].T,
        total[1].T,
        total[2].T,
        total[3],
        lax.dynamic_slice_in_dim(grad_table, part * (heads // 2), heads // 2, 1),
        grad_w_delete,
        own_half(grad_ln_ffn),
        grad_gate.T,
        grad_up.T,
        grad_down,
    )


def solution(mesh):
    return jax.shard_map(
        body,
        mesh=mesh,
        in_specs=(
            P("dp", "mp"),
            P("dp", "mp"),
            P("dp"),
            P("dp"),
            P(),
            P(None, "mp"),
            P(None, "mp"),
            P(None, "mp"),
            P("mp", None),
            P(None, "mp"),
            P(),
            P(),
            P(None, "mp"),
            P(None, "mp"),
            P("mp", None),
        ),
        out_specs=(
            P("dp", "mp"),
            P("dp", "mp"),
            P("mp"),
            P(None, "mp"),
            P(None, "mp"),
            P(None, "mp"),
            P("mp", None),
            P(None, "mp"),
            P(),
            P("mp"),
            P(None, ("mp", "dp")),
            P(None, ("mp", "dp")),
            P(("mp", "dp"), None),
        ),
        check_vma=False,
    )
```

profile of v0, /device:TPU:0, one launch (start us, length us, event | category | flops | bytes accessed | tf_op | source)
XLA Modules:
  0.0 644.7 jit_solution(5703986886131777121)
XLA Ops:
  0.6 2.0 select_reduce_fusion.2
  4.5 2.0 add_select_fusion
  6.5 6.9 %compact.2 = (bf16[736,1024]{1,0:T(8,128)(2,1)}, bf16[736,1024]{1,0:T(8,128)(2,1)}) custom-call(s32[1]{0:T(128)} %bitcast.part_ref, s32[1,2048]{1,0:T(1,128)} %bitcast.230, bf16[736,2048]{1,0:T(8,128)(2,1)} %bitcast.240), custom_call_target="tpu_custom_call" | custom-call | flops 3472883712 | bytes 6029312 | tf_op jit(solution)/shard_map/compact/pallas_call | solution.py:69
  16.1 6.9 %compact.3 = (bf16[736,1024]{1,0:T(8,128)(2,1)}, bf16[736,1024]{1,0:T(8,128)(2,1)}) custom-call(s32[1]{0:T(128)} %bitcast.part_ref, s32[1,2048]{1,0:T(1,128)} %bitcast.231, bf16[736,2048]{1,0:T(8,128)(2,1)} %bitcast.241), custom_call_target="tpu_custom_call" | custom-call | flops 3472883712 | bytes 6029312 | tf_op jit(solution)/shard_map/compact/pallas_call | solution.py:69
  28.6 5.1 bias_strip.1.strip_ref
  33.7 2.5 fusion.4
  36.3 3.2 fusion.45
  40.1 3.9 maximum_select_fusion.3.cot_ref.b_peer
  44.1 3.8 maximum_select_fusion.2.cot_ref.b_own
  47.9 4.1 maximum_select_fusion
  55.9 7.4 %convolution_convert_fusion.q_ref.k_ref.v_ref = bf16[1152,1024]{1,0:T(8,128)(2,1)} fusion(bf16[1152,1472]{1,0:T(8,128)(2,1)S(1)} %bitcast.205, f32[1472]{0:T(1024)S(1)} %copy-done.39, f32[1024]{0:T(1024)S(1)} %add_rsqrt_fusion.1, bf16[736,1024]{1,0:T(8,128)(2,1)} %collective-permute-done, bf16[736,1024]{1,0:T(8,128)(2,1)S(1)} %copy-done.13, pred[]{:T(512)S(6)} %eq.37), kind=kOutput, calls=%fused_computation.31 | convolution fusion | flops 3493658624 | bytes 8775425 | tf_op jit(solution)/shard_map/dot_general | solution.py:34
  63.3 24.3 %attend.1 = (bf16[6,1024,1024]{2,1,0:T(8,128)(2,1)}, bf16[384,1024]{1,0:T(8,128)(2,1)}) custom-call(bf16[1152,1024]{1,0:T(8,128)(2,1)} %convolution_convert_fusion.q_ref.k_ref.v_ref, bf16[1152,1024]{1,0:T(8,128)(2,1)} %convolution_convert_fusion.q_ref.k_ref.v_ref, bf16[1152,1024]{1,0:T(8,128)(2,1)} %convolution_convert_fusion.q_ref.k_ref.v_ref, ...), custom_call_target="tpu_custom_call" | custom-call | flops 6442450944 | bytes 12582912 | tf_op jit(solution)/shard_map/attend/pallas_call | solution.py:183
  87.7 4.7 multiply_reduce_fusion.3
  92.4 2.2 multiply_convert_fusion.x_ref.b_own
  94.7 23.9 %ffn.2 = (bf16[1792,1024]{1,0:T(8,128)(2,1)}, bf16[1792,1024]{1,0:T(8,128)(2,1)}, bf16[1792,1024]{1,0:T(8,128)(2,1)}) custom-call(bf16[1472,1792]{1,0:T(8,128)(2,1)} %refs_0_.3, bf16[1472,1792]{1,0:T(8,128)(2,1)} %refs_1_.3, bf16[1472,1792]{1,0:T(8,128)(2,1)} %bitcast.236, bf16[1472,1024]{1,0:T(8,128)(2,1)} %multiply_convert_fusion.x_ref.b_own, ...), custom_call_target="tpu_custom_call" | custom-call | flops 16206790656 | bytes 32866304 | tf_op jit(solution)/shard_map/ffn/pallas_call | solution.py:317
  118.6 10.1 %project.4 = f32[1472,1024]{1,0:T(8,128)} custom-call(bf16[1472,1792]{1,0:T(8,128)(2,1)} %bitcast.237, bf16[1792,1024]{1,0:T(8,128)(2,1)} %get-tuple-element.35.refs_1_.a_own), custom_call_target="tpu_custom_call" | custom-call | flops 5402263552 | bytes 14974976 | tf_op jit(solution)/shard_map/project/pallas_call | solution.py:364
  128.7 16.6 %project.6 = f32[1472,1024]{1,0:T(8,128)} custom-call(bf16[1472,1792]{1,0:T(8,128)(2,1)} %refs_0_.3, bf16[1472,1792]{1,0:T(8,128)(2,1)} %refs_1_.3, bf16[1792,1024]{1,0:T(8,128)(2,1)} %get-tuple-element.37.refs_2_.a_own, bf16[1792,1024]{1,0:T(8,128)(2,1)} %get-tuple-element.38.refs_3_.a_own), custom_call_target="tpu_custom_call" | custom-call | flops 10804527104 | bytes 23920640 | tf_op jit(solution)/shard_map/project/pallas_call | solution.py:364
  145.4 24.0 %ffn.3 = (bf16[1792,1024]{1,0:T(8,128)(2,1)}, bf16[1792,1024]{1,0:T(8,128)(2,1)}, bf16[1792,1024]{1,0:T(8,128)(2,1)}) custom-call(bf16[1472,1792]{1,0:T(8,128)(2,1)} %refs_0_.3, bf16[1472,1792]{1,0:T(8,128)(2,1)} %refs_1_.3, bf16[1472,1792]{1,0:T(8,128)(2,1)} %bitcast.238, bf16[1472,1024]{1,0:T(8,128)(2,1)} %collective-permute-done.4.x_ref.b_peer, ...), custom_call_target="tpu_custom_call" | custom-call | flops 16206790656 | bytes 32866304 | tf_op jit(solution)/shard_map/ffn/pallas_call | solution.py:317
  169.4 17.3 %weight_grad.4 = bf16[1792,1472]{1,0:T(8,128)(2,1)} custom-call(bf16[1792,1024]{1,0:T(8,128)(2,1)} %get-tuple-element.38.refs_3_.a_own, bf16[1792,1024]{1,0:T(8,128)(2,1)} %get-tuple-element.40.refs_3_.a_peer, bf16[1472,1024]{1,0:T(8,128)(2,1)} %multiply_convert_fusion.x_ref.b_own, bf16[1472,1024]{1,0:T(8,128)(2,1)} %collective-permute-done.4.x_ref.b_peer), custom_call_target="tpu_custom_call" | custom-call | flops 10804527104 | bytes 18644992 | tf_op jit(solution)/shard_map/weight_grad/pallas_call | solution.py:339
  186.7 3.8 slice.93
  190.5 3.3 slice.94
  193.8 16.9 %weight_grad.5 = bf16[1792,1472]{1,0:T(8,128)(2,1)} custom-call(bf16[1792,1024]{1,0:T(8,128)(2,1)} %get-tuple-element.35.refs_1_.a_own, bf16[1792,1024]{1,0:T(8,128)(2,1)} %get-tuple-element.36.refs_1_.a_peer, bf16[1472,1024]{1,0:T(8,128)(2,1)} %maximum_select_fusion.2.cot_ref.b_own, bf16[1472,1024]{1,0:T(8,128)(2,1)} %maximum_select_fusion.3.cot_ref.b_peer), custom_call_target="tpu_custom_call" | custom-call | flops 10804527104 | bytes 18644992 | tf_op jit(solution)/shard_map/weight_grad/pallas_call | solution.py:339
  210.7 4.4 constant_dynamic-slice_fusion.1
  216.9 3.0 collective-permute-start.31
  225.2 16.9 %weight_grad.3 = bf16[1792,1472]{1,0:T(8,128)(2,1)} custom-call(bf16[1792,1024]{1,0:T(8,128)(2,1)} %get-tuple-element.37.refs_2_.a_own, bf16[1792,1024]{1,0:T(8,128)(2,1)} %get-tuple-element.39.refs_2_.a_peer, bf16[1472,1024]{1,0:T(8,128)(2,1)} %multiply_convert_fusion.x_ref.b_own, bf16[1472,1024]{1,0:T(8,128)(2,1)} %collective-permute-done.4.x_ref.b_peer), custom_call_target="tpu_custom_call" | custom-call | flops 10804527104 | bytes 18644992 | tf_op jit(solution)/shard_map/weight_grad/pallas_call | solution.py:339
  242.1 4.5 constant_dynamic-slice_fusion.5
  248.9 3.6 collective-permute-done.27
  255.8 16.4 %project.7 = bf16[1472,1024]{1,0:T(8,128)(2,1)} custom-call(bf16[1472,1792]{1,0:T(8,128)(2,1)} %refs_0_.3, bf16[1472,1792]{1,0:T(8,128)(2,1)} %refs_1_.3, bf16[1792,1024]{1,0:T(8,128)(2,1)} %get-tuple-element.39.refs_2_.a_peer, bf16[1792,1024]{1,0:T(8,128)(2,1)} %get-tuple-element.40.refs_3_.a_peer), custom_call_target="tpu_custom_call" | custom-call | flops 10804527104 | bytes 23920640 | tf_op jit(solution)/shard_map/project/pallas_call | solution.py:364
  272.2 54.2 %collective-permute-done.28 = bf16[2,2,48,1472]{3,2,0,1:T(8,128)(2,1)} collective-permute-done((bf16[2,2,48,1472]{3,2,0,1:T(8,128)(2,1)S(1)}, bf16[2,2,48,1472]{3,2,0,1:T(8,128)(2,1)}, u32[]{:S(2)}, u32[]{:S(2)}) %collective-permute-start.28) | collective-permute-done | bytes 565280 | tf_op jit(solution)/shard_map/ppermute | solution.py:389
  329.6 2.3 fusion.11
  336.2 2.6 collective-permute-start.30
  338.8 9.7 %project.5 = bf16[1472,1024]{1,0:T(8,128)(2,1)} custom-call(bf16[1472,1792]{1,0:T(8,128)(2,1)} %bitcast.239, bf16[1792,1024]{1,0:T(8,128)(2,1)} %get-tuple-element.36.refs_1_.a_peer), custom_call_target="tpu_custom_call" | custom-call | flops 5402263552 | bytes 14974976 | tf_op jit(solution)/shard_map/project/pallas_call | solution.py:364
  349.2 2.4 collective-permute-done.24
  353.4 2.6 fusion.8
  359.3 2.8 fusion.9
  362.2 2.5 collective-permute-start.26
  367.5 5.4 collective-permute-done.26
  373.9 2.8 multiply_reduce_fusion.1
  376.8 9.3 %multiply_subtract_fusion = (f32[1472,1024]{1,0:T(8,128)S(1)}, bf16[1472,1024]{1,0:T(8,128)(2,1)}) fusion(f32[1472,1024]{1,0:T(8,128)S(1)} %get-tuple-element.117, bf16[1472,1024]{1,0:T(8,128)(2,1)S(1)} %copy-done.3, f32[1024]{0:T(1024)S(1)} %fusion.36, f32[1472]{0:T(1024)S(1)} %copy-done.30, f32[1024]{0:T(1024)S(1)} %add_rsqrt_fusion, ...), kind=kLoop, calls=%fused_computation.17 | loop fusion | flops 18087936 | bytes 36189952 | tf_op jit(solution)/shard_map/sub | solution.py:513
  386.1 4.5 fusion.23.go_ref
  392.4 27.7 %attend_back.1 = (bf16[384,1024]{1,0:T(8,128)(2,1)}, bf16[384,1024]{1,0:T(8,128)(2,1)}, bf16[384,1024]{1,0:T(8,128)(2,1)}, f32[6,8,1024]{2,1,0:T(8,128)}, f32[6,32,8,128]{3,2,1,0:T(8,128)}) custom-call(bf16[1152,1024]{1,0:T(8,128)(2,1)} %convolution_convert_fusion.q_ref.k_ref.v_ref, bf16[1152,1024]{1,0:T(8,128)(2,1)} %convolution_convert_fusion.q_ref.k_ref.v_ref, ...), custom_call_target="tpu_custom_call" | custom-call | flops 12884901888 | bytes 12582912 | tf_op jit(solution)/shard_map/attend_back/pallas_call | solution.py:266
  424.1 9.2 %fusion.43 = f32[1152,1472]{0,1:T(8,128)} fusion(bf16[1152,1024]{1,0:T(8,128)(2,1)S(1)} %constant_dynamic-update-slice_fusion, f32[1472]{0:T(1024)S(1)} %copy-done.40, f32[1024]{0:T(1024)S(1)} %copy-done.35, bf16[736,1024]{1,0:T(8,128)(2,1)} %collective-permute-done, bf16[736,1024]{1,0:T(8,128)(2,1)S(1)} %copy-done.14, pred[]{:T(512)S(6)} %eq.37), kind=kOutput, calls=%fused_computation.156 | convolution fusion | flops 3492478976 | bytes 12166913 | tf_op jit(solution)/shard_map/dot_general | solution.py:34
  433.4 7.7 %pad_maximum_fusion = f32[1536,1472]{0,1:T(8,128)} fusion(f32[384,1472]{0,1:T(8,128)S(1)} %fusion.19, f32[1152,1472]{0,1:T(8,128)} %fusion.43), kind=kLoop, calls=%fused_computation.5 | loop fusion | flops 2260992 | bytes 18087936 | tf_op jit(solution)/shard_map/concatenate | solution.py:559
  441.1 9.5 %copy.67 = f32[1536,1472]{1,0:T(8,128)} copy(f32[1536,1472]{0,1:T(8,128)} %pad_maximum_fusion) | data formatting | bytes 18087936 | tf_op jit(solution)/shard_map/concatenate | solution.py:559
  450.5 4.1 fusion.14
  454.8 13.9 %fusion.3 = (f32[1472]{0:T(1024)S(1)}, f32[1024]{0:T(1024)S(1)}, f32[1472]{0:T(1024)S(1)}, f32[1472,1024]{1,0:T(8,128)}) fusion(f32[1024]{0:T(1024)S(1)} %multiply_multiply_fusion.2, f32[1472]{0:T(1024)S(1)} %copy-done.33, f32[1024]{0:T(1024)S(1)} %copy-done.35, bf16[736,1024]{1,0:T(8,128)(2,1)S(1)} %copy-done.14, ...), kind=kOutput, calls=%fused_computation.9 | convolution fusion | flops 3507548160 | bytes 14830593 | tf_op jit(solution)/shard_map/dot_general | solution.py:34
  469.7 38.9 %psum.7 = f32[4608]{0:T(1024)S(1)} all-reduce(f32[4608]{0:T(1024)S(1)} %concatenate.135), channel_id=1, replica_groups=mesh['dp'=16,'mp'=2] {'dp','mp'}, use_global_device_ids=true, to_apply=%region_15.16 | all-reduce | flops 4608 | bytes 36864 | tf_op jit(solution)/shard_map/psum | solution.py:551
  509.4 7.6 %fusion.7 = bf16[1472,1024]{1,0:T(8,128)(2,1)S(1)} fusion(f32[1472,1024]{1,0:T(8,128)} %copy-done, f32[1472,1024]{1,0:T(8,128)} %get-tuple-element.118, f32[1024]{0:T(1024)S(1)} %fusion.38, f32[1024]{0:T(1024)S(1)} %multiply_multiply_fusion.2, f32[1472]{0:T(1024)S(1)} %copy-done.33, f32[1472]{0:T(1024)S(1)} %copy-done.40, f32[1024]{0:T(1024)S(1)} %copy-done.35, ...), kind=kLoop, calls=%fused_computation.13 | loop fusion | flops 27131904 | bytes 18112000 | tf_op jit(solution)/shard_map/convert_element_type | solution.py:533
  519.0 3.8 fusion.10
  523.0 2.3 collective-permute-start.11
  530.8 2.2 collective-permute-start.33
  533.0 17.0 %collective-permute-done.11 = bf16[2,2,2,48,1472]{4,3,2,1,0:T(8,128)(2,1)S(1)} collective-permute-done((bf16[2,2,2,48,1472]{4,3,2,1,0:T(8,128)(2,1)S(1)}, bf16[2,2,2,48,1472]{4,3,2,1,0:T(8,128)(2,1)S(1)}, u32[]{:S(2)}, u32[]{:S(2)}) %collective-permute-start.11) | collective-permute-done | bytes 1130528 | tf_op jit(solution)/shard_map/ppermute | solution.py:389
  553.7 2.2 collective-permute-start.21
  555.9 7.8 %collective-permute-done.12 = bf16[2,2,48,1472]{3,2,1,0:T(8,128)(2,1)S(1)} collective-permute-done((bf16[2,2,48,1472]{3,2,1,0:T(8,128)(2,1)S(1)}, bf16[2,2,48,1472]{3,2,1,0:T(8,128)(2,1)S(1)}, u32[]{:S(2)}, u32[]{:S(2)}) %collective-permute-start.12) | collective-permute-done | bytes 565280 | tf_op jit(solution)/shard_map/ppermute | solution.py:389
  563.8 2.2 collective-permute-start.13
  567.2 6.4 spread.3
  573.5 6.4 spread.2
  581.1 12.1 %collective-permute-done.14 = bf16[48,1472]{1,0:T(8,128)(2,1)S(1)} collective-permute-done((bf16[48,1472]{1,0:T(8,128)(2,1)S(1)}, bf16[48,1472]{1,0:T(8,128)(2,1)S(1)}, u32[]{:S(2)}, u32[]{:S(2)}) %collective-permute-start.14) | collective-permute-done | bytes 141344 | tf_op jit(solution)/shard_map/ppermute | solution.py:389
  593.3 3.0 collective-permute-start.34
  596.3 4.6 collective-permute-done.15
  601.8 8.9 %collective-permute-done.16 = bf16[2,48,1472]{2,1,0:T(8,128)(2,1)S(1)} collective-permute-done((bf16[2,48,1472]{2,1,0:T(8,128)(2,1)S(1)}, bf16[2,48,1472]{2,1,0:T(8,128)(2,1)S(1)}, u32[]{:S(2)}, u32[]{:S(2)}) %collective-permute-start.16) | collective-permute-done | bytes 282656 | tf_op jit(solution)/shard_map/ppermute | solution.py:402
  613.0 7.8 %collective-permute-done.17 = bf16[2,2,48,1472]{3,2,0,1:T(8,128)(2,1)S(1)} collective-permute-done((bf16[2,2,48,1472]{3,2,0,1:T(8,128)(2,1)S(1)}, bf16[2,2,48,1472]{3,2,0,1:T(8,128)(2,1)S(1)}, u32[]{:S(2)}, u32[]{:S(2)}) %collective-permute-start.17) | collective-permute-done | bytes 565280 | tf_op jit(solution)/shard_map/ppermute | solution.py:402
  625.0 16.0 %collective-permute-done.18 = bf16[2,2,2,48,1472]{4,3,0,1,2:T(8,128)(2,1)S(1)} collective-permute-done((bf16[2,2,2,48,1472]{4,3,0,1,2:T(8,128)(2,1)S(1)}, bf16[2,2,2,48,1472]{4,3,0,1,2:T(8,128)(2,1)S(1)}, u32[]{:S(2)}, u32[]{:S(2)}) %collective-permute-start.18) | collective-permute-done | bytes 1130528 | tf_op jit(solution)/shard_map/ppermute | solution.py:402
  642.0 2.3 fusion.48
  (243 shorter events, 71.8 us)
Async XLA Ops:
  6.5 7.4 %copy-start.18 = (bf16[192,1472]{1,0:T(8,128)(2,1)S(1)}, bf16[192,1472]{1,0:T(8,128)(2,1)}, u32[]{:S(2)}) copy-start(bf16[192,1472]{1,0:T(8,128)(2,1)} %param.23) | copy-start | bytes 1695748
  6.5 7.4 %copy-start.19 = (bf16[1472,192]{0,1:T(8,128)(2,1)S(1)}, bf16[1472,192]{0,1:T(8,128)(2,1)}, u32[]{:S(2)}) copy-start(bf16[1472,192]{0,1:T(8,128)(2,1)} %param.22) | copy-start | bytes 1695748
  6.5 7.4 %copy-start.20 = (bf16[1472,192]{0,1:T(8,128)(2,1)S(1)}, bf16[1472,192]{0,1:T(8,128)(2,1)}, u32[]{:S(2)}) copy-start(bf16[1472,192]{0,1:T(8,128)(2,1)} %param.21) | copy-start | bytes 1695748
  6.5 7.4 %copy-start.21 = (bf16[1472,192]{0,1:T(8,128)(2,1)S(1)}, bf16[1472,192]{0,1:T(8,128)(2,1)}, u32[]{:S(2)}) copy-start(bf16[1472,192]{0,1:T(8,128)(2,1)} %param.20) | copy-start | bytes 1695748
  13.4 20.2 %collective-permute-start = (bf16[736,1024]{1,0:T(8,128)(2,1)}, bf16[736,1024]{1,0:T(8,128)(2,1)}, u32[]{:S(2)}, u32[]{:S(2)}) collective-permute-start(bf16[736,1024]{1,0:T(8,128)(2,1)} %get-tuple-element.31), channel_id=1, source_target_pairs={{0,1},{1,0},{2,3},{3,2},{4,5},{5,4},{6,7},{7,6},{8,9},{9,8},{10,11... | collective-permute-start | bytes 4521992 | tf_op jit(solution)/shard_map/ppermute | solution.py:413
  15.6 32.3 %collective-permute-start.1 = (bf16[4,192,1472]{2,1,0:T(8,128)(2,1)}, bf16[4,192,1472]{2,1,0:T(8,128)(2,1)}, u32[]{:S(2)}, u32[]{:S(2)}) collective-permute-start(bf16[4,192,1472]{2,1,0:T(8,128)(2,1)} %pad_maximum_fusion.1), channel_id=1, source_target_pairs={{0,1},{1,0},{2,3},{3,2},{4,5},{5,4},{6,7},{7,6},{8,9},{9,8},{10,11... | collective-permute-start | bytes 6782984 | tf_op jit(solution)/shard_map/ppermute | solution.py:413
  15.7 12.1 %collective-permute-start.2 = (f32[32,3]{0,1:T(4,128)S(1)}, f32[32,3]{0,1:T(4,128)S(1)}, u32[]{:S(2)}, u32[]{:S(2)}) collective-permute-start(f32[32,3]{0,1:T(4,128)S(1)} %copy-done.43), channel_id=1, source_target_pairs={{0,1},{1,0},{2,3},{3,2},{4,5},{5,4},{6,7},{7,6},{8,9},{9,8},{10,11... | collective-permute-start | bytes 1160 | tf_op jit(solution)/shard_map/ppermute | solution.py:413
  16.1 7.4 %copy-start.36 = (bf16[1472]{0:T(1024)(128)(2,1)S(1)}, bf16[1472]{0:T(1024)(128)(2,1)}, u32[]{:S(2)}) copy-start(bf16[1472]{0:T(1024)(128)(2,1)} %param.25) | copy-start | bytes 8836
  23.0 17.1 %collective-permute-start.5 = (bf16[736,1024]{1,0:T(8,128)(2,1)}, bf16[736,1024]{1,0:T(8,128)(2,1)}, u32[]{:S(2)}, u32[]{:S(2)}) collective-permute-start(bf16[736,1024]{1,0:T(8,128)(2,1)} %get-tuple-element.33), channel_id=1, source_target_pairs={{0,1},{1,0},{2,3},{3,2},{4,5},{5,4},{6,7},{7,6},{8,9},{9,8},{10,11... | collective-permute-start | bytes 4521992 | tf_op jit(solution)/shard_map/ppermute | solution.py:413
  23.0 21.0 %collective-permute-start.3 = (bf16[736,1024]{1,0:T(8,128)(2,1)}, bf16[736,1024]{1,0:T(8,128)(2,1)}, u32[]{:S(2)}, u32[]{:S(2)}) collective-permute-start(bf16[736,1024]{1,0:T(8,128)(2,1)} %get-tuple-element.34), channel_id=1, source_target_pairs={{0,1},{1,0},{2,3},{3,2},{4,5},{5,4},{6,7},{7,6},{8,9},{9,8},{10,11... | collective-permute-start | bytes 4521992 | tf_op jit(solution)/shard_map/ppermute | solution.py:413
  27.8 5.9 copy-start.13
  28.6 7.7 %copy-start.39 = (f32[1472]{0:T(1024)S(1)}, f32[1472]{0:T(1024)}, u32[]{:S(2)}) copy-start(f32[1472]{0:T(1024)} %param.19) | copy-start | bytes 17668
  36.3 17.9 %copy-start.34 = (f32[1024]{0:T(1024)}, f32[1024]{0:T(1024)S(1)}, u32[]{:S(2)}) copy-start(f32[1024]{0:T(1024)S(1)} %add_rsqrt_fusion.1) | copy-start | bytes 12292
  39.4 4.6 copy-start.37
  87.6 4.8 copy-start.30
  94.6 50.8 %collective-permute-start.4 = (bf16[1472,1024]{1,0:T(8,128)(2,1)}, bf16[1472,1024]{1,0:T(8,128)(2,1)}, u32[]{:S(2)}, u32[]{:S(2)}) collective-permute-start(bf16[1472,1024]{1,0:T(8,128)(2,1)} %multiply_convert_fusion.x_ref.b_own), channel_id=1, source_target_pairs={{0,1},{1,0},{2,3},{3,2},{4,5},{5,4},{6,7},{7,6},{8,9},{9,8},{10,11... | collective-permute-start | bytes 9043976 | tf_op jit(solution)/shard_map/ppermute | solution.py:413
  215.1 4.8 copy-start.2
  215.1 7.2 %copy-start.12 = (bf16[16,48,1472]{2,1,0:T(8,128)(2,1)S(1)}, bf16[16,48,1472]{2,1,0:T(8,128)(2,1)}, u32[]{:S(2)}) copy-start(bf16[16,48,1472]{2,1,0:T(8,128)(2,1)} %slice.94) | copy-start | bytes 6782980
  216.9 136.5 %collective-permute-start.31 = (bf16[2,2,2,112,1472]{4,3,0,1,2:T(8,128)(2,1)}, bf16[2,2,2,112,1472]{4,3,0,1,2:T(8,128)(2,1)}, u32[]{:S(2)}, u32[]{:S(2)}) collective-permute-start(bf16[2,2,2,112,1472]{4,3,0,1,2:T(8,128)(2,1)} %bitcast.187), channel_id=1, source_target_pairs={{0,2},{2,0},{4,6},{6,4},{8,10},{10,8},{12,14},{14,12},{16,18},{18,... | collective-permute-start | bytes 7913480 | tf_op jit(solution)/shard_map/ppermute | solution.py:389
  221.3 108.3 %collective-permute-start.23 = (bf16[2,2,2,64,1472]{4,3,2,1,0:T(8,128)(2,1)}, bf16[2,2,2,64,1472]{4,3,2,1,0:T(8,128)(2,1)}, u32[]{:S(2)}, u32[]{:S(2)}) collective-permute-start(bf16[2,2,2,64,1472]{4,3,2,1,0:T(8,128)(2,1)} %dynamic-slice_bitcast_fusion), channel_id=1, source_target_pairs={{0,2},{2,0},{4,6},{6,4},{8,10},{10,8},{12,14},{14,12},{16,18},{18,... | collective-permute-start | bytes 4521992 | tf_op jit(solution)/shard_map/ppermute | solution.py:389
  223.7 28.7 %collective-permute-start.27 = (bf16[2,2,2,48,1472]{4,3,0,1,2:T(8,128)(2,1)}, bf16[2,2,2,48,1472]{4,3,0,1,2:T(8,128)(2,1)}, u32[]{:S(2)}, u32[]{:S(2)}) collective-permute-start(bf16[2,2,2,48,1472]{4,3,0,1,2:T(8,128)(2,1)} %bitcast.189), channel_id=1, source_target_pairs={{0,4},{2,6},{4,0},{6,2},{8,12},{10,14},{12,8},{14,10},{16,20},{18,... | collective-permute-start | bytes 3391496 | tf_op jit(solution)/shard_map/ppermute | solution.py:389
  248.4 110.3 %collective-permute-start.19 = (bf16[2,2,2,112,1472]{4,3,0,1,2:T(8,128)(2,1)}, bf16[2,2,2,112,1472]{4,3,0,1,2:T(8,128)(2,1)}, u32[]{:S(2)}, u32[]{:S(2)}) collective-permute-start(bf16[2,2,2,112,1472]{4,3,0,1,2:T(8,128)(2,1)} %bitcast.188), channel_id=1, source_target_pairs={{0,4},{2,6},{4,0},{6,2},{8,12},{10,14},{12,8},{14,10},{16,20},{18,... | collective-permute-start | bytes 7913480 | tf_op jit(solution)/shard_map/ppermute | solution.py:389
  255.1 71.3 %copy-start.16 = (bf16[2,2,2,48,1472]{4,3,0,1,2:T(8,128)(2,1)S(1)}, bf16[2,2,2,48,1472]{4,3,0,1,2:T(8,128)(2,1)}, u32[]{:S(2)}) copy-start(bf16[2,2,2,48,1472]{4,3,0,1,2:T(8,128)(2,1)} %copy-done.15) | copy-start | bytes 3391492
  255.1 71.3 %collective-permute-start.28 = (bf16[2,2,48,1472]{3,2,0,1:T(8,128)(2,1)S(1)}, bf16[2,2,48,1472]{3,2,0,1:T(8,128)(2,1)}, u32[]{:S(2)}, u32[]{:S(2)}) collective-permute-start(bf16[2,2,48,1472]{3,2,0,1:T(8,128)(2,1)S(1)} %dynamic-slice_bitcast_fusion.7), channel_id=1, source_target_pairs={{0,2},{2,0},{4,6},{6,4},{8,10},{10,8},{12,14},{14,12},{16,18},{18,... | collective-permute-start | bytes 1695752 | tf_op jit(solution)/shard_map/ppermute | solution.py:389
  327.7 8.5 %collective-permute-start.29 = (bf16[2,48,1472]{2,1,0:T(8,128)(2,1)S(1)}, bf16[2,48,1472]{2,1,0:T(8,128)(2,1)S(1)}, u32[]{:S(2)}, u32[]{:S(2)}) collective-permute-start(bf16[2,48,1472]{2,1,0:T(8,128)(2,1)S(1)} %dynamic-slice_bitcast_fusion.12), channel_id=1, source_target_pairs={{0,8},{2,10},{4,12},{6,14},{8,0},{10,2},{12,4},{14,6},{16,24},{18,... | collective-permute-start | bytes 847880 | tf_op jit(solution)/shard_map/ppermute | solution.py:389
  332.8 18.7 %collective-permute-start.24 = (bf16[2,2,64,1472]{3,2,1,0:T(8,128)(2,1)}, bf16[2,2,64,1472]{3,2,1,0:T(8,128)(2,1)}, u32[]{:S(2)}, u32[]{:S(2)}) collective-permute-start(bf16[2,2,64,1472]{3,2,1,0:T(8,128)(2,1)} %dynamic-slice_bitcast_fusion.4), channel_id=1, source_target_pairs={{0,4},{2,6},{4,0},{6,2},{8,12},{10,14},{12,8},{14,10},{16,20},{18,... | collective-permute-start | bytes 2261000 | tf_op jit(solution)/shard_map/ppermute | solution.py:389
  336.2 12.4 %collective-permute-start.30 = (bf16[48,1472]{1,0:T(8,128)(2,1)S(1)}, bf16[48,1472]{1,0:T(8,128)(2,1)S(1)}, u32[]{:S(2)}, u32[]{:S(2)}) collective-permute-start(bf16[48,1472]{1,0:T(8,128)(2,1)S(1)} %dynamic-slice_bitcast_fusion.15), channel_id=1, source_target_pairs={{0,16},{2,18},{4,20},{6,22},{8,24},{10,26},{12,28},{14,30},{16,0},... | collective-permute-start | bytes 423944 | tf_op jit(solution)/shard_map/ppermute | solution.py:389
  348.5 4.9 copy-start.10
  348.5 25.3 %collective-permute-start.8 = (bf16[1472,1024]{1,0:T(8,128)(2,1)}, bf16[1472,1024]{1,0:T(8,128)(2,1)S(1)}, u32[]{:S(2)}, u32[]{:S(2)}) collective-permute-start(bf16[1472,1024]{1,0:T(8,128)(2,1)} %project.7), channel_id=1, source_target_pairs={{0,1},{1,0},{2,3},{3,2},{4,5},{5,4},{6,7},{7,6},{8,9},{9,8},{10,11... | collective-permute-start | bytes 9043976 | tf_op jit(solution)/shard_map/ppermute | solution.py:413
  348.6 28.1 %collective-permute-start.6 = (bf16[1472,1024]{1,0:T(8,128)(2,1)}, bf16[1472,1024]{1,0:T(8,128)(2,1)}, u32[]{:S(2)}, u32[]{:S(2)}) collective-permute-start(bf16[1472,1024]{1,0:T(8,128)(2,1)} %project.5), channel_id=1, source_target_pairs={{0,1},{1,0},{2,3},{3,2},{4,5},{5,4},{6,7},{7,6},{8,9},{9,8},{10,11... | collective-permute-start | bytes 9043976 | tf_op jit(solution)/shard_map/ppermute | solution.py:413
  352.9 9.2 %collective-permute-start.25 = (bf16[2,64,1472]{2,1,0:T(8,128)(2,1)S(1)}, bf16[2,64,1472]{2,1,0:T(8,128)(2,1)S(1)}, u32[]{:S(2)}, u32[]{:S(2)}) collective-permute-start(bf16[2,64,1472]{2,1,0:T(8,128)(2,1)S(1)} %dynamic-slice_bitcast_fusion.9), channel_id=1, source_target_pairs={{0,8},{2,10},{4,12},{6,14},{8,0},{10,2},{12,4},{14,6},{16,24},{18,... | collective-permute-start | bytes 1130504 | tf_op jit(solution)/shard_map/ppermute | solution.py:389
  357.2 171.4 %collective-permute-start.32 = (bf16[2,2,112,1472]{3,2,0,1:T(8,128)(2,1)}, bf16[2,2,112,1472]{3,2,0,1:T(8,128)(2,1)}, u32[]{:S(2)}, u32[]{:S(2)}) collective-permute-start(bf16[2,2,112,1472]{3,2,0,1:T(8,128)(2,1)} %dynamic-slice_bitcast_fusion.1), channel_id=1, source_target_pairs={{0,4},{2,6},{4,0},{6,2},{8,12},{10,14},{12,8},{14,10},{16,20},{18,... | collective-permute-start | bytes 3956744 | tf_op jit(solution)/shard_map/ppermute | solution.py:389
  358.7 15.1 %slice-start = ((s8[6029312]{0:T(1024)(128)(4,1)}), s8[4194304]{0:T(1024)(128)(4,1)S(1)}, s32[]{:S(2)}) async-start(s8[6029312]{0:T(1024)(128)(4,1)} %bitcast.193), calls=%async_computation | async-start | bytes 8388608
  359.3 14.6 %slice-start.1 = ((s8[6029312]{0:T(1024)(128)(4,1)}), s8[1835008]{0:T(1024)(128)(4,1)S(1)}, s32[]{:S(2)}) async-start(s8[6029312]{0:T(1024)(128)(4,1)} %bitcast.193), calls=%async_computation.1 | async-start | bytes 3670016
  362.1 11.7 %copy-start.6 = (bf16[2,2,2,112,1472]{4,3,0,1,2:T(8,128)(2,1)}, bf16[2,2,2,112,1472]{4,3,0,1,2:T(8,128)(2,1)S(1)}, u32[]{:S(2)}) copy-start(bf16[2,2,2,112,1472]{4,3,0,1,2:T(8,128)(2,1)S(1)} %fusion.9) | copy-start | bytes 7913476
  362.2 10.6 %collective-permute-start.26 = (bf16[64,1472]{1,0:T(8,128)(2,1)S(1)}, bf16[64,1472]{1,0:T(8,128)(2,1)S(1)}, u32[]{:S(2)}, u32[]{:S(2)}) collective-permute-start(bf16[64,1472]{1,0:T(8,128)(2,1)S(1)} %dynamic-slice_bitcast_fusion.14), channel_id=1, source_target_pairs={{0,16},{2,18},{4,20},{6,22},{8,24},{10,26},{12,28},{14,30},{16,0},... | collective-permute-start | bytes 565256 | tf_op jit(solution)/shard_map/ppermute | solution.py:389
  366.0 185.9 %collective-permute-start.20 = (bf16[2,2,112,1472]{3,2,0,1:T(8,128)(2,1)}, bf16[2,2,112,1472]{3,2,0,1:T(8,128)(2,1)}, u32[]{:S(2)}, u32[]{:S(2)}) collective-permute-start(bf16[2,2,112,1472]{3,2,0,1:T(8,128)(2,1)} %dynamic-slice_bitcast_fusion.2), channel_id=1, source_target_pairs={{0,2},{2,0},{4,6},{6,4},{8,10},{10,8},{12,14},{14,12},{16,18},{18,... | collective-permute-start | bytes 3956744 | tf_op jit(solution)/shard_map/ppermute | solution.py:389
  386.1 4.5 copy-start
  386.1 4.5 copy-start.25
  450.5 4.1 copy-start.27
  450.5 4.2 copy-start.38
  450.5 4.2 copy-start.33
  454.7 64.4 %collective-permute-start.10 = (bf16[4,192,1472]{2,1,0:T(8,128)(2,1)}, bf16[4,192,1472]{2,1,0:T(8,128)(2,1)}, u32[]{:S(2)}, u32[]{:S(2)}) collective-permute-start(bf16[4,192,1472]{2,1,0:T(8,128)(2,1)} %fusion.14), channel_id=1, source_target_pairs={{0,1},{1,0},{2,3},{3,2},{4,5},{5,4},{6,7},{7,6},{8,9},{9,8},{10,11... | collective-permute-start | bytes 6782984 | tf_op jit(solution)/shard_map/ppermute | solution.py:413
  454.7 13.9 %copy-start.28 = (f32[6,32,8,128]{3,2,1,0:T(8,128)S(1)}, f32[6,32,8,128]{3,2,1,0:T(8,128)}, u32[]{:S(2)}) copy-start(f32[6,32,8,128]{3,2,1,0:T(8,128)} %get-tuple-element.46) | copy-start | bytes 2359300
  454.7 14.4 %copy-start.41 = (pred[8,8]{0,1:T(8,128)(4,1)S(1)}, pred[8,8]{0,1:T(8,128)(4,1)}, u32[]{:S(2)}) copy-start(pred[8,8]{0,1:T(8,128)(4,1)} %get-tuple-element.119) | copy-start | bytes 196
  454.8 14.4 %copy-start.42 = (pred[8,8]{0,1:T(8,128)(4,1)S(1)}, pred[8,8]{0,1:T(8,128)(4,1)}, u32[]{:S(2)}) copy-start(pred[8,8]{0,1:T(8,128)(4,1)} %get-tuple-element.120) | copy-start | bytes 196
  454.8 14.5 %copy-start.44 = (pred[32]{0:T(512)(128)(4,1)S(1)}, pred[32]{0:T(512)(128)(4,1)}, u32[]{:S(2)}) copy-start(pred[32]{0:T(512)(128)(4,1)} %get-tuple-element.121) | copy-start | bytes 100
  454.8 14.5 %copy-start.45 = (pred[32]{0:T(512)(128)(4,1)S(1)}, pred[32]{0:T(512)(128)(4,1)}, u32[]{:S(2)}) copy-start(pred[32]{0:T(512)(128)(4,1)} %get-tuple-element.122) | copy-start | bytes 100
  454.8 53.9 %copy-start.32 = (f32[1024]{0:T(1024)S(1)}, f32[1024]{0:T(1024)}, u32[]{:S(2)}) copy-start(f32[1024]{0:T(1024)} %copy-done.31) | copy-start | bytes 12292
  523.0 27.0 %collective-permute-start.11 = (bf16[2,2,2,48,1472]{4,3,2,1,0:T(8,128)(2,1)S(1)}, bf16[2,2,2,48,1472]{4,3,2,1,0:T(8,128)(2,1)S(1)}, u32[]{:S(2)}, u32[]{:S(2)}) collective-permute-start(bf16[2,2,2,48,1472]{4,3,2,1,0:T(8,128)(2,1)S(1)} %dynamic-slice_bitcast_fusion.3), channel_id=1, source_target_pairs={{0,2},{2,0},{4,6},{6,4},{8,10},{10,8},{12,14},{14,12},{16,18},{18,... | collective-permute-start | bytes 3391496 | tf_op jit(solution)/shard_map/ppermute | solution.py:389
  526.7 39.3 %collective-permute-start.9 = (bf16[736,1024]{1,0:T(8,128)(2,1)S(1)}, bf16[736,1024]{1,0:T(8,128)(2,1)S(1)}, u32[]{:S(2)}, u32[]{:S(2)}) collective-permute-start(bf16[736,1024]{1,0:T(8,128)(2,1)S(1)} %get-tuple-element.105), channel_id=1, source_target_pairs={{0,1},{1,0},{2,3},{3,2},{4,5},{5,4},{6,7},{7,6},{8,9},{9,8},{10,11... | collective-permute-start | bytes 4521992 | tf_op jit(solution)/shard_map/ppermute | solution.py:413
  528.1 45.4 %collective-permute-start.7 = (bf16[736,1024]{1,0:T(8,128)(2,1)S(1)}, bf16[736,1024]{1,0:T(8,128)(2,1)}, u32[]{:S(2)}, u32[]{:S(2)}) collective-permute-start(bf16[736,1024]{1,0:T(8,128)(2,1)S(1)} %get-tuple-element.107), channel_id=1, source_target_pairs={{0,1},{1,0},{2,3},{3,2},{4,5},{5,4},{6,7},{7,6},{8,9},{9,8},{10,11... | collective-permute-start | bytes 4521992 | tf_op jit(solution)/shard_map/ppermute | solution.py:413
  530.7 21.2 %copy-start.7 = (bf16[2,2,2,112,1472]{4,3,0,1,2:T(8,128)(2,1)S(1)}, bf16[2,2,2,112,1472]{4,3,0,1,2:T(8,128)(2,1)}, u32[]{:S(2)}) copy-start(bf16[2,2,2,112,1472]{4,3,0,1,2:T(8,128)(2,1)} %copy-done.6) | copy-start | bytes 7913476
  530.8 50.2 %collective-permute-start.33 = (bf16[2,112,1472]{2,1,0:T(8,128)(2,1)S(1)}, bf16[2,112,1472]{2,1,0:T(8,128)(2,1)S(1)}, u32[]{:S(2)}, u32[]{:S(2)}) collective-permute-start(bf16[2,112,1472]{2,1,0:T(8,128)(2,1)S(1)} %dynamic-slice_bitcast_fusion.5), channel_id=1, source_target_pairs={{0,8},{2,10},{4,12},{6,14},{8,0},{10,2},{12,4},{14,6},{16,24},{18,... | collective-permute-start | bytes 1978376 | tf_op jit(solution)/shard_map/ppermute | solution.py:389
  550.4 13.2 %collective-permute-start.12 = (bf16[2,2,48,1472]{3,2,1,0:T(8,128)(2,1)S(1)}, bf16[2,2,48,1472]{3,2,1,0:T(8,128)(2,1)S(1)}, u32[]{:S(2)}, u32[]{:S(2)}) collective-permute-start(bf16[2,2,48,1472]{3,2,1,0:T(8,128)(2,1)S(1)} %dynamic-slice_bitcast_fusion.8), channel_id=1, source_target_pairs={{0,4},{2,6},{4,0},{6,2},{8,12},{10,14},{12,8},{14,10},{16,20},{18,... | collective-permute-start | bytes 1695752 | tf_op jit(solution)/shard_map/ppermute | solution.py:389
  553.7 48.0 %collective-permute-start.21 = (bf16[2,112,1472]{2,1,0:T(8,128)(2,1)S(1)}, bf16[2,112,1472]{2,1,0:T(8,128)(2,1)S(1)}, u32[]{:S(2)}, u32[]{:S(2)}) collective-permute-start(bf16[2,112,1472]{2,1,0:T(8,128)(2,1)S(1)} %dynamic-slice_bitcast_fusion.6), channel_id=1, source_target_pairs={{0,8},{2,10},{4,12},{6,14},{8,0},{10,2},{12,4},{14,6},{16,24},{18,... | collective-permute-start | bytes 1978376 | tf_op jit(solution)/shard_map/ppermute | solution.py:389
  563.8 16.1 %collective-permute-start.13 = (bf16[2,48,1472]{2,1,0:T(8,128)(2,1)S(1)}, bf16[2,48,1472]{2,1,0:T(8,128)(2,1)S(1)}, u32[]{:S(2)}, u32[]{:S(2)}) collective-permute-start(bf16[2,48,1472]{2,1,0:T(8,128)(2,1)S(1)} %dynamic-slice_bitcast_fusion.13), channel_id=1, source_target_pairs={{0,8},{2,10},{4,12},{6,14},{8,0},{10,2},{12,4},{14,6},{16,24},{18,... | collective-permute-start | bytes 847880 | tf_op jit(solution)/shard_map/ppermute | solution.py:389
  580.0 13.1 %collective-permute-start.14 = (bf16[48,1472]{1,0:T(8,128)(2,1)S(1)}, bf16[48,1472]{1,0:T(8,128)(2,1)S(1)}, u32[]{:S(2)}, u32[]{:S(2)}) collective-permute-start(bf16[48,1472]{1,0:T(8,128)(2,1)S(1)} %dynamic-slice_bitcast_fusion.16), channel_id=1, source_target_pairs={{0,16},{2,18},{4,20},{6,22},{8,24},{10,26},{12,28},{14,30},{16,0},... | collective-permute-start | bytes 423944 | tf_op jit(solution)/shard_map/ppermute | solution.py:389
  593.2 7.6 %collective-permute-start.15 = (bf16[48,1472]{1,0:T(8,128)(2,1)S(1)}, bf16[48,1472]{1,0:T(8,128)(2,1)S(1)}, u32[]{:S(2)}, u32[]{:S(2)}) collective-permute-start(bf16[48,1472]{1,0:T(8,128)(2,1)S(1)} %fusion.34), channel_id=1, source_target_pairs={{0,16},{2,18},{4,20},{6,22},{8,24},{10,26},{12,28},{14,30},{16,0},... | collective-permute-start | bytes 423944 | tf_op jit(solution)/shard_map/ppermute | solution.py:402
  593.3 29.5 %collective-permute-start.34 = (bf16[112,1472]{1,0:T(8,128)(2,1)S(1)}, bf16[112,1472]{1,0:T(8,128)(2,1)S(1)}, u32[]{:S(2)}, u32[]{:S(2)}) collective-permute-start(bf16[112,1472]{1,0:T(8,128)(2,1)S(1)} %dynamic-slice_bitcast_fusion.10), channel_id=1, source_target_pairs={{0,16},{2,18},{4,20},{6,22},{8,24},{10,26},{12,28},{14,30},{16,0},... | collective-permute-start | bytes 989192 | tf_op jit(solution)/shard_map/ppermute | solution.py:389
  600.9 9.8 %collective-permute-start.16 = (bf16[2,48,1472]{2,1,0:T(8,128)(2,1)S(1)}, bf16[2,48,1472]{2,1,0:T(8,128)(2,1)S(1)}, u32[]{:S(2)}, u32[]{:S(2)}) collective-permute-start(bf16[2,48,1472]{2,1,0:T(8,128)(2,1)S(1)} %maximum_select_fusion.10), channel_id=1, source_target_pairs={{0,8},{2,10},{4,12},{6,14},{8,0},{10,2},{12,4},{14,6},{16,24},{18,... | collective-permute-start | bytes 847880 | tf_op jit(solution)/shard_map/ppermute | solution.py:402
  610.8 9.9 %collective-permute-start.17 = (bf16[2,2,48,1472]{3,2,0,1:T(8,128)(2,1)S(1)}, bf16[2,2,48,1472]{3,2,0,1:T(8,128)(2,1)S(1)}, u32[]{:S(2)}, u32[]{:S(2)}) collective-permute-start(bf16[2,2,48,1472]{3,2,0,1:T(8,128)(2,1)S(1)} %maximum_select_fusion.8), channel_id=1, source_target_pairs={{0,4},{2,6},{4,0},{6,2},{8,12},{10,14},{12,8},{14,10},{16,20},{18,... | collective-permute-start | bytes 1695752 | tf_op jit(solution)/shard_map/ppermute | solution.py:402
  612.7 11.1 %collective-permute-start.22 = (bf16[112,1472]{1,0:T(8,128)(2,1)S(1)}, bf16[112,1472]{1,0:T(8,128)(2,1)S(1)}, u32[]{:S(2)}, u32[]{:S(2)}) collective-permute-start(bf16[112,1472]{1,0:T(8,128)(2,1)S(1)} %dynamic-slice_bitcast_fusion.11), channel_id=1, source_target_pairs={{0,16},{2,18},{4,20},{6,22},{8,24},{10,26},{12,28},{14,30},{16,0},... | collective-permute-start | bytes 989192 | tf_op jit(solution)/shard_map/ppermute | solution.py:389
  621.0 20.0 %collective-permute-start.18 = (bf16[2,2,2,48,1472]{4,3,0,1,2:T(8,128)(2,1)S(1)}, bf16[2,2,2,48,1472]{4,3,0,1,2:T(8,128)(2,1)S(1)}, u32[]{:S(2)}, u32[]{:S(2)}) collective-permute-start(bf16[2,2,2,48,1472]{4,3,0,1,2:T(8,128)(2,1)S(1)} %maximum_select_fusion.6), channel_id=1, source_target_pairs={{0,2},{2,0},{4,6},{6,4},{8,10},{10,8},{12,14},{14,12},{16,18},{18,... | collective-permute-start | bytes 3391496 | tf_op jit(solution)/shard_map/ppermute | solution.py:402
  (20 other events, 57.0 us)
where the time goes:
time: 652 us; the launch traced here: 645 us
  Pallas kernels  236 us (36%)
  waiting for transfers between devices  142 us (22%)
  other arithmetic  78 us (12%)
  local copies, waits for them, and re-layouts  61.1 us (9%)
  matrix products  44.6 us (7%)
  starting transfers between devices  40.4 us (6%)
  blocking collectives  38.9 us (6%)
    ppermute x20, waiting for transfers between devices, halve(): came = lax.ppermute(give, 'dp', [(i, i ^ 1 << bit) for i in range(size)])  104 us
    pallas_call x4, Pallas kernels, project(): call(functools.partial(project_kernel, count), 'project', 2 * count * D *...  52.9 us
    pallas_call x3, Pallas kernels, weight_grad(): call(weight_grad_kernel, 'weight_grad', 4 * D * units * LMAX, 4 * D * LMA...  51.1 us
    pallas_call x2, Pallas kernels, ffn(): call(ffn_kernel, 'ffn', 6 * D * units * LMAX, 3 * D * units * 2 + 2 * D *...  48 us
    dot_general x7, matrix products, dot(): return lax.dot_general(a, b, dims, preferred_element_type=F32)  44.6 us
    psum x1, blocking collectives, body(): small = lax.psum(small, ('dp', 'mp'))  38.9 us
    ppermute x4, waiting for transfers between devices, regather(): came = lax.ppermute(values, 'dp', [(i, i ^ 1 << bit) for i in range(size)])  37.3 us
    ppermute x20, starting transfers between devices, halve(): came = lax.ppermute(give, 'dp', [(i, i ^ 1 << bit) for i in range(size)])  33.3 us
  transfers between devices with their start and end apart: 35, of which 12 were waited for; matrix products, arithmetic and copies ran while one was open for 21% of the time, Pallas kernels for 23%

commit v1 on v0

v1 whole, which is shorter than its diff:
```python
import functools

import jax
import jax.numpy as jnp
import numpy as np
from jax import lax
from jax.experimental import pallas as pl
from jax.experimental.pallas import tpu as pltpu
from jax.sharding import PartitionSpec as P

D = 1472
HDIM = 64
BUCKETS = 32
LMAX = 1024
ROWS_DEV = 2048

EPSILON = 1e-06
DELETE_DEPTH = 4.0
NEG_LARGE = -1e30
NEAR_STEPS = (1, 2, 3, 4, 5, 6, 7, 8, 12, 16, 23, 32, 46, 64, 91)
TILE = 128
QBLOCK = 256
ABLOCK = 512
AUG = 16
F32 = jnp.float32
BF16 = jnp.bfloat16
GELU_C = float(np.sqrt(2.0 / np.pi))

NN = (((1,), (0,)), ((), ()))
TN = (((0,), (0,)), ((), ()))
NT = (((1,), (1,)), ((), ()))


def dot(a, b, dims):
    return lax.dot_general(a, b, dims, preferred_element_type=F32)


def with_side(kernel, inputs, outputs, pairs, bits_ref, *refs):
    first = inputs + 2 * pairs
    last = first + outputs + 2 * pairs
    kernel(*refs[:inputs], *refs[first : first + outputs], *refs[last:])
    for pair in range(pairs):
        keep_ref, came_ref = refs[inputs + 2 * pair : inputs + 2 * pair + 2]
        outs = refs[first + outputs + 2 * pair : first + outputs + 2 * pair + 2]
        mine = bits_ref[pair]
        for out, which in zip(outs, (mine, 1 - mine)):
            total = keep_ref[:, which].astype(F32) + came_ref[:, which].astype(F32)
            out[...] = total.astype(BF16)


def call(kernel, name, flops, nbytes, limit, side=(), **kw):
    for _, keep, came in side:
        nbytes += 6 * keep.size
    extra = ()
    outputs = 1
    if side:
        single = not isinstance(kw["out_shape"], list)
        out_specs = [kw["out_specs"]] if single else list(kw["out_specs"])
        out_shape = [kw["out_shape"]] if single else list(kw["out_shape"])
        outputs, inputs = len(out_shape), len(kw["in_specs"])
        in_specs = list(kw["in_specs"])
        for _, keep, came in side:
            outer, _, rows, width = keep.shape
            block = pl.BlockSpec(
                (1, 2, rows, width), lambda i, n=outer: (jnp.minimum(i, n - 1), 0, 0, 0)
            )
            out = pl.BlockSpec(
                (1, rows, width), lambda i, n=outer: (jnp.minimum(i, n - 1), 0, 0)
            )
            in_specs += [block, block]
            out_specs += [out, out]
            out_shape += [jax.ShapeDtypeStruct((outer, rows, width), BF16)] * 2
            extra += (keep, came)
        kernel = functools.partial(with_side, kernel, inputs, outputs, len(side))
        kw.update(in_specs=[SMEM] + in_specs, out_specs=out_specs, out_shape=out_shape)
    run = pl.pallas_call(
        kernel,
        name=name,
        cost_estimate=pl.CostEstimate(
            flops=int(flops), bytes_accessed=int(nbytes), transcendentals=0
        ),
        compiler_params=pltpu.CompilerParams(vmem_limit_bytes=56 << 20),
        **kw,
    )
    if not side:
        return run

    def launch(*args):
        out = run(jnp.stack([bit for bit, _, _ in side]), *args, *extra)
        main = out[0] if single else out[:outputs]
        return main, out[outputs:]

    return launch


VMEM = pl.BlockSpec(memory_space=pltpu.VMEM)
SMEM = pl.BlockSpec(memory_space=pltpu.SMEM)
ANY = pl.BlockSpec(memory_space=pl.ANY)


def place_kernel(
    part_ref, length_ref, mask_ref, q_ref, k_ref, v_ref, out_ref, slot_ref, count_ref, stack_ref
):
    for i, ref in enumerate((q_ref, k_ref, v_ref, out_ref)):
        stack_ref[i] = ref[...]
    mask = mask_ref[...]
    rows = lax.broadcasted_iota(jnp.int32, (1, ROWS_DEV), 1)
    first = (rows < length_ref[0]).astype(jnp.int32)
    pieces = []
    before = jnp.zeros((1, 1), F32)
    ahead = lax.broadcasted_iota(jnp.int32, (QBLOCK, QBLOCK), 0) <= lax.broadcasted_iota(
        jnp.int32, (QBLOCK, QBLOCK), 1
    )
    ahead = ahead.astype(F32).astype(BF16)
    flags = mask.astype(F32).astype(BF16)
    for block in range(ROWS_DEV // QBLOCK):
        part = flags[:, block * QBLOCK : (block + 1) * QBLOCK]
        ranks = dot(jnp.broadcast_to(part, (16, QBLOCK)), ahead, NN)[:1] + before
        before = ranks[:, QBLOCK - 1 :]
        pieces.append(ranks)
    ranks = jnp.concatenate(pieces, axis=1).astype(jnp.int32)
    kept_first = jnp.sum(mask * first, axis=1, keepdims=True)
    total = jnp.sum(mask, axis=1, keepdims=True)
    rank = ranks - 1 + jnp.where(first > 0, 0, LMAX - kept_first)
    slot_ref[...] = jnp.where(mask > 0, rank, -1)
    count = jnp.where(part_ref[0] == 0, kept_first, total - kept_first)
    count_ref[...] = jnp.broadcast_to(count, (1, 128))


def places(part, lengths, mask, weights):
    return call(
        place_kernel,
        "places",
        1e6,
        1e5,
        16,
        in_specs=[SMEM, SMEM, VMEM] + [VMEM] * 4,
        out_specs=[VMEM, VMEM, VMEM],
        out_shape=[
            jax.ShapeDtypeStruct((1, ROWS_DEV), jnp.int32),
            jax.ShapeDtypeStruct((1, 128), jnp.int32),
            jax.ShapeDtypeStruct((4, *weights[0].shape), BF16),
        ],
    )(part, lengths, mask, *weights)


def compact_half(item, slot_ref, x_ref, out_ref):
    for block in range(LMAX // QBLOCK):
        width = ROWS_DEV - 512 - block * QBLOCK
        start = pl.multiple_of(item * 512 + block * QBLOCK, 128)
        ids = item * LMAX + block * QBLOCK + lax.broadcasted_iota(jnp.int32, (QBLOCK, 1), 0)
        hot = (slot_ref[:, pl.ds(start, width)] == ids).astype(F32).astype(BF16)
        rows = dot(x_ref[:, pl.ds(start, width)], hot, NT)
        out_ref[:, block * QBLOCK : (block + 1) * QBLOCK] = rows.astype(BF16)


def compact_kernel(part_ref, slot_ref, x_ref, own_ref, peer_ref):
    compact_half(part_ref[0], slot_ref, x_ref, own_ref)
    compact_half(1 - part_ref[0], slot_ref, x_ref, peer_ref)


def halves(part, own, came, whole, hold, sems):
    size = own.shape[0]
    copies_in, copies_out = [], []
    for i, (ref, place) in enumerate(((own, part), (came, 1 - part))):
        copies_in.append(pltpu.make_async_copy(ref, hold.at[i], sems.at[0, i]))
        target = whole.at[pl.ds(pl.multiple_of(place * size, 16), size)]
        copies_out.append(pltpu.make_async_copy(hold.at[i], target, sems.at[1, i]))
    return copies_in, copies_out


def compact_join_kernel(
    part_ref, slot_ref, x_ref, stack_ref, came_ref, own_ref, peer_ref, qkv_ref, out_ref, hold, sems
):
    part = part_ref[0]
    inner = out_ref.shape[0]
    copies_in, copies_out = [], []
    for i in range(4):
        whole = qkv_ref.at[pl.ds(i * inner, inner)] if i < 3 else out_ref
        ins, outs = halves(part, stack_ref.at[i], came_ref.at[i], whole, hold.at[i], sems.at[i])
        copies_in += ins
        copies_out += outs
    for copy in copies_in:
        copy.start()
    compact_half(part, slot_ref, x_ref, own_ref)
    for copy, following in zip(copies_in, copies_out):
        copy.wait()
        following.start()
    compact_half(1 - part, slot_ref, x_ref, peer_ref)
    for copy in copies_out:
        copy.wait()


def compact_join(part, slot, columns, stack, came):
    width = columns.shape[0]
    inner = 2 * stack.shape[1]
    shape = jax.ShapeDtypeStruct((width, LMAX), BF16)
    return call(
        compact_join_kernel,
        "compact_join",
        2 * width * 2 * 4608 * 256,
        width * 2048 * 4,
        24,
        in_specs=[SMEM, VMEM, VMEM, ANY, ANY],
        out_specs=[VMEM, VMEM, ANY, ANY],
        out_shape=[
            shape,
            shape,
            jax.ShapeDtypeStruct((3 * inner, D), BF16),
            jax.ShapeDtypeStruct((inner, D), BF16),
        ],
        scratch_shapes=[
            pltpu.VMEM((4, 2, inner // 2, D), BF16), pltpu.SemaphoreType.DMA((4, 2, 2))
        ],
    )(part, slot, columns, stack, came)


def compact(part, slot, columns):
    width = columns.shape[0]
    shape = jax.ShapeDtypeStruct((width, LMAX), BF16)
    return call(
        compact_kernel,
        "compact",
        2 * width * 2 * 4608 * 256,
        width * 2048 * 4,
        16,
        in_specs=[SMEM, VMEM, VMEM],
        out_specs=[VMEM, VMEM],
        out_shape=[shape, shape],
    )(part, slot, columns)


def spread_kernel(part_ref, slot_ref, own_ref, peer_ref, out_ref):
    first = part_ref[0] == 0
    items = (
        jnp.where(first, own_ref[...], peer_ref[...]),
        jnp.where(first, peer_ref[...], own_ref[...]),
    )
    for block in range(ROWS_DEV // QBLOCK):
        end = (block + 1) * QBLOCK
        slots = slot_ref[:, end - QBLOCK : end]
        total = None
        for item in range(2):
            reach = min(end - 512 * item, LMAX)
            if reach <= 0 or (item == 0 and end > LMAX):
                continue
            ids = item * LMAX + lax.broadcasted_iota(jnp.int32, (reach, 1), 0)
            hot = (slots == ids).astype(F32).astype(BF16)
            part = dot(items[item][:, :reach], hot, NN)
            total = part if total is None else total + part
        out_ref[:, end - QBLOCK : end] = total.astype(BF16)


def spread(part, slot, own, peer):
    width = own.shape[0]
    return call(
        spread_kernel,
        "spread",
        2 * width * 7168 * 256,
        width * 2048 * 4,
        16,
        in_specs=[SMEM, VMEM, VMEM, VMEM],
        out_specs=VMEM,
        out_shape=jax.ShapeDtypeStruct((width, ROWS_DEV), BF16),
    )(part, slot, own, peer)


COLUMNS = 3
ROWS = pl.BlockSpec((D, QBLOCK), lambda i: (0, i))
LINE = pl.BlockSpec((1, QBLOCK), lambda i: (0, i))
COLUMN = pl.BlockSpec((D, COLUMNS), lambda i: (0, 0))
SUMS = pl.BlockSpec((D, 128), lambda i: (0, 0))


def fixed_spec(shape):
    return pl.BlockSpec(shape, lambda i: (0,) * len(shape), pipeline_mode=pl.Buffered(1))


def whole_spec(array):
    return fixed_spec(array.shape)


def line(rows=1, dtype=F32):
    return jax.ShapeDtypeStruct((rows, LMAX), dtype)


def folded(values):
    return sum(values[:, i * 128 : (i + 1) * 128] for i in range(values.shape[1] // 128))


def input_kernel(
    part_ref, own_ref, came_ref, gain_ref, weight_ref, count_ref,
    state_ref, normed_ref, qkv_ref, gate_ref, logit_ref, scale_ref,
):
    first = part_ref[0] == 0
    own, came = own_ref[...], came_ref[...]
    half = own.shape[0]
    state_ref[:half] = jnp.where(first, own, came)
    state_ref[half:] = jnp.where(first, came, own)
    state = state_ref[...].astype(F32)
    scale = lax.rsqrt(jnp.sum(state * state, axis=0, keepdims=True) / D + EPSILON)
    normed = (state * scale * gain_ref[:, 0:1]).astype(BF16)
    normed_ref[...] = normed
    scale_ref[...] = scale
    qkv_ref[...] = dot(weight_ref[...], normed, NN).astype(BF16)
    logit = jnp.sum(normed.astype(F32) * gain_ref[:, 2:3], axis=0, keepdims=True)
    logit_ref[...] = logit
    gate = -DELETE_DEPTH * jax.nn.sigmoid(-logit)
    rows = pl.program_id(0) * QBLOCK + lax.broadcasted_iota(jnp.int32, (1, QBLOCK), 1)
    gate = jnp.where(rows < count_ref[:, :1], gate, NEG_LARGE)
    place = lax.broadcasted_iota(jnp.int32, (AUG, QBLOCK), 0)
    gate_ref[...] = jnp.where(place == 0, gate, 0.0).astype(BF16)


def input_part(part, own, came, gain, weights, count):
    inner = weights.shape[0]
    half = pl.BlockSpec((own.shape[0], QBLOCK), lambda i: (0, i))
    return call(
        input_kernel,
        "norm_project",
        2 * D * LMAX * weights.shape[0],
        D * LMAX * 10,
        24,
        grid=(LMAX // QBLOCK,),
        in_specs=[SMEM, half, half, COLUMN, whole_spec(weights), whole_spec(count)],
        out_specs=[
            ROWS,
            ROWS,
            pl.BlockSpec((inner, QBLOCK), lambda i: (0, i)),
            pl.BlockSpec((AUG, QBLOCK), lambda i: (0, i)),
            LINE,
            LINE,
        ],
        out_shape=[line(D, BF16), line(D, BF16), line(inner, BF16), line(AUG, BF16), line(), line()],
    )(part, own, came, gain, weights, count)


def middle_kernel(weight_ref, attended_ref, state_ref, gain_ref, mid_ref, normed_ref, scale_ref):
    mid = state_ref[...].astype(F32) + dot(weight_ref[...], attended_ref[...], TN)
    scale = lax.rsqrt(jnp.sum(mid * mid, axis=0, keepdims=True) / D + EPSILON)
    mid_ref[...] = mid
    scale_ref[...] = scale
    normed_ref[...] = (mid * scale * gain_ref[:, 1:2]).astype(BF16)


def middle_part(weights, attended, state, gain):
    inner = attended.shape[0]
    return call(
        middle_kernel,
        "attention_out_norm",
        2 * D * LMAX * inner,
        D * LMAX * 8,
        24,
        grid=(LMAX // QBLOCK,),
        in_specs=[
            whole_spec(weights),
            pl.BlockSpec((inner, QBLOCK), lambda i: (0, i)),
            ROWS,
            COLUMN,
        ],
        out_specs=[ROWS, ROWS, LINE],
        out_shape=[line(D), line(D, BF16), line()],
    )(weights, attended, state, gain)


def middle_back_kernel(
    gate_ref, up_ref, gg_ref, gu_ref, came_ref, mid_ref, cot_ref, gain_ref, scale_ref, weight_ref,
    grad_mid_ref, grad_attn_ref, attended_ref, sums_ref,
):
    grad = dot(gate_ref[...], gg_ref[...], NN) + dot(up_ref[...], gu_ref[...], NN)
    grad = grad + came_ref[...].astype(F32)
    mid, scale = mid_ref[...], scale_ref[...]
    weighted = grad * gain_ref[:, 1:2]
    inner = jnp.sum(weighted * mid, axis=0, keepdims=True)
    grad_mid = (
        cot_ref[...].astype(F32) + scale * weighted - mid * (scale * scale * scale * inner / D)
    )
    grad_mid_ref[...] = grad_mid
    grad_attn = grad_mid.astype(BF16)
    grad_attn_ref[...] = grad_attn
    attended_ref[...] = dot(weight_ref[...], grad_attn, NN).astype(BF16)

    @pl.when(pl.program_id(0) == 0)
    def _():
        sums_ref[...] = jnp.zeros_like(sums_ref)

    sums_ref[...] += folded(grad * (mid * scale))


def middle_back(w_gate, w_up, gg, gu, came, mid, cot, gain, scale, w_out):
    inner, units = w_out.shape[0], w_gate.shape[1]
    unit_rows = pl.BlockSpec((units, QBLOCK), lambda i: (0, i))
    return call(
        middle_back_kernel,
        "norm_back",
        4 * D * LMAX * units,
        D * LMAX * 20 + 4 * D * units,
        44,
        grid=(LMAX // QBLOCK,),
        in_specs=[
            whole_spec(w_gate), whole_spec(w_up), unit_rows, unit_rows, ROWS, ROWS, ROWS, COLUMN,
            LINE, whole_spec(w_out),
        ],
        out_specs=[ROWS, ROWS, pl.BlockSpec((inner, QBLOCK), lambda i: (0, i)), SUMS],
        out_shape=[
            line(D), line(D, BF16), line(inner, BF16), jax.ShapeDtypeStruct((D, 128), F32),
        ],
    )(w_gate, w_up, gg, gu, came, mid, cot, gain, scale, w_out)


def input_back_block(q, k, v, weight_ref, normed, state, grad_mid, scale, logit, sums, columns):
    heads = sums.shape[0]
    gate = sums[0]
    for head in range(1, heads):
        gate = gate + sums[head]
    gate = jnp.sum(gate, axis=0, keepdims=True)
    grad_logit = gate * DELETE_DEPTH * jax.nn.sigmoid(logit) * jax.nn.sigmoid(-logit)
    inner = q.shape[0]
    grad = dot(weight_ref[:inner], q, TN)
    grad = grad + dot(weight_ref[inner : 2 * inner], k, TN)
    grad = grad + dot(weight_ref[2 * inner : 3 * inner], v, TN)
    grad = grad + columns[:, 2:3] * grad_logit
    state = state.astype(F32)
    weighted = grad * columns[:, 0:1]
    total = jnp.sum(weighted * state, axis=0, keepdims=True)
    grad_state = grad_mid + scale * weighted - state * (scale * scale * scale * total / D)
    gain_part = folded(grad * (state * scale))
    delete_part = folded(normed.astype(F32) * grad_logit)
    return grad_state.astype(BF16), gain_part, delete_part


def input_back_kernel(
    q_ref, k_ref, v_ref, weight_ref, normed_ref, state_ref, grad_mid_ref, scale_ref, logit_ref,
    sums_ref, columns_ref, grad_ref, gain_sum_ref, delete_sum_ref,
):
    grad_ref[...], gain_part, delete_part = input_back_block(
        q_ref[...], k_ref[...], v_ref[...], weight_ref, normed_ref[...], state_ref[...],
        grad_mid_ref[...], scale_ref[...], logit_ref[...], sums_ref[...], columns_ref[...],
    )

    @pl.when(pl.program_id(0) == 0)
    def _():
        gain_sum_ref[...] = jnp.zeros_like(gain_sum_ref)
        delete_sum_ref[...] = jnp.zeros_like(delete_sum_ref)

    gain_sum_ref[...] += gain_part
    delete_sum_ref[...] += delete_part


def input_back(side, q, k, v, weights, normed, state, grad_mid, scale, logit, sums, gain):
    inner = q.shape[0]
    head_rows = pl.BlockSpec((inner, QBLOCK), lambda i: (0, i))
    return call(
        input_back_kernel,
        "project_norm_back",
        6 * D * LMAX * inner,
        D * LMAX * 12,
        28,
        side=side,
        grid=(LMAX // QBLOCK,),
        in_specs=[
            head_rows, head_rows, head_rows, whole_spec(weights), ROWS, ROWS, ROWS, LINE, LINE,
            pl.BlockSpec((sums.shape[0], sums.shape[1], QBLOCK), lambda i: (0, 0, i)),
            COLUMN,
        ],
        out_specs=[ROWS, SUMS, SUMS],
        out_shape=[
            line(D, BF16),
            jax.ShapeDtypeStruct((D, 128), F32),
            jax.ShapeDtypeStruct((D, 128), F32),
        ],
    )(q, k, v, weights, normed, state, grad_mid, scale, logit, sums, gain)


def mixed_kernel(down_ref, hid_ref, came_ref, mid_ref, out_ref):
    mixed = mid_ref[...] + dot(down_ref[...], hid_ref[...], NN)
    out_ref[...] = (mixed + came_ref[...].astype(F32)).astype(BF16)


def mixed_part(down, hid, came, mid):
    width = D // 4
    units = down.shape[1]
    rows = pl.BlockSpec((width, LMAX), lambda i: (i, 0))
    return call(
        mixed_kernel,
        "mixed",
        2 * D * LMAX * units,
        D * LMAX * 8 + D * units * 2,
        24,
        grid=(D // width,),
        in_specs=[pl.BlockSpec((width, units), lambda i: (i, 0)), whole_spec(hid), rows, rows],
        out_specs=rows,
        out_shape=line(D, BF16),
    )(down, hid, came, mid)


def head_grad_kernel(part_ref, q_ref, v_ref, k_ref, attended_ref, normed_ref, back_ref, *outs):
    keep_ref, give_ref, hold = outs
    part = part_ref[0]
    rows = hold.shape[0] // 2
    pieces = (
        (q_ref, normed_ref), (v_ref, normed_ref), (k_ref, normed_ref), (attended_ref, back_ref),
    )
    for place, (left, right) in enumerate(pieces):
        hold[...] = dot(left[...], right[...], NT).astype(BF16)
        keep_ref[place] = hold[pl.ds(pl.multiple_of(part * rows, 16), rows)]
        give_ref[place] = hold[pl.ds(pl.multiple_of((1 - part) * rows, 16), rows)]


def head_grads(part, q, k, v, normed, attended, back):
    inner = q.shape[0]
    shape = jax.ShapeDtypeStruct((4, inner // 2, D), BF16)
    return call(
        head_grad_kernel,
        "head_grads",
        8 * D * LMAX * inner,
        D * LMAX * 4 + 4 * LMAX * inner * 2 + 16 * inner * D,
        36,
        in_specs=[SMEM] + [VMEM] * 6,
        out_specs=[VMEM, VMEM],
        out_shape=[shape, shape],
        scratch_shapes=[pltpu.VMEM((inner, D), BF16)],
    )(part, q, v, k, attended, normed, back)


MESH = pl.DeviceIdType.MESH


class Sender:
    def __init__(self, send_sems, recv_sems):
        self.send_sems, self.recv_sems, self.made = send_sems, recv_sems, []

    def start(self, source, target, device):
        place = len(self.made)
        copy = pltpu.make_async_remote_copy(
            src_ref=source,
            dst_ref=target,
            send_sem=self.send_sems.at[place],
            recv_sem=self.recv_sems.at[place],
            device_id=device,
            device_id_type=MESH,
        )
        copy.start()
        self.made.append(copy)
        return copy

    def finish(self):
        for copy in self.made:
            copy.wait_send()


def arrived(copies):
    for copy in copies:
        copy.wait_recv()


def plus(first, *others):
    total = first.astype(F32)
    for other in others:
        total = total + other.astype(F32)
    return total


def neighbours():
    me, part = lax.axis_index("dp"), lax.axis_index("mp")
    x, y, z = me % 2, (me // 2) % 2, me // 4
    across_x, across_y = 1 - 2 * x, 2 - 4 * y
    planes = [(z + k) % 4 for k in range(1, 4)]
    return dict(
        x=x,
        y=y,
        z=z,
        part=part,
        planes=planes,
        to_core=(me, 1 - part),
        to_x=(me + across_x, part),
        to_y=(me + across_y, part),
        to_corner=(me + across_x + across_y, part),
        to_plane=[(p * 4 + me % 4, part) for p in planes],
    )


def meet(devices):
    barrier = pltpu.get_barrier_semaphore()
    for device in devices:
        pl.semaphore_signal(barrier, inc=1, device_id=device, device_id_type=MESH)
    pl.semaphore_wait(barrier, len(devices))


CHUNK = 16


def tail_kernel(
    keep_ref, give_ref, keep_x, came_x, keep_y, came_y, ffn_sum_ref, near_ref,
    q_ref, k_ref, v_ref, weight_ref, normed_ref, state_ref, grad_mid_ref, scale_ref, logit_ref,
    sums_ref, columns_ref,
    out_ref, share_ref, vector_ref, own_ref, came_grad_ref,
    came_ref, total, from_x, from_y, sum_x, sum_y, last_x, last_y, plane_sum, from_planes,
    give_x, give_y, second_x, second_y, whole, from_whole,
    vector, vector_core, vector_near, vector_far, grad_state, send_sems, recv_sems,
):
    at = neighbours()
    x, y, z = at["x"], at["y"], at["z"]
    to_x, to_y = at["to_x"], at["to_y"]
    rows = keep_ref.shape[3]
    chunks = [slice(c * CHUNK, (c + 1) * CHUNK) for c in range(rows // CHUNK)]
    sender = Sender(send_sems, recv_sems)
    meet([at["to_core"], to_x, to_y, at["to_corner"], *at["to_plane"]])

    cores = [
        sender.start(give_ref.at[:, :, :, c], came_ref.at[:, :, :, c], at["to_core"])
        for c in chunks
    ]
    give_x[...] = plus(keep_x[:, 1 - y], came_x[:, 1 - y]).astype(BF16)
    give_y[...] = plus(keep_y[:, 1 - x], came_y[:, 1 - x]).astype(BF16)

    def first(c):
        arrived([cores[c]])
        c = chunks[c]
        total[:, :, :, c] = plus(keep_ref[:, :, :, c], came_ref[:, :, :, c]).astype(BF16)
        return [
            sender.start(total.at[0:2, :, 1 - x, c], from_x.at[:, :, c], to_x),
            sender.start(total.at[2:4, 1 - y, :, c], from_y.at[:, :, c], to_y),
        ]

    def second(c, copies):
        arrived(copies)
        c = chunks[c]
        sum_x[:, :, c] = plus(total[0:2, :, x, c], from_x[:, :, c]).astype(BF16)
        sum_y[:, :, c] = plus(total[2:4, y, :, c], from_y[:, :, c]).astype(BF16)
        return [
            sender.start(sum_x.at[:, 1 - y, c], last_x.at[:, c], to_y),
            sender.start(sum_y.at[:, 1 - x, c], last_y.at[:, c], to_x),
        ]

    def third(c, copies):
        arrived(copies)
        c = chunks[c]
        plane_sum[0:2, c] = plus(sum_x[:, y, c], last_x[:, c]).astype(BF16)
        plane_sum[2:4, c] = plus(sum_y[:, x, c], last_y[:, c]).astype(BF16)
        return [
            sender.start(plane_sum.at[p, c], from_planes.at[k, c], device)
            for k, (p, device) in enumerate(zip(at["planes"], at["to_plane"]))
        ]

    def fourth(c, copies):
        arrived(copies)
        c = chunks[c]
        got = [from_planes[k, c] for k in range(3)]
        out_ref[z, y, x, c] = plus(plane_sum[z, c], *got).astype(BF16)
        here = out_ref.at[z, y, x, c]
        return [sender.start(here, here, device) for device in at["to_plane"]]

    def fifth(c, copies):
        arrived(copies)
        c = chunks[c]
        here_x, here_y = out_ref.at[0:2, y, x, c], out_ref.at[2:4, y, x, c]
        return [sender.start(here_x, here_x, to_y), sender.start(here_y, here_y, to_x)]

    def sixth(c, copies):
        arrived(copies)
        c = chunks[c]
        here_x, here_y = out_ref.at[0:2, :, x, c], out_ref.at[2:4, y, :, c]
        return [sender.start(here_x, here_x, to_x), sender.start(here_y, here_y, to_y)]

    stages = [first, second, third, fourth, fifth, sixth]
    flying = [None] * len(chunks)

    def advance(c, stage):
        flying[c] = stages[stage](c, flying[c]) if stage else first(c)

    half = own_ref.shape[0]
    mine = pl.ds(pl.multiple_of(at["part"] * half, 16), half)
    other = pl.ds(pl.multiple_of((1 - at["part"]) * half, 16), half)
    parts = []
    came_grads = []

    def compute(block):
        cols = slice(block * QBLOCK, (block + 1) * QBLOCK)
        grad, gain_part, delete_part = input_back_block(
            q_ref[:, cols], k_ref[:, cols], v_ref[:, cols], weight_ref, normed_ref[:, cols],
            state_ref[:, cols], grad_mid_ref[:, cols], scale_ref[:, cols], logit_ref[:, cols],
            sums_ref[:, :, cols], columns_ref[...],
        )
        grad_state[:, cols] = grad
        own_ref[:, cols] = grad_state[mine, cols]
        came_grads.append(
            sender.start(grad_state.at[other, cols], came_grad_ref.at[:, cols], at["to_core"])
        )
        parts.append((gain_part, delete_part))

    advance(0, 0)
    seconds = [
        sender.start(give_x, second_x, to_y),
        sender.start(give_y, second_y, to_x),
    ]
    advance(1, 0)
    advance(2, 0)
    compute(0)
    advance(0, 1)
    compute(1)
    advance(1, 1)
    advance(0, 2)
    arrived(seconds)
    cut = keep_x.shape[2]
    whole[:, :cut] = plus(keep_x[:, y], came_x[:, y], second_x[...]).astype(BF16)
    whole[:, cut:] = plus(keep_y[:, x], came_y[:, x], second_y[...]).astype(BF16)
    wholes = [
        sender.start(whole.at[p], from_whole.at[k], device)
        for k, (p, device) in enumerate(zip(at["planes"], at["to_plane"]))
    ]
    compute(2)
    advance(2, 1)
    advance(1, 2)
    advance(0, 3)
    compute(3)
    advance(2, 2)
    advance(1, 3)
    advance(0, 4)

    ones = jnp.ones((8, 128), F32)

    def line_of(values):
        return lax.dot_general(
            ones, values, NT, preferred_element_type=F32, precision=lax.Precision.HIGHEST
        )[:1]

    vector[...] = jnp.zeros_like(vector)
    vector[0:1] = line_of(ffn_sum_ref[...])
    vector[1:2] = line_of(sum(p[0] for p in parts))
    vector[2:3] = line_of(sum(p[1] for p in parts))
    vector[3:4, : near_ref.shape[0]] = line_of(near_ref[...])
    vectors = [sender.start(vector, vector_core, at["to_core"])]
    advance(2, 3)
    advance(1, 4)
    advance(0, 5)
    arrived(vectors)
    vector_core[...] = vector_core[...] + vector[...]
    vectors = [
        sender.start(vector_core, vector_near.at[k], device)
        for k, device in enumerate((to_x, to_y, at["to_corner"]))
    ]
    advance(2, 4)
    advance(1, 5)
    arrived(vectors)
    vector_ref[...] = vector_core[...] + vector_near[0] + vector_near[1] + vector_near[2]
    vectors = [
        sender.start(vector_ref, vector_far.at[k], device)
        for k, device in enumerate(at["to_plane"])
    ]
    advance(2, 5)
    arrived(wholes)
    share_ref[...] = plus(whole[z], from_whole[0], from_whole[1], from_whole[2])
    for copies in flying:
        arrived(copies)
    arrived(came_grads)
    arrived(vectors)
    sender.finish()
    vector_ref[...] = vector_ref[...] + vector_far[0] + vector_far[1] + vector_far[2]


def tail(keep, give, up_x, up_y, ffn_sum, near, *values):
    rows = keep.shape[1] // 4
    (keep_x, came_x), (keep_y, came_y) = up_x, up_y
    cut, rest = keep_x.shape[2], keep_y.shape[2]
    share = cut + rest
    shape = (4, 2, 2, rows, D)
    copies = 80

    def hold(*dims, dtype=BF16):
        return pltpu.VMEM(dims, dtype)

    return pl.pallas_call(
        tail_kernel,
        name="tail",
        in_specs=[VMEM] * (8 + len(values)),
        out_specs=[VMEM] * 5,
        out_shape=[
            jax.ShapeDtypeStruct(shape, BF16),
            jax.ShapeDtypeStruct((share, D), F32),
            jax.ShapeDtypeStruct((8, D), F32),
            jax.ShapeDtypeStruct((D // 2, LMAX), BF16),
            jax.ShapeDtypeStruct((D // 2, LMAX), BF16),
        ],
        scratch_shapes=[
            hold(*shape), hold(*shape), hold(2, 2, rows, D), hold(2, 2, rows, D),
            hold(2, 2, rows, D), hold(2, 2, rows, D), hold(2, rows, D), hold(2, rows, D),
            hold(4, rows, D), hold(3, rows, D),
            hold(4, cut, D), hold(4, rest, D), hold(4, cut, D), hold(4, rest, D),
            hold(4, share, D), hold(3, share, D),
            hold(8, D, dtype=F32), hold(8, D, dtype=F32), hold(3, 8, D, dtype=F32),
            hold(3, 8, D, dtype=F32), hold(D, LMAX),
            pltpu.SemaphoreType.DMA((copies,)),
            pltpu.SemaphoreType.DMA((copies,)),
        ],
        cost_estimate=pl.CostEstimate(
            flops=6 * D * LMAX * 384, bytes_accessed=60 << 20, transcendentals=0
        ),
        compiler_params=pltpu.CompilerParams(
            vmem_limit_bytes=63 << 20, collective_id=1, has_side_effects=True
        ),
    )(keep.reshape(shape), give.reshape(shape), keep_x, came_x, keep_y, came_y, ffn_sum, near, *values)


STRIP = LMAX + LMAX - TILE


def offsets(shift):
    keys = lax.broadcasted_iota(jnp.int32, (TILE, TILE), 0)
    queries = lax.broadcasted_iota(jnp.int32, (TILE, TILE), 1)
    return shift * TILE + keys - queries


def strip_kernel(table_ref, strip_ref):
    head = pl.program_id(0)
    middle = LMAX - TILE

    def value(bucket):
        return table_ref[bucket, head]

    def side(distance, base, start):
        tile = jnp.full((TILE, TILE), start, F32)
        for count, step in enumerate(NEAR_STEPS):
            tile = jnp.where(distance >= step, value(base + count + 1), tile)
        return tile

    strip_ref[0, : middle - TILE, :] = jnp.full((middle - TILE, TILE), value(15), F32)
    strip_ref[0, middle + 2 * TILE :, :] = jnp.full((STRIP - middle - 2 * TILE, TILE), value(31), F32)
    before = offsets(-1)
    strip_ref[0, middle - TILE : middle, :] = side(-before, 0, value(0))
    relative = offsets(0)
    strip_ref[0, middle : middle + TILE, :] = jnp.where(
        relative > 0, side(relative, 16, value(0)), side(-relative, 0, value(0))
    )
    after = offsets(1)
    strip_ref[0, middle + TILE : middle + 2 * TILE, :] = side(after, 16, value(0))


def bias_strip(table, heads):
    return call(
        strip_kernel,
        "bias_strip",
        heads * 3e6,
        heads * STRIP * TILE * 4,
        8,
        grid=(heads,),
        in_specs=[SMEM],
        out_specs=pl.BlockSpec((1, STRIP, TILE), lambda h: (h, 0, 0)),
        out_shape=jax.ShapeDtypeStruct((heads, STRIP, TILE), F32),
    )(table)


def attend_kernel(
    part_ref, q_ref, k_ref, v_ref, gate_ref, strip_ref, own_ref, peer_ref, came_own_ref, came_peer_ref,
    prob_ref, out_ref, wide_ref, cot_own_ref, cot_peer_ref, hold, sems,
):
    head = pl.program_id(0)
    part = part_ref[0]
    copies_in, copies_out = halves(part, own_ref, came_own_ref, cot_own_ref, hold.at[0], sems.at[0])
    ins, outs = halves(part, peer_ref, came_peer_ref, cot_peer_ref, hold.at[1], sems.at[1])
    copies_in, copies_out = copies_in + ins, copies_out + outs

    @pl.when(head == 0)
    def _():
        for copy in copies_in:
            copy.start()

    @pl.when(head == 2)
    def _():
        for copy, following in zip(copies_in, copies_out):
            copy.wait()
            following.start()

    ones = (lax.broadcasted_iota(jnp.int32, (AUG, LMAX), 0) == 0).astype(F32).astype(BF16)
    scale = HDIM ** (-0.5)
    queries = jnp.concatenate([(q_ref[...].astype(F32) * scale).astype(BF16), ones], axis=0)
    keys = jnp.concatenate([k_ref[...], gate_ref[...]], axis=0)
    for block in range(LMAX // ABLOCK):
        low = block * ABLOCK
        scores = dot(keys, queries[:, low : low + ABLOCK], TN)
        bias = []
        for sub in range(ABLOCK // TILE):
            start = LMAX - TILE - (low + sub * TILE)
            bias.append(strip_ref[0, start : start + LMAX, :])
        scores = scores + jnp.concatenate(bias, axis=1)
        top = jnp.max(scores, axis=0, keepdims=True)
        weights = jnp.exp(scores - top)
        total = jnp.sum(weights, axis=0, keepdims=True)
        prob = (weights * (1.0 / total)).astype(BF16)
        prob_ref[0, :, low : low + ABLOCK] = prob
        out = dot(v_ref[...], prob, NN)
        wide_ref[:, low : low + ABLOCK] = out
        out_ref[:, low : low + ABLOCK] = out.astype(BF16)

    @pl.when(head == pl.num_programs(0) - 1)
    def _():
        for copy in copies_out:
            copy.wait()


def attend(part, qkv, gate, strip, own, peer, came_own, came_peer, heads):
    return call(
        attend_kernel,
        "attend",
        heads * 4 * LMAX * LMAX * HDIM * 4,
        heads * LMAX * LMAX * 2,
        36,
        grid=(heads,),
        in_specs=[
            SMEM,
            pl.BlockSpec((HDIM, LMAX), lambda h: (h, 0)),
            pl.BlockSpec((HDIM, LMAX), lambda h: (heads + h, 0)),
            pl.BlockSpec((HDIM, LMAX), lambda h: (2 * heads + h, 0)),
            pl.BlockSpec((AUG, LMAX), lambda h: (0, 0)),
            pl.BlockSpec((1, STRIP, TILE), lambda h: (h, 0, 0)),
            ANY, ANY, ANY, ANY,
        ],
        out_specs=[
            pl.BlockSpec((1, LMAX, LMAX), lambda h: (h, 0, 0)),
            pl.BlockSpec((HDIM, LMAX), lambda h: (h, 0)),
            pl.BlockSpec((HDIM, LMAX), lambda h: (h, 0)),
            ANY, ANY,
        ],
        out_shape=[
            jax.ShapeDtypeStruct((heads, LMAX, LMAX), BF16),
            jax.ShapeDtypeStruct((heads * HDIM, LMAX), BF16),
            jax.ShapeDtypeStruct((heads * HDIM, LMAX), F32),
            line(D, BF16), line(D, BF16),
        ],
        scratch_shapes=[
            pltpu.VMEM((2, 2, D // 2, LMAX), BF16), pltpu.SemaphoreType.DMA((2, 2, 2))
        ],
    )(part, qkv, qkv, qkv, gate, strip, own, peer, came_own, came_peer)


def attend_back_kernel(
    q_ref, k_ref, v_ref, prob_ref, go_ref, wide_ref, gq_ref, gk_ref, gv_ref, sums_ref, near_ref
):
    scale = HDIM ** (-0.5)
    blocks = LMAX // TILE
    member = (
        lax.broadcasted_iota(jnp.int32, (AUG, LMAX), 0)
        == lax.broadcasted_iota(jnp.int32, (AUG, LMAX), 1) // TILE
    )
    queries = jnp.concatenate([q_ref[...], member.astype(F32).astype(BF16)], axis=0)
    near = [jnp.zeros((TILE, TILE), F32) for _ in range(3)]
    key_total = jnp.zeros((HDIM + AUG, LMAX), F32)
    val_total = jnp.zeros((HDIM, LMAX), F32)
    for block in range(LMAX // ABLOCK):
        low = block * ABLOCK
        prob = prob_ref[0, :, low : low + ABLOCK]
        grad_out = go_ref[:, low : low + ABLOCK]
        soft = prob.astype(F32)
        grad_prob = dot(v_ref[...], grad_out, TN)
        wide = wide_ref[:, low : low + ABLOCK]
        inner = jnp.sum(grad_out.astype(F32) * wide, axis=0, keepdims=True)
        grad_scores = (soft * (grad_prob - inner)).astype(BF16)
        gq_ref[:, low : low + ABLOCK] = (dot(k_ref[...], grad_scores, NN) * scale).astype(BF16)
        key_total = key_total + dot(queries[:, low : low + ABLOCK], grad_scores, NT)
        val_total = val_total + dot(grad_out, prob, NT)
        for sub in range(ABLOCK // TILE):
            place = block * (ABLOCK // TILE) + sub
            for shift in (-1, 0, 1):
                at = place + shift
                if 0 <= at < blocks:
                    piece = grad_scores[at * TILE : (at + 1) * TILE, sub * TILE : (sub + 1) * TILE]
                    near[shift + 1] = near[shift + 1] + piece.astype(F32)
    gk_ref[...] = (key_total[:HDIM] * scale).astype(BF16)
    gv_ref[...] = val_total.astype(BF16)
    sums = key_total[HDIM : HDIM + blocks]
    sums_ref[0] = sums
    shifts = (
        lax.broadcasted_iota(jnp.int32, (blocks, LMAX), 1) // TILE
        - lax.broadcasted_iota(jnp.int32, (blocks, LMAX), 0)
    )

    def fold(tile):
        return jnp.sum(tile, axis=0, keepdims=True)

    def far(chosen):
        return folded(fold(jnp.where(chosen, sums, 0.0)))

    before, same, after = near
    for sign, base, other, shift in ((-1, 0, before, -1), (1, 16, after, 1)):
        near_offset = sign * offsets(0)
        far_offset = sign * offsets(shift)
        floor = 0 if sign < 0 else 1
        last = fold(jnp.where(near_offset >= floor, same, 0.0)) + fold(
            jnp.where(far_offset >= floor, other, 0.0)
        )
        for count, step in enumerate(NEAR_STEPS):
            following = fold(jnp.where(near_offset >= step, same, 0.0)) + fold(
                jnp.where(far_offset >= step, other, 0.0)
            )
            near_ref[0, base + count : base + count + 1] = last - following
            last = following
        near_ref[0, base + 15 : base + 16] = last + far(sign * shifts >= 2)


def attend_back(side, qkv, prob, grad_attended, wide, heads):
    blocks = LMAX // TILE
    rows = jax.ShapeDtypeStruct((heads * HDIM, LMAX), BF16)
    spec = pl.BlockSpec((HDIM, LMAX), lambda h: (h, 0))
    return call(
        attend_back_kernel,
        "attend_back",
        heads * 8 * LMAX * LMAX * HDIM * 4,
        heads * LMAX * LMAX * 2,
        28,
        side=side,
        grid=(heads,),
        in_specs=[
            spec,
            pl.BlockSpec((HDIM, LMAX), lambda h: (heads + h, 0)),
            pl.BlockSpec((HDIM, LMAX), lambda h: (2 * heads + h, 0)),
            pl.BlockSpec((1, LMAX, LMAX), lambda h: (h, 0, 0)),
            spec,
            spec,
        ],
        out_specs=[
            spec,
            spec,
            spec,
            pl.BlockSpec((1, blocks, LMAX), lambda h: (h, 0, 0)),
            pl.BlockSpec((1, BUCKETS, TILE), lambda h: (h, 0, 0)),
        ],
        out_shape=[
            rows,
            rows,
            rows,
            jax.ShapeDtypeStruct((heads, blocks, LMAX), F32),
            jax.ShapeDtypeStruct((heads, BUCKETS, TILE), F32),
        ],
    )(qkv, qkv, qkv, prob, grad_attended, wide)


def ffn_kernel(gate_ref, up_ref, down_ref, x_ref, cot_ref, hid_ref, gg_ref, gu_ref):
    gate = dot(gate_ref[...], x_ref[...], TN)
    up = dot(up_ref[...], x_ref[...], TN)
    grad = dot(down_ref[...], cot_ref[...], TN)
    square = gate * gate
    bend = jnp.tanh(GELU_C * gate * (1.0 + 0.044715 * square))
    half = 0.5 * (1.0 + bend)
    gelu = gate * half
    slope = half + 0.5 * gate * (1.0 - bend * bend) * (GELU_C * (1.0 + 3 * 0.044715 * square))
    hid_ref[...] = (gelu * up).astype(BF16)
    gg_ref[...] = (grad * up * slope).astype(BF16)
    gu_ref[...] = (grad * gelu).astype(BF16)


def ffn(w_gate, w_up, w_down_t, normed, cot):
    units = w_gate.shape[1]
    width = 256
    weight = pl.BlockSpec((D, width), lambda i: (0, i))
    whole = fixed_spec((D, LMAX))
    out = pl.BlockSpec((width, LMAX), lambda i: (i, 0))
    shape = jax.ShapeDtypeStruct((units, LMAX), BF16)
    return call(
        ffn_kernel,
        "ffn",
        6 * D * units * LMAX,
        3 * D * units * 2 + 2 * D * LMAX * 2 + 3 * units * LMAX * 2,
        28,
        grid=(units // width,),
        in_specs=[weight, weight, weight, whole, whole],
        out_specs=[out, out, out],
        out_shape=[shape, shape, shape],
    )(w_gate, w_up, w_down_t, normed, cot)


def weight_grad_kernel(a_own, a_peer, b_own, b_peer, out_ref):
    total = dot(a_own[...], b_own[...], NT) + dot(a_peer[...], b_peer[...], NT)
    out_ref[...] = total.astype(BF16)


def weight_grad(a_own, a_peer, b_own, b_peer):
    units = a_own.shape[0]
    width = 256
    left = pl.BlockSpec((width, LMAX), lambda i: (i, 0))
    whole = fixed_spec((D, LMAX))
    return call(
        weight_grad_kernel,
        "weight_grad",
        4 * D * units * LMAX,
        4 * D * LMAX + 4 * units * LMAX + 2 * units * D,
        28,
        grid=(units // width,),
        in_specs=[left, left, whole, whole],
        out_specs=pl.BlockSpec((width, D), lambda i: (i, 0)),
        out_shape=jax.ShapeDtypeStruct((units, D), BF16),
    )(a_own, a_peer, b_own, b_peer)


def project_kernel(count, *refs):
    total = dot(refs[0][...], refs[count][...], NN)
    for i in range(1, count):
        total = total + dot(refs[i][...], refs[count + i][...], NN)
    refs[-1][...] = total.astype(refs[-1].dtype)


def project(side, weights, values, dtype):
    count = len(weights)
    units = weights[0].shape[1]
    width = D // 4
    weight = pl.BlockSpec((width, units), lambda i: (i, 0))
    whole = fixed_spec((units, LMAX))
    return call(
        functools.partial(project_kernel, count),
        "project",
        2 * count * D * units * LMAX,
        2 * count * (D * units + units * LMAX) + 4 * D * LMAX,
        28,
        side=side,
        grid=(D // width,),
        in_specs=[weight] * count + [whole] * count,
        out_specs=pl.BlockSpec((width, LMAX), lambda i: (i, 0)),
        out_shape=jax.ShapeDtypeStruct((D, LMAX), dtype),
    )(*weights, *values)


def split_grad_kernel(cut, bits_ref, a_own, a_peer, b_own, b_peer, *refs):
    keep_x, give_x, keep_y, give_y, hold = refs
    total = dot(a_own[...], b_own[...], NT) + dot(a_peer[...], b_peer[...], NT)
    hold[...] = total.reshape(hold.shape).astype(BF16)
    x, y = bits_ref[0], bits_ref[1]
    for other in range(2):
        keep_x[0, other] = hold[other, x, :cut]
        give_x[0, other] = hold[other, 1 - x, :cut]
        keep_y[0, other] = hold[y, other, cut:]
        give_y[0, other] = hold[1 - y, other, cut:]


def split_grad(cut, bits, a_own, a_peer, b_own, b_peer):
    units = a_own.shape[0]
    width = units // 4
    share = width // 4
    left = pl.BlockSpec((width, LMAX), lambda i: (i, 0))

    def out(rows):
        return pl.BlockSpec((1, 2, rows, D), lambda i: (i, 0, 0, 0))

    def shape(rows):
        return jax.ShapeDtypeStruct((4, 2, rows, D), BF16)

    return call(
        functools.partial(split_grad_kernel, cut),
        "weight_grad",
        4 * D * units * LMAX,
        4 * D * LMAX + 4 * units * LMAX + 2 * units * D,
        28,
        grid=(4,),
        in_specs=[SMEM, left, left, whole_spec(b_own), whole_spec(b_peer)],
        out_specs=[out(cut), out(cut), out(share - cut), out(share - cut)],
        out_shape=[shape(cut), shape(cut), shape(share - cut), shape(share - cut)],
        scratch_shapes=[pltpu.VMEM((2, 2, share, D), BF16)],
    )(bits, a_own, a_peer, b_own, b_peer)


def fold_kernel(bit_ref, keep_ref, came_ref, keep_out, give_out):
    mine = bit_ref[0]
    for out, which in ((keep_out, mine), (give_out, 1 - mine)):
        total = keep_ref[:, which].astype(F32) + came_ref[:, which].astype(F32)
        out[...] = total.astype(BF16)


def fold(bit, keep, came):
    outer, _, rows, width = keep.shape
    steps = 2 if outer % 2 == 0 else 1
    block = pl.BlockSpec((outer // steps, 2, rows, width), lambda i: (i, 0, 0, 0))
    out = pl.BlockSpec((outer // steps, rows, width), lambda i: (i, 0, 0))
    shape = jax.ShapeDtypeStruct((outer, rows, width), BF16)
    return call(
        fold_kernel,
        "fold",
        4 * keep.size,
        6 * keep.size,
        16,
        grid=(steps,),
        in_specs=[SMEM, block, block],
        out_specs=[out, out],
        out_shape=[shape, shape],
    )(bit.reshape(1), keep, came)


def across(values, bit):
    size = lax.axis_size("dp")
    return lax.ppermute(values, "dp", [(i, i ^ (1 << bit)) for i in range(size)])


def bit_of(bit):
    return (lax.axis_index("dp") >> bit) & 1


def join_kernel(count, bit_ref, *refs):
    keep_out, give_out = refs[4 * count :]
    mine = bit_ref[0]
    for i in range(count):
        keep_x, keep_y, came_x, came_y = refs[4 * i : 4 * i + 4]
        cut = keep_x.shape[2]
        for out, which in ((keep_out, mine), (give_out, 1 - mine)):
            total = keep_x[0, which].astype(F32) + came_x[0, which].astype(F32)
            out[0, i, :cut] = total.astype(BF16)
            total = keep_y[0, which].astype(F32) + came_y[0, which].astype(F32)
            out[0, i, cut:] = total.astype(BF16)


def join(bit, groups):
    count = len(groups)
    specs, args = [], []
    for group in groups:
        for array in group:
            rows = array.shape[1]
            specs.append(pl.BlockSpec((1, 2, rows, D), lambda i: (i, 0, 0, 0)))
            args.append(array.reshape(2, 2, rows, D))
    share = groups[0][0].shape[1] + groups[0][1].shape[1]
    out = pl.BlockSpec((1, count, share, D), lambda i: (i, 0, 0, 0))
    shape = jax.ShapeDtypeStruct((2, count, share, D), BF16)
    return call(
        functools.partial(join_kernel, count),
        "join",
        8 * count * share * D,
        24 * count * share * D,
        24,
        grid=(2,),
        in_specs=[SMEM] + specs,
        out_specs=[out, out],
        out_shape=[shape, shape],
    )(bit.reshape(1), *args)


def finish_groups(groups):
    count = len(groups)
    keep, give = join(bit_of(2), groups)
    share = keep.shape[2]
    came = across(give, 2)
    keep, give = fold(
        bit_of(3), keep.reshape(1, 2, count * share, D), came.reshape(1, 2, count * share, D)
    )
    came = across(give, 3)
    keep, came = keep.reshape(count, share, D), came.reshape(count, share, D)
    return [keep[i].astype(F32) + came[i].astype(F32) for i in range(count)]


def stacked(values, came, mine, axis):
    return jnp.where(mine == 0, jnp.stack([values, came], axis), jnp.stack([came, values], axis))


def sum_everywhere(keep, came):
    bits = lax.axis_size("dp").bit_length() - 1
    rows = keep.shape[1] // 4
    keep, came = (v.reshape(4, 2, 2, rows, D) for v in (keep, came))
    keep_x, give_x = fold(
        bit_of(0), keep[:2].reshape(4, 2, rows, D), came[:2].reshape(4, 2, rows, D)
    )
    keep_y, give_y = fold(
        bit_of(1), keep[2:].reshape(2, 2, 2 * rows, D), came[2:].reshape(2, 2, 2 * rows, D)
    )
    came_x, came_y = across(give_x, 0), across(give_y, 1)
    keep_x, give_x = fold(
        bit_of(1), keep_x.reshape(2, 2, rows, D), came_x.reshape(2, 2, rows, D)
    )
    keep_y, give_y = fold(
        bit_of(0), keep_y.reshape(2, 2, rows, D), came_y.reshape(2, 2, rows, D)
    )
    came_x, came_y = across(give_x, 1), across(give_y, 0)
    keep = jnp.concatenate([keep_x, keep_y], axis=0).reshape(2, 2, rows, D)
    came = jnp.concatenate([came_x, came_y], axis=0).reshape(2, 2, rows, D)
    keep, give = fold(bit_of(2), keep, came)
    came = across(give, 2)
    keep, give = fold(bit_of(3), keep.reshape(1, 2, rows, D), came.reshape(1, 2, rows, D))
    came = across(give, 3)
    total = (keep.astype(F32) + came.astype(F32)).astype(BF16)
    for bit in range(4, bits):
        total = (total.astype(F32) + across(total, bit).astype(F32)).astype(BF16)
    total = stacked(total, across(total, 3), bit_of(3), 1)
    total = stacked(total, across(total, 2), bit_of(2), 2).reshape(4, rows, D)
    total_x, total_y = total[:2], total[2:]
    total_x = stacked(total_x, across(total_x, 1), bit_of(1), 1)
    total_y = stacked(total_y, across(total_y, 0), bit_of(0), 1)
    total_x = stacked(total_x, across(total_x, 0), bit_of(0), 2)
    total_y = stacked(total_y, across(total_y, 1), bit_of(1), 1)
    return [v.reshape(4 * rows, D).astype(F32) for v in (*total_x, *total_y)]


def sum_small(values):
    bits = lax.axis_size("dp").bit_length() - 1
    values = values + swap(values)
    for bit in range(bits):
        values = values + across(values, bit)
    return values


def halve(values, order):
    size = lax.axis_size("dp")
    bits = size.bit_length() - 1
    index = lax.axis_index("dp")
    rows = values.shape[0] // size
    values = values.reshape((2,) * bits + (rows, values.shape[1]))
    left = list(range(bits - 1, -1, -1))
    for step, bit in enumerate(order):
        axis = left.index(bit)
        left.pop(axis)
        mine = (index >> bit) & 1
        keep = lax.dynamic_index_in_dim(values, mine, axis, keepdims=False)
        give = lax.dynamic_index_in_dim(values, 1 - mine, axis, keepdims=False)
        came = lax.ppermute(give, "dp", [(i, i ^ (1 << bit)) for i in range(size)])
        total = keep.astype(F32) + came.astype(F32)
        values = total if step == bits - 1 else total.astype(BF16)
    return values


def swap(values):
    return lax.ppermute(values, "mp", [(0, 1), (1, 0)])


def body(
    tokens,
    cotangent,
    lengths,
    keep_mask,
    ln_attn,
    w_query,
    w_key,
    w_value,
    w_attn_out,
    rel_table,
    w_delete,
    ln_ffn,
    w_gate,
    w_up,
    w_ffn_out,
):
    dev_count = lax.axis_size("dp")
    bits = dev_count.bit_length() - 1
    part = lax.axis_index("mp")
    inner = 2 * w_query.shape[1]
    heads = inner // HDIM
    half = tokens.shape[1]
    first = part == 0
    part_ref = part.reshape(1).astype(jnp.int32)

    def in_parts(own, peer, axis):
        return jnp.where(
            first, jnp.concatenate([own, peer], axis), jnp.concatenate([peer, own], axis)
        )

    def home(values):
        mine = lax.dynamic_slice_in_dim(values, part * half, half, 0)
        other = lax.dynamic_slice_in_dim(values, (1 - part) * half, half, 0)
        return spread(part_ref, slot, mine, swap(other)).T

    own_weights = (w_query.T, w_key.T, w_value.T, w_attn_out)
    slot, count, stack = places(part_ref, lengths, keep_mask.reshape(1, ROWS_DEV), own_weights)
    came_stack = swap(stack)
    own_tokens, peer_tokens = compact(part_ref, slot, tokens.T)
    came_tokens = swap(peer_tokens)
    own_cot, peer_cot, w_qkv, w_out = compact_join(
        part_ref, slot, cotangent.T, stack, came_stack
    )
    came_cot_own, came_cot_peer = swap(peer_cot), swap(own_cot)
    table = in_parts(rel_table, swap(rel_table), 1)
    strip = bias_strip(table, heads)
    columns = jnp.stack([ln_attn, ln_ffn, w_delete.astype(F32)], axis=1)

    state, normed_one, qkv, gate_rows, del_logit, scale_one = input_part(
        part_ref, own_tokens, came_tokens, columns, w_qkv, count
    )
    prob, attended, wide, cot_own, cot_peer = attend(
        part_ref, qkv, gate_rows, strip, own_cot, peer_cot, came_cot_own, came_cot_peer, heads
    )
    mid, normed_two, scale_two = middle_part(w_out, attended, state, columns)
    normed_two_peer = swap(normed_two)
    w_down_t = w_ffn_out.T
    hid_own, gg_own, gu_own = ffn(w_gate, w_up, w_down_t, normed_two, cot_own)
    hid_peer, gg_peer, gu_peer = ffn(w_gate, w_up, w_down_t, normed_two_peer, cot_peer)

    share = w_gate.shape[1] // dev_count
    split = bits == 4 and share % 16 == 0
    if split:
        cut = (share // 2 + 15) // 16 * 16
        my_bits = jnp.stack([bit_of(0), bit_of(1)])
        make = functools.partial(split_grad, cut, my_bits)
    else:
        make = weight_grad

    def first_step(pieces):
        if not split:
            return ()
        keep_x, give_x, keep_y, give_y = pieces
        return (
            (bit_of(1), keep_x, across(give_x, 0)),
            (bit_of(0), keep_y, across(give_y, 1)),
        )

    def second_step(folded_pieces):
        keep_x, give_x, keep_y, give_y = folded_pieces
        return keep_x, keep_y, across(give_x, 1), across(give_y, 0)

    def run(kernel, side, *args):
        out = kernel(side, *args)
        return out if side else (out, ())

    part_down = make(hid_own, hid_peer, cot_own, cot_peer)
    side_down = first_step(part_down)
    part_gate = make(gg_own, gg_peer, normed_two, normed_two_peer)
    side_gate = first_step(part_gate)
    part_up = make(gu_own, gu_peer, normed_two, normed_two_peer)
    side_up = first_step(part_up)
    gg_peer, gu_peer, gg_own, gu_own, _ = lax.optimization_barrier(
        (gg_peer, gu_peer, gg_own, gu_own, part_up)
    )
    back_peer, fold_down = run(project, side_down, (w_gate, w_up), (gg_peer, gu_peer), BF16)
    grad_mid, grad_attn, grad_attended, sum_ffn = middle_back(
        w_gate, w_up, gg_own, gu_own, swap(back_peer), mid, cot_own, columns, scale_two, w_out
    )
    (grad_q, grad_k, grad_v, sums, near), fold_gate = run(
        attend_back, side_gate, qkv, prob, grad_attended, wide, heads
    )
    keep, give = head_grads(part_ref, grad_q, grad_k, grad_v, normed_one, attended, grad_attn)
    back_args = (
        grad_q, grad_k, grad_v, w_qkv, normed_one, state, grad_mid, scale_one, del_logit, sums, columns
    )
    if split:
        grad_down, grad_gate = finish_groups([second_step(fold_down), second_step(fold_gate)])
        (_, keep_x, came_x), (_, keep_y, came_y) = side_up
        totals, grad_up, small, state_own, state_came = tail(
            keep, give, (keep_x, came_x), (keep_y, came_y), sum_ffn,
            near.reshape(heads * BUCKETS, TILE), *back_args,
        )
        total_q, total_v, total_k, total_out = totals.reshape(4, inner // 2, D).astype(F32)
        grad_tokens = spread(part_ref, slot, state_own, state_came).T
        grad_ln_ffn, grad_ln_attn, grad_w_delete = small[0], small[1], small[2]
        grad_table = small[3, : heads * BUCKETS].reshape(heads, BUCKETS).T
    else:
        total_q, total_v, total_k, total_out = sum_everywhere(keep, swap(give))
        order = tuple(range(bits))
        grad_down, grad_gate, grad_up = (halve(v, order) for v in (part_down, part_gate, part_up))
        grad_state, sum_attn, sum_delete = input_back((), *back_args)
        grad_tokens = home(grad_state)
        grad_table = jnp.sum(near, axis=2).T
        small = jnp.concatenate(
            [jnp.sum(v, axis=1) for v in (sum_ffn, sum_attn, sum_delete)]
            + [grad_table.reshape(-1)]
        )
        small = sum_small(small)
        grad_ln_ffn, grad_ln_attn = small[:D], small[D : 2 * D]
        grad_w_delete = small[2 * D : 3 * D]
        grad_table = small[3 * D :].reshape(BUCKETS, heads)

    mixed_peer = project((), (w_down_t,), (hid_peer,), BF16)
    mixed = mixed_part(w_down_t, hid_own, swap(mixed_peer), mid)

    def own_half(values):
        return lax.dynamic_slice_in_dim(values, part * half, half, 0)

    return (
        home(mixed),
        grad_tokens,
        own_half(grad_ln_attn),
        total_q.T,
        total_k.T,
        total_v.T,
        total_out,
        lax.dynamic_slice_in_dim(grad_table, part * (heads // 2), heads // 2, 1),
        grad_w_delete,
        own_half(grad_ln_ffn),
        grad_gate.T,
        grad_up.T,
        grad_down,
    )


def solution(mesh):
    return jax.shard_map(
        body,
        mesh=mesh,
        in_specs=(
            P("dp", "mp"),
            P("dp", "mp"),
            P("dp"),
            P("dp"),
            P(),
            P(None, "mp"),
            P(None, "mp"),
            P(None, "mp"),
            P("mp", None),
            P(None, "mp"),
            P(),
            P(),
            P(None, "mp"),
            P(None, "mp"),
            P("mp", None),
        ),
        out_specs=(
            P("dp", "mp"),
            P("dp", "mp"),
            P("mp"),
            P(None, "mp"),
            P(None, "mp"),
            P(None, "mp"),
            P("mp", None),
            P(None, "mp"),
            P(),
            P("mp"),
            P(None, ("mp", "dp")),
            P(None, ("mp", "dp")),
            P(("mp", "dp"), None),
        ),
        check_vma=False,
    )
```

time: 652 us -> 527 us (0.81)
  Pallas kernels: 236 us -> 400 us
  other arithmetic: 78 us -> 3.05 us
  waiting for transfers between devices: 142 us -> 79.1 us
  matrix products: 44.6 us -> 0 us
  local copies, waits for them, and re-layouts: 61.1 us -> 18.6 us
  blocking collectives: 38.9 us -> 0 us
  starting transfers between devices: 40.4 us -> 18.9 us
    pallas_call x6 -> x17, Pallas kernels: 91.6 us -> 314 us  [the longest x1 125 us: tail(): pl.pallas_call(tail_kernel, name='tail', in_specs=[VMEM] * (8 + len(value...]
    ppermute x24 -> x12, waiting for transfers between devices: 141 us -> 76.6 us  [across(): return lax.ppermute(values, 'dp', [(i, i ^ 1 << bit) for i in range(size)])]
    dot_general x7 -> x0, matrix products: 44.6 us -> none  [dot(): return lax.dot_general(a, b, dims, preferred_element_type=F32)]
    pallas_call x4 -> x1, Pallas kernels: 52.9 us -> 9.56 us  [project(): call(functools.partial(project_kernel, count), 'project', 2 * count * D *...]
    psum x1 -> x0, blocking collectives: 38.9 us -> none  [body(): small = lax.psum(small, ('dp', 'mp'))]
    convert_element_type x21 -> x0, other arithmetic: 30.9 us -> none  [the longest x15 16.2 us: halve(): values = total if step == bits - 1 else total.astype(BF16)]
    ppermute x24 -> x12, starting transfers between devices: 37.8 us -> 16.5 us  [across(): return lax.ppermute(values, 'dp', [(i, i ^ 1 << bit) for i in range(size)])]
    dynamic_slice x6 -> x0, local copies, waits for them, and re-layouts: 13.8 us -> none  [the longest x3 9.17 us: halve(): keep = lax.dynamic_index_in_dim(values, mine, axis, keepdims=False)]
  transfers between devices with their start and end apart: 35 -> 21, of which waited for: 12 -> 8; matrix products, arithmetic and copies ran while one was open for 21% -> 2% of each run, Pallas kernels for 23% -> 59%
where the time goes in v1:
time: 527 us; the launch traced here: 521 us
  Pallas kernels  400 us (76%)
  waiting for transfers between devices  79.1 us (15%)
  starting transfers between devices  18.9 us (4%)
  local copies, waits for them, and re-layouts  18.6 us (4%)
    pallas_call x1, Pallas kernels, tail(): pl.pallas_call(tail_kernel, name='tail', in_specs=[VMEM] * (8 + len(value...  125 us
    ppermute x12, waiting for transfers between devices, across(): return lax.ppermute(values, 'dp', [(i, i ^ 1 << bit) for i in range(size)])  76.6 us
    pallas_call x3, Pallas kernels, split_grad(): call(functools.partial(split_grad_kernel, cut), 'weight_grad', 4 * D * un...  51.3 us
    pallas_call x2, Pallas kernels, ffn(): call(ffn_kernel, 'ffn', 6 * D * units * LMAX, 3 * D * units * 2 + 2 * D *...  48 us
    pallas_call x2, Pallas kernels, launch(): out = run(jnp.stack([bit for bit, _, _ in side]), *args, *extra)  37.7 us
    pallas_call x1, Pallas kernels, middle_back(): call(middle_back_kernel, 'norm_back', 4 * D * LMAX * units, D * LMAX * 20...  26.5 us
    pallas_call x1, Pallas kernels, attend(): call(attend_kernel, 'attend', heads * 4 * LMAX * LMAX * HDIM * 4, heads *...  16.5 us
    ppermute x12, starting transfers between devices, across(): return lax.ppermute(values, 'dp', [(i, i ^ 1 << bit) for i in range(size)])  16.5 us
  transfers between devices with their start and end apart: 21, of which 8 were waited for; matrix products, arithmetic and copies ran while one was open for 2% of the time, Pallas kernels for 59%

profile of v1, /device:TPU:0, one launch (start us, length us, event | category | flops | bytes accessed | tf_op | source)
XLA Modules:
  0.0 520.5 jit_solution(13799083639800668608)
XLA Ops:
  0.7 3.7 places.1
  4.4 0.5 collective-permute-start
  4.8 6.8 %compact.1 = (bf16[736,1024]{1,0:T(8,128)(2,1)}, bf16[736,1024]{1,0:T(8,128)(2,1)}) custom-call(s32[1]{0:T(128)} %bitcast.part_ref, s32[1,2048]{1,0:T(1,128)} %get-tuple-element.87.slot_ref, bf16[736,2048]{1,0:T(8,128)(2,1)} %bitcast.68), custom_call_target="tpu_custom_call" | custom-call | flops 3472883712 | bytes 6029312 | tf_op jit(solution)/shard_map/compact/pallas_call | solution.py:221
  11.7 1.4 copy-done.10
  13.1 10.2 %compact_join.1 = (bf16[736,1024]{1,0:T(8,128)(2,1)}, bf16[736,1024]{1,0:T(8,128)(2,1)}, bf16[1152,1472]{1,0:T(8,128)(2,1)}, bf16[384,1472]{1,0:T(8,128)(2,1)}) custom-call(s32[1]{0:T(128)} %bitcast.part_ref, s32[1,2048]{1,0:T(1,128)} %get-tuple-element.87.slot_ref, bf16[736,2048]{1,0:T(8,128)(2,1)} %bitcast.69, ...), custom_call_target="tpu_custom_call" | custom-call | flops 3472883712 | bytes 6029312 | tf_op jit(solution)/shard_map/compact_join/pallas_call | solution.py:198
  23.3 0.5 collective-permute-start.4
  23.9 0.4 collective-permute-start.2
  24.4 1.2 copy.37.gain_ref.columns_ref
  25.6 2.5 collective-permute-done.2
  28.3 0.6 broadcast_select_fusion.table_ref
  28.9 5.1 bias_strip.1.strip_ref
  34.0 1.1 copy-done.13
  35.1 8.7 %norm_project.1 = (bf16[1472,1024]{1,0:T(8,128)(2,1)}, bf16[1472,1024]{1,0:T(8,128)(2,1)}, bf16[1152,1024]{1,0:T(8,128)(2,1)}, bf16[16,1024]{1,0:T(8,128)(2,1)}, f32[1,1024]{1,0:T(1,128)}, /*index=5*/f32[1,1024]{1,0:T(1,128)}) custom-call(s32[1]{0:T(128)} %bitcast.part_ref, bf16[736,1024]{1,0:T(8,128)(2,1)} %get-tuple-element.90.own_ref, ...), custom_call_target="tpu_custom_call" | custom-call | flops 3472883712 | bytes 15073280 | tf_op jit(solution)/shard_map/norm_project/pallas_call | solution.py:318
  43.9 1.1 copy-done.12
  45.0 16.5 %attend.1 = (bf16[6,1024,1024]{2,1,0:T(8,128)(2,1)}, bf16[384,1024]{1,0:T(8,128)(2,1)}, f32[384,1024]{1,0:T(8,128)}, bf16[1472,1024]{1,0:T(8,128)(2,1)}, bf16[1472,1024]{1,0:T(8,128)(2,1)}) custom-call(s32[1]{0:T(128)} %bitcast.part_ref, bf16[1152,1024]{1,0:T(8,128)(2,1)} %get-tuple-element.94.q_ref.k_ref.v_ref.refs_0_.refs_1_.refs_2_, ...), custom_call_target="tpu_custom_call" | custom-call | flops 6442450944 | bytes 12582912 | tf_op jit(solution)/shard_map/attend/pallas_call | solution.py:902
  61.5 8.0 %attention_out_norm.1 = (f32[1472,1024]{1,0:T(8,128)}, bf16[1472,1024]{1,0:T(8,128)(2,1)}, f32[1,1024]{1,0:T(1,128)}) custom-call(bf16[384,1472]{1,0:T(8,128)(2,1)} %get-tuple-element.89.weight_ref, bf16[384,1024]{1,0:T(8,128)(2,1)} %get-tuple-element.98.attended_ref, bf16[1472,1024]{1,0:T(8,128)(2,1)} %get-tuple-element.99.state_ref, ...), custom_call_target="tpu_custom_call" | custom-call | flops 1157627904 | bytes 12058624 | tf_op jit(solution)/shard_map/attention_out_norm/pallas_call | solution.py:348
  69.5 0.4 collective-permute-start.5
  69.9 0.6 pad_add_fusion.1.bits_ref
  70.5 24.0 %ffn.2 = (bf16[1792,1024]{1,0:T(8,128)(2,1)}, bf16[1792,1024]{1,0:T(8,128)(2,1)}, bf16[1792,1024]{1,0:T(8,128)(2,1)}) custom-call(bf16[1472,1792]{1,0:T(8,128)(2,1)} %gate_ref.5, bf16[1472,1792]{1,0:T(8,128)(2,1)} %up_ref.5, bf16[1472,1792]{1,0:T(8,128)(2,1)} %bitcast.46, bf16[1472,1024]{1,0:T(8,128)(2,1)} %get-tuple-element.100.x_ref.b_own, ...), custom_call_target="tpu_custom_call" | custom-call | flops 16206790656 | bytes 32866304 | tf_op jit(solution)/shard_map/ffn/pallas_call | solution.py:1058
  94.5 1.6 copy-done.9
  96.1 24.0 %ffn.3 = (bf16[1792,1024]{1,0:T(8,128)(2,1)}, bf16[1792,1024]{1,0:T(8,128)(2,1)}, bf16[1792,1024]{1,0:T(8,128)(2,1)}) custom-call(bf16[1472,1792]{1,0:T(8,128)(2,1)} %gate_ref.5, bf16[1472,1792]{1,0:T(8,128)(2,1)} %up_ref.5, bf16[1472,1792]{1,0:T(8,128)(2,1)} %bitcast.47, bf16[1472,1024]{1,0:T(8,128)(2,1)} %copy-done.9, ...), custom_call_target="tpu_custom_call" | custom-call | flops 16206790656 | bytes 32866304 | tf_op jit(solution)/shard_map/ffn/pallas_call | solution.py:1058
  120.1 17.2 %weight_grad.4 = (bf16[4,2,64,1472]{3,2,1,0:T(8,128)(2,1)}, bf16[4,2,64,1472]{3,2,1,0:T(8,128)(2,1)}, bf16[4,2,48,1472]{3,2,1,0:T(8,128)(2,1)}, bf16[4,2,48,1472]{3,2,1,0:T(8,128)(2,1)}) custom-call(s32[2]{0:T(128)} %pad_add_fusion.1.bits_ref, bf16[1792,1024]{1,0:T(8,128)(2,1)} %get-tuple-element.102.hid_ref.a_own, ...), custom_call_target="tpu_custom_call" | custom-call | flops 10804527104 | bytes 18644992 | tf_op jit(solution)/shard_map/weight_grad/pallas_call | solution.py:1145
  137.3 2.6 collective-permute-start.8
  139.9 1.6 collective-permute-start.9
  141.5 0.6 pad_add_fusion.bits_ref
  142.1 17.0 %weight_grad.3 = (bf16[4,2,64,1472]{3,2,1,0:T(8,128)(2,1)}, bf16[4,2,64,1472]{3,2,1,0:T(8,128)(2,1)}, bf16[4,2,48,1472]{3,2,1,0:T(8,128)(2,1)}, bf16[4,2,48,1472]{3,2,1,0:T(8,128)(2,1)}) custom-call(s32[2]{0:T(128)} %pad_add_fusion.1.bits_ref, bf16[1792,1024]{1,0:T(8,128)(2,1)} %get-tuple-element.116.a_own.gu_ref, ...), custom_call_target="tpu_custom_call" | custom-call | flops 10804527104 | bytes 18644992 | tf_op jit(solution)/shard_map/weight_grad/pallas_call | solution.py:1145
  159.1 9.1 %collective-permute-done.9.refs_7_ = bf16[4,2,48,1472]{3,2,1,0:T(8,128)(2,1)S(1)} collective-permute-done((bf16[4,2,48,1472]{3,2,1,0:T(8,128)(2,1)}, bf16[4,2,48,1472]{3,2,1,0:T(8,128)(2,1)S(1)}, u32[]{:S(2)}, u32[]{:S(2)}) %collective-permute-start.9) | collective-permute-done | bytes 1130528 | tf_op jit(solution)/shard_map/ppermute | solution.py:1187
  168.1 6.9 %collective-permute-done.8.refs_5_ = bf16[4,2,64,1472]{3,2,1,0:T(8,128)(2,1)S(1)} collective-permute-done((bf16[4,2,64,1472]{3,2,1,0:T(8,128)(2,1)}, bf16[4,2,64,1472]{3,2,1,0:T(8,128)(2,1)S(1)}, u32[]{:S(2)}, u32[]{:S(2)}) %collective-permute-start.8) | collective-permute-done | bytes 1507360 | tf_op jit(solution)/shard_map/ppermute | solution.py:1187
  175.1 1.2 copy-done.11
  176.2 18.3 %project.3 = (bf16[1472,1024]{1,0:T(8,128)(2,1)}, bf16[4,64,1472]{2,1,0:T(8,128)(2,1)}, bf16[4,64,1472]{2,1,0:T(8,128)(2,1)}, bf16[4,48,1472]{2,1,0:T(8,128)(2,1)}, bf16[4,48,1472]{2,1,0:T(8,128)(2,1)}) custom-call(s32[2]{0:T(128)} %pad_add_fusion.bits_ref, bf16[1472,1792]{1,0:T(8,128)(2,1)} %gate_ref.5, bf16[1472,1792]{1,0:T(8,128)(2,1)} %up_ref.5, ...), custom_call_target="tpu_custom_call" | custom-call | flops 10804527104 | bytes 31834112 | tf_op jit(solution)/shard_map/project/pallas_call | solution.py:89
  194.6 9.6 %project.2 = bf16[1472,1024]{1,0:T(8,128)(2,1)} custom-call(bf16[1472,1792]{1,0:T(8,128)(2,1)} %bitcast.48, bf16[1792,1024]{1,0:T(8,128)(2,1)} %get-tuple-element.104.refs_1_.a_peer), custom_call_target="tpu_custom_call" | custom-call | flops 5402263552 | bytes 14974976 | tf_op jit(solution)/shard_map/project/pallas_call | solution.py:1107
  204.2 0.5 collective-permute-start.6
  204.7 17.0 %weight_grad.5 = (bf16[4,2,64,1472]{3,2,1,0:T(8,128)(2,1)}, bf16[4,2,64,1472]{3,2,1,0:T(8,128)(2,1)}, bf16[4,2,48,1472]{3,2,1,0:T(8,128)(2,1)}, bf16[4,2,48,1472]{3,2,1,0:T(8,128)(2,1)}) custom-call(s32[2]{0:T(128)} %pad_add_fusion.1.bits_ref, bf16[1792,1024]{1,0:T(8,128)(2,1)} %get-tuple-element.115.gg_ref.a_own, ...), custom_call_target="tpu_custom_call" | custom-call | flops 10804527104 | bytes 18644992 | tf_op jit(solution)/shard_map/weight_grad/pallas_call | solution.py:1145
  221.7 1.8 collective-permute-start.11
  223.5 1.5 collective-permute-start.12
  225.0 0.5 collective-permute-start.14
  225.5 0.3 collective-permute-start.13
  225.8 26.5 %norm_back.1 = (f32[1472,1024]{1,0:T(8,128)}, bf16[1472,1024]{1,0:T(8,128)(2,1)}, bf16[384,1024]{1,0:T(8,128)(2,1)}, f32[1472,128]{1,0:T(8,128)}) custom-call(bf16[1472,1792]{1,0:T(8,128)(2,1)} %gate_ref.5, bf16[1472,1792]{1,0:T(8,128)(2,1)} %up_ref.5, bf16[1792,1024]{1,0:T(8,128)(2,1)} %get-tuple-element.115.gg_ref.a_own, ...), custom_call_target="tpu_custom_call" | custom-call | flops 10804527104 | bytes 40697856 | tf_op jit(solution)/shard_map/norm_back/pallas_call | solution.py:393
  252.3 0.3 collective-permute-done.12.refs_9_
  252.6 1.5 collective-permute-start.16
  254.2 5.1 collective-permute-done.11.refs_7_
  259.3 1.8 collective-permute-start.15
  261.1 19.4 %attend_back.1 = (bf16[384,1024]{1,0:T(8,128)(2,1)}, bf16[384,1024]{1,0:T(8,128)(2,1)}, bf16[384,1024]{1,0:T(8,128)(2,1)}, f32[6,8,1024]{2,1,0:T(8,128)}, f32[6,...) custom-call(s32[2]{0:T(128)} %pad_add_fusion.bits_ref, ...), custom_call_target="tpu_custom_call" | custom-call | flops 12884901888 | bytes 20496384 | tf_op jit(solution)/shard_map/attend_back/pallas_call | solution.py:89
  280.5 24.1 %collective-permute-done.16 = bf16[4,48,1472]{2,1,0:T(8,128)(2,1)S(1)} collective-permute-done((bf16[4,48,1472]{2,1,0:T(8,128)(2,1)S(1)}, bf16[4,48,1472]{2,1,0:T(8,128)(2,1)S(1)}, u32[]{:S(2)}, u32[]{:S(2)}) %collective-permute-start.16) | collective-permute-done | bytes 565280 | tf_op jit(solution)/shard_map/ppermute | solution.py:1187
  304.6 1.7 collective-permute-start.18
  306.4 1.5 collective-permute-start.17
  308.0 11.4 %mixed.1 = bf16[1472,1024]{1,0:T(8,128)(2,1)} custom-call(bf16[1472,1792]{1,0:T(8,128)(2,1)} %bitcast.49, bf16[1792,1024]{1,0:T(8,128)(2,1)} %get-tuple-element.102.hid_ref.a_own, bf16[1472,1024]{1,0:T(8,128)(2,1)} %copy-done.1, f32[1472,1024]{1,0:T(8,128)} %get-tuple-element.105.mid_ref), custom_call_target="tpu_custom_call" | custom-call | flops 5402263552 | bytes 17334272 | tf_op jit(solution)/shard_map/mixed/pallas_call | solution.py:484
  319.4 3.8 constant_dynamic-slice_fusion
  323.2 1.9 collective-permute-done.17
  325.0 4.0 join.1
  329.0 1.6 collective-permute-start.19
  330.6 11.1 %head_grads.1 = (bf16[4,192,1472]{2,1,0:T(8,128)(2,1)}, bf16[4,192,1472]{2,1,0:T(8,128)(2,1)}) custom-call(s32[1]{0:T(128)} %bitcast.part_ref, bf16[384,1024]{1,0:T(8,128)(2,1)} %get-tuple-element.131.q_ref, bf16[384,1024]{1,0:T(8,128)(2,1)} %get-tuple-element.132.v_ref, bf16[384,1024]{1,0:T(8,128)(2,1)} %get-tuple-element.133.k_ref, ...), custom_call_target="tpu_custom_call" | custom-call | flops 4630511616 | bytes 18219008 | tf_op jit(solution)/shard_map/head_grads/pallas_call | solution.py:513
  341.8 125.0 %tail.1 = (bf16[4,2,2,48,1472]{4,3,2,1,0:T(8,128)(2,1)}, f32[112,1472]{1,0:T(8,128)}, f32[8,1472]{1,0:T(8,128)}, bf16[736,1024]{1,0:T(8,128)(2,1)}, bf16[736,1024]{1,0:T(8,128)(2,1)}) custom-call(bf16[4,2,2,48,1472]{4,3,2,1,0:T(8,128)(2,1)} %bitcast.50, bf16[4,2,2,48,1472]{4,3,2,1,0:T(8,128)(2,1)} %bitcast.51, ...), custom_call_target="tpu_custom_call" | custom-call | flops 3472883712 | bytes 62914560 | tf_op jit(solution)/shard_map/tail/pallas_call | solution.py:773
  466.8 0.7 slice_reduce_fusion.1
  467.6 1.5 fusion.1
  469.1 6.4 %spread.3 = bf16[736,2048]{1,0:T(8,128)(2,1)} custom-call(s32[1]{0:T(128)} %bitcast.part_ref, s32[1,2048]{1,0:T(1,128)} %get-tuple-element.87.slot_ref, bf16[736,1024]{1,0:T(8,128)(2,1)} %get-tuple-element.144.own_ref, bf16[736,1024]{1,0:T(8,128)(2,1)} %get-tuple-element.145.peer_ref), custom_call_target="tpu_custom_call" | custom-call | flops 2701131776 | bytes 6029312 | tf_op jit(solution)/shard_map/spread/pallas_call | solution.py:256
  475.5 6.7 %spread.2 = bf16[736,2048]{1,0:T(8,128)(2,1)} custom-call(s32[1]{0:T(128)} %bitcast.part_ref, s32[1,2048]{1,0:T(1,128)} %get-tuple-element.87.slot_ref, bf16[736,1024]{1,0:T(8,128)(2,1)} %get-tuple-element.162.own_ref, bf16[736,1024]{1,0:T(8,128)(2,1)} %collective-permute-done.7.peer_ref), custom_call_target="tpu_custom_call" | custom-call | flops 2701131776 | bytes 6029312 | tf_op jit(solution)/shard_map/spread/pallas_call | solution.py:256
  482.2 3.1 fold.1
  485.3 0.6 dynamic-slice_bitcast_fusion
  485.9 0.7 dynamic-slice_reduce_fusion
  486.6 2.4 fusion
  489.0 29.1 %collective-permute-done.20 = bf16[1,224,1472]{2,1,0:T(8,128)(2,1)S(1)} collective-permute-done((bf16[1,224,1472]{2,1,0:T(8,128)(2,1)}, bf16[1,224,1472]{2,1,0:T(8,128)(2,1)S(1)}, u32[]{:S(2)}, u32[]{:S(2)}) %collective-permute-start.20) | collective-permute-done | bytes 659488 | tf_op jit(solution)/shard_map/ppermute | solution.py:1187
  518.1 1.3 add_bitcast_fusion
  519.4 0.8 copy.44
  (55 shorter events, 0.7 us)
Async XLA Ops:
  4.4 7.3 %collective-permute-start = (bf16[4,192,1472]{2,1,0:T(8,128)(2,1)}, bf16[4,192,1472]{2,1,0:T(8,128)(2,1)S(1)}, u32[]{:S(2)}, u32[]{:S(2)}) collective-permute-start(bf16[4,192,1472]{2,1,0:T(8,128)(2,1)} %get-tuple-element.88.stack_ref), channel_id=1, source_target_pairs={{0,1},{1,0},{2,3},{3,2},{4,5},{5,4},{6,7},{7,6},{8,9},{9,8},{10,11... | collective-permute-start | bytes 6782984 | tf_op jit(solution)/shard_map/ppermute | solution.py:1313
  11.6 22.4 %collective-permute-start.1 = (bf16[736,1024]{1,0:T(8,128)(2,1)}, bf16[736,1024]{1,0:T(8,128)(2,1)S(1)}, u32[]{:S(2)}, u32[]{:S(2)}) collective-permute-start(bf16[736,1024]{1,0:T(8,128)(2,1)} %get-tuple-element.91), channel_id=1, source_target_pairs={{0,1},{1,0},{2,3},{3,2},{4,5},{5,4},{6,7},{7,6},{8,9},{9,8},{10,11... | collective-permute-start | bytes 4521992 | tf_op jit(solution)/shard_map/ppermute | solution.py:1313
  11.7 1.4 copy-start.10
  13.1 10.8 %copy-start.8 = (f32[32,3]{0,1:T(4,128)S(1)}, f32[32,3]{0,1:T(4,128)}, u32[]{:S(2)}) copy-start(f32[32,3]{0,1:T(4,128)} %param.24) | copy-start | bytes 1156
  13.1 11.2 %copy-start.5 = (f32[1472]{0:T(1024)S(1)}, f32[1472]{0:T(1024)}, u32[]{:S(2)}) copy-start(f32[1472]{0:T(1024)} %param.19) | copy-start | bytes 17668
  13.1 11.2 %copy-start.7 = (bf16[1472]{0:T(1024)(128)(2,1)S(1)}, bf16[1472]{0:T(1024)(128)(2,1)}, u32[]{:S(2)}) copy-start(bf16[1472]{0:T(1024)(128)(2,1)} %param.25) | copy-start | bytes 8836
  13.1 11.3 %copy-start.6 = (f32[1472]{0:T(1024)S(1)}, f32[1472]{0:T(1024)}, u32[]{:S(2)}) copy-start(f32[1472]{0:T(1024)} %param.26) | copy-start | bytes 17668
  23.3 20.6 %collective-permute-start.4 = (bf16[736,1024]{1,0:T(8,128)(2,1)}, bf16[736,1024]{1,0:T(8,128)(2,1)S(1)}, u32[]{:S(2)}, u32[]{:S(2)}) collective-permute-start(bf16[736,1024]{1,0:T(8,128)(2,1)} %get-tuple-element.96.own_ref), channel_id=1, source_target_pairs={{0,1},{1,0},{2,3},{3,2},{4,5},{5,4},{6,7},{7,6},{8,9},{9,8},{10,11... | collective-permute-start | bytes 4521992 | tf_op jit(solution)/shard_map/ppermute | solution.py:1313
  23.8 20.1 %collective-permute-start.3 = (bf16[736,1024]{1,0:T(8,128)(2,1)}, bf16[736,1024]{1,0:T(8,128)(2,1)}, u32[]{:S(2)}, u32[]{:S(2)}) collective-permute-start(bf16[736,1024]{1,0:T(8,128)(2,1)} %get-tuple-element.97.peer_ref), channel_id=1, source_target_pairs={{0,1},{1,0},{2,3},{3,2},{4,5},{5,4},{6,7},{7,6},{8,9},{9,8},{10,11... | collective-permute-start | bytes 4521992 | tf_op jit(solution)/shard_map/ppermute | solution.py:1313
  23.9 4.2 collective-permute-start.2
  34.0 1.1 copy-start.13
  43.9 1.2 copy-start.12
  69.5 25.0 %collective-permute-start.5 = (bf16[1472,1024]{1,0:T(8,128)(2,1)}, bf16[1472,1024]{1,0:T(8,128)(2,1)S(1)}, u32[]{:S(2)}, u32[]{:S(2)}) collective-permute-start(bf16[1472,1024]{1,0:T(8,128)(2,1)} %get-tuple-element.100.x_ref.b_own), channel_id=1, source_target_pairs={{0,1},{1,0},{2,3},{3,2},{4,5},{5,4},{6,7},{7,6},{8,9},{9,8},{10,11... | collective-permute-start | bytes 9043976 | tf_op jit(solution)/shard_map/ppermute | solution.py:1313
  94.5 1.6 copy-start.9
  137.3 37.8 %collective-permute-start.8 = (bf16[4,2,64,1472]{3,2,1,0:T(8,128)(2,1)}, bf16[4,2,64,1472]{3,2,1,0:T(8,128)(2,1)S(1)}, u32[]{:S(2)}, u32[]{:S(2)}) collective-permute-start(bf16[4,2,64,1472]{3,2,1,0:T(8,128)(2,1)} %get-tuple-element.120), channel_id=1, source_target_pairs={{0,2},{2,0},{4,6},{6,4},{8,10},{10,8},{12,14},{14,12},{16,18},{18,... | collective-permute-start | bytes 4521992 | tf_op jit(solution)/shard_map/ppermute | solution.py:1187
  139.9 28.2 %collective-permute-start.9 = (bf16[4,2,48,1472]{3,2,1,0:T(8,128)(2,1)}, bf16[4,2,48,1472]{3,2,1,0:T(8,128)(2,1)S(1)}, u32[]{:S(2)}, u32[]{:S(2)}) collective-permute-start(bf16[4,2,48,1472]{3,2,1,0:T(8,128)(2,1)} %get-tuple-element.122), channel_id=1, source_target_pairs={{0,4},{2,6},{4,0},{6,2},{8,12},{10,14},{12,8},{14,10},{16,20},{18,... | collective-permute-start | bytes 3391496 | tf_op jit(solution)/shard_map/ppermute | solution.py:1187
  168.1 6.9 %copy-start.14 = (bf16[4,2,48,1472]{3,2,1,0:T(8,128)(2,1)}, bf16[4,2,48,1472]{3,2,1,0:T(8,128)(2,1)S(1)}, u32[]{:S(2)}) copy-start(bf16[4,2,48,1472]{3,2,1,0:T(8,128)(2,1)S(1)} %collective-permute-done.9.refs_7_) | copy-start | bytes 3391492
  175.1 1.2 copy-start.11
  194.6 30.9 %collective-permute-start.10 = (bf16[1472,1024]{1,0:T(8,128)(2,1)}, bf16[1472,1024]{1,0:T(8,128)(2,1)}, u32[]{:S(2)}, u32[]{:S(2)}) collective-permute-start(bf16[1472,1024]{1,0:T(8,128)(2,1)} %get-tuple-element.123), channel_id=1, source_target_pairs={{0,1},{1,0},{2,3},{3,2},{4,5},{5,4},{6,7},{7,6},{8,9},{9,8},{10,11... | collective-permute-start | bytes 9043976 | tf_op jit(solution)/shard_map/ppermute | solution.py:1313
  204.2 102.2 %collective-permute-start.6 = (bf16[1472,1024]{1,0:T(8,128)(2,1)}, bf16[1472,1024]{1,0:T(8,128)(2,1)S(1)}, u32[]{:S(2)}, u32[]{:S(2)}) collective-permute-start(bf16[1472,1024]{1,0:T(8,128)(2,1)} %project.2), channel_id=1, source_target_pairs={{0,1},{1,0},{2,3},{3,2},{4,5},{5,4},{6,7},{7,6},{8,9},{9,8},{10,11... | collective-permute-start | bytes 9043976 | tf_op jit(solution)/shard_map/ppermute | solution.py:1313
  221.7 37.6 %collective-permute-start.11 = (bf16[4,2,64,1472]{3,2,1,0:T(8,128)(2,1)}, bf16[4,2,64,1472]{3,2,1,0:T(8,128)(2,1)}, u32[]{:S(2)}, u32[]{:S(2)}) collective-permute-start(bf16[4,2,64,1472]{3,2,1,0:T(8,128)(2,1)} %get-tuple-element.128), channel_id=1, source_target_pairs={{0,2},{2,0},{4,6},{6,4},{8,10},{10,8},{12,14},{14,12},{16,18},{18,... | collective-permute-start | bytes 4521992 | tf_op jit(solution)/shard_map/ppermute | solution.py:1187
  223.5 29.2 %collective-permute-start.12 = (bf16[4,2,48,1472]{3,2,1,0:T(8,128)(2,1)}, bf16[4,2,48,1472]{3,2,1,0:T(8,128)(2,1)}, u32[]{:S(2)}, u32[]{:S(2)}) collective-permute-start(bf16[4,2,48,1472]{3,2,1,0:T(8,128)(2,1)} %get-tuple-element.130), channel_id=1, source_target_pairs={{0,4},{2,6},{4,0},{6,2},{8,12},{10,14},{12,8},{14,10},{16,20},{18,... | collective-permute-start | bytes 3391496 | tf_op jit(solution)/shard_map/ppermute | solution.py:1187
  225.0 116.8 %collective-permute-start.14 = (bf16[4,2,48,1472]{3,2,1,0:T(8,128)(2,1)}, bf16[4,2,48,1472]{3,2,1,0:T(8,128)(2,1)}, u32[]{:S(2)}, u32[]{:S(2)}) collective-permute-start(bf16[4,2,48,1472]{3,2,1,0:T(8,128)(2,1)} %get-tuple-element.114), channel_id=1, source_target_pairs={{0,4},{2,6},{4,0},{6,2},{8,12},{10,14},{12,8},{14,10},{16,20},{18,... | collective-permute-start | bytes 3391496 | tf_op jit(solution)/shard_map/ppermute | solution.py:1187
  225.5 116.3 %collective-permute-start.13 = (bf16[4,2,64,1472]{3,2,1,0:T(8,128)(2,1)}, bf16[4,2,64,1472]{3,2,1,0:T(8,128)(2,1)}, u32[]{:S(2)}, u32[]{:S(2)}) collective-permute-start(bf16[4,2,64,1472]{3,2,1,0:T(8,128)(2,1)} %get-tuple-element.112), channel_id=1, source_target_pairs={{0,2},{2,0},{4,6},{6,4},{8,10},{10,8},{12,14},{14,12},{16,18},{18,... | collective-permute-start | bytes 4521992 | tf_op jit(solution)/shard_map/ppermute | solution.py:1187
  225.8 26.9 %copy-start.16 = (bf16[4,48,1472]{2,1,0:T(8,128)(2,1)S(1)}, bf16[4,48,1472]{2,1,0:T(8,128)(2,1)}, u32[]{:S(2)}) copy-start(bf16[4,48,1472]{2,1,0:T(8,128)(2,1)} %get-tuple-element.151) | copy-start | bytes 1695748
  225.8 33.5 %copy-start.15 = (bf16[4,64,1472]{2,1,0:T(8,128)(2,1)S(1)}, bf16[4,64,1472]{2,1,0:T(8,128)(2,1)}, u32[]{:S(2)}) copy-start(bf16[4,64,1472]{2,1,0:T(8,128)(2,1)} %get-tuple-element.150) | copy-start | bytes 2260996
  252.6 52.0 %collective-permute-start.16 = (bf16[4,48,1472]{2,1,0:T(8,128)(2,1)S(1)}, bf16[4,48,1472]{2,1,0:T(8,128)(2,1)S(1)}, u32[]{:S(2)}, u32[]{:S(2)}) collective-permute-start(bf16[4,48,1472]{2,1,0:T(8,128)(2,1)S(1)} %copy-done.16), channel_id=1, source_target_pairs={{0,2},{2,0},{4,6},{6,4},{8,10},{10,8},{12,14},{14,12},{16,18},{18,... | collective-permute-start | bytes 1695752 | tf_op jit(solution)/shard_map/ppermute | solution.py:1187
  259.3 63.9 %collective-permute-start.15 = (bf16[4,64,1472]{2,1,0:T(8,128)(2,1)S(1)}, bf16[4,64,1472]{2,1,0:T(8,128)(2,1)}, u32[]{:S(2)}, u32[]{:S(2)}) collective-permute-start(bf16[4,64,1472]{2,1,0:T(8,128)(2,1)S(1)} %copy-done.15), channel_id=1, source_target_pairs={{0,4},{2,6},{4,0},{6,2},{8,12},{10,14},{12,8},{14,10},{16,20},{18,... | collective-permute-start | bytes 2261000 | tf_op jit(solution)/shard_map/ppermute | solution.py:1187
  304.6 14.8 %copy-start.4 = (bf16[4,48,1472]{2,1,0:T(8,128)(2,1)}, bf16[4,48,1472]{2,1,0:T(8,128)(2,1)S(1)}, u32[]{:S(2)}) copy-start(bf16[4,48,1472]{2,1,0:T(8,128)(2,1)S(1)} %collective-permute-done.16) | copy-start | bytes 1695748
  304.6 18.5 %collective-permute-start.18 = (bf16[4,48,1472]{2,1,0:T(8,128)(2,1)}, bf16[4,48,1472]{2,1,0:T(8,128)(2,1)}, u32[]{:S(2)}, u32[]{:S(2)}) collective-permute-start(bf16[4,48,1472]{2,1,0:T(8,128)(2,1)} %get-tuple-element.155), channel_id=1, source_target_pairs={{0,2},{2,0},{4,6},{6,4},{8,10},{10,8},{12,14},{14,12},{16,18},{18,... | collective-permute-start | bytes 1695752 | tf_op jit(solution)/shard_map/ppermute | solution.py:1187
  306.4 1.6 copy-start.1
  306.4 18.7 %collective-permute-start.17 = (bf16[4,64,1472]{2,1,0:T(8,128)(2,1)}, bf16[4,64,1472]{2,1,0:T(8,128)(2,1)}, u32[]{:S(2)}, u32[]{:S(2)}) collective-permute-start(bf16[4,64,1472]{2,1,0:T(8,128)(2,1)} %get-tuple-element.154), channel_id=1, source_target_pairs={{0,4},{2,6},{4,0},{6,2},{8,12},{10,14},{12,8},{14,10},{16,20},{18,... | collective-permute-start | bytes 2261000 | tf_op jit(solution)/shard_map/ppermute | solution.py:1187
  323.1 152.3 %collective-permute-start.7 = (bf16[736,1024]{1,0:T(8,128)(2,1)}, bf16[736,1024]{1,0:T(8,128)(2,1)}, u32[]{:S(2)}, u32[]{:S(2)}) collective-permute-start(bf16[736,1024]{1,0:T(8,128)(2,1)} %get-tuple-element.161), channel_id=1, source_target_pairs={{0,1},{1,0},{2,3},{3,2},{4,5},{5,4},{6,7},{7,6},{8,9},{9,8},{10,11... | collective-permute-start | bytes 4521992 | tf_op jit(solution)/shard_map/ppermute | solution.py:1313
  329.0 153.1 %collective-permute-start.19 = (bf16[2,2,112,1472]{3,2,1,0:T(8,128)(2,1)}, bf16[2,2,112,1472]{3,2,1,0:T(8,128)(2,1)}, u32[]{:S(2)}, u32[]{:S(2)}) collective-permute-start(bf16[2,2,112,1472]{3,2,1,0:T(8,128)(2,1)} %get-tuple-element.157), channel_id=1, source_target_pairs={{0,8},{2,10},{4,12},{6,14},{8,0},{10,2},{12,4},{14,6},{16,24},{18,... | collective-permute-start | bytes 3956744 | tf_op jit(solution)/shard_map/ppermute | solution.py:1187
  482.2 4.4 copy-start
  485.3 32.8 %collective-permute-start.20 = (bf16[1,224,1472]{2,1,0:T(8,128)(2,1)}, bf16[1,224,1472]{2,1,0:T(8,128)(2,1)S(1)}, u32[]{:S(2)}, u32[]{:S(2)}) collective-permute-start(bf16[1,224,1472]{2,1,0:T(8,128)(2,1)} %get-tuple-element.159), channel_id=1, source_target_pairs={{0,16},{2,18},{4,20},{6,22},{8,24},{10,26},{12,28},{14,30},{16,0},... | collective-permute-start | bytes 1978376 | tf_op jit(solution)/shard_map/ppermute | solution.py:1187
  486.6 31.5 %copy-start.3 = (bf16[1,224,1472]{2,1,0:T(8,128)(2,1)S(1)}, bf16[1,224,1472]{2,1,0:T(8,128)(2,1)}, u32[]{:S(2)}) copy-start(bf16[1,224,1472]{2,1,0:T(8,128)(2,1)} %get-tuple-element.158) | copy-start | bytes 1978372
  489.0 30.4 %copy-start.2 = (f32[112,1472]{1,0:T(8,128)S(1)}, f32[112,1472]{1,0:T(8,128)}, u32[]{:S(2)}) copy-start(f32[112,1472]{1,0:T(8,128)} %get-tuple-element.160) | copy-start | bytes 1978372

commit v2 on v1

--- a/solution.py
+++ b/solution.py
@@ -689,18 +689,42 @@
         )
         parts.append((gain_part, delete_part))
 
+    ones = jnp.ones((8, 128), F32)
+
+    def line_of(values):
+        return lax.dot_general(
+            ones, values, NT, preferred_element_type=F32, precision=lax.Precision.HIGHEST
+        )[:1]
+
     advance(0, 0)
+    compute(0)
+    advance(0, 1)
+    advance(1, 0)
+    compute(1)
+    advance(0, 2)
+    advance(1, 1)
+    advance(2, 0)
+    compute(2)
+    advance(0, 3)
+    advance(1, 2)
+    advance(2, 1)
     seconds = [
         sender.start(give_x, second_x, to_y),
         sender.start(give_y, second_y, to_x),
     ]
-    advance(1, 0)
-    advance(2, 0)
-    compute(0)
-    advance(0, 1)
-    compute(1)
-    advance(1, 1)
-    advance(0, 2)
+    compute(3)
+    advance(0, 4)
+    advance(1, 3)
+    advance(2, 2)
+    vector[...] = jnp.zeros_like(vector)
+    vector[0:1] = line_of(ffn_sum_ref[...])
+    vector[1:2] = line_of(sum(p[0] for p in parts))
+    vector[2:3] = line_of(sum(p[1] for p in parts))
+    vector[3:4, : near_ref.shape[0]] = line_of(near_ref[...])
+    vectors = [sender.start(vector, vector_core, at["to_core"])]
+    advance(0, 5)
+    advance(1, 4)
+    advance(2, 3)
     arrived(seconds)
     cut = keep_x.shape[2]
     whole[:, :cut] = plus(keep_x[:, y], came_x[:, y], second_x[...]).astype(BF16)
@@ -709,39 +733,14 @@
         sender.start(whole.at[p], from_whole.at[k], device)
         for k, (p, device) in enumerate(zip(at["planes"], at["to_plane"]))
     ]
-    compute(2)
-    advance(2, 1)
-    advance(1, 2)
-    advance(0, 3)
-    compute(3)
-    advance(2, 2)
-    advance(1, 3)
-    advance(0, 4)
-
-    ones = jnp.ones((8, 128), F32)
-
-    def line_of(values):
-        return lax.dot_general(
-            ones, values, NT, preferred_element_type=F32, precision=lax.Precision.HIGHEST
-        )[:1]
-
-    vector[...] = jnp.zeros_like(vector)
-    vector[0:1] = line_of(ffn_sum_ref[...])
-    vector[1:2] = line_of(sum(p[0] for p in parts))
-    vector[2:3] = line_of(sum(p[1] for p in parts))
-    vector[3:4, : near_ref.shape[0]] = line_of(near_ref[...])
-    vectors = [sender.start(vector, vector_core, at["to_core"])]
-    advance(2, 3)
-    advance(1, 4)
-    advance(0, 5)
     arrived(vectors)
     vector_core[...] = vector_core[...] + vector[...]
     vectors = [
         sender.start(vector_core, vector_near.at[k], device)
         for k, device in enumerate((to_x, to_y, at["to_corner"]))
     ]
+    advance(1, 5)
     advance(2, 4)
-    advance(1, 5)
     arrived(vectors)
     vector_ref[...] = vector_core[...] + vector_near[0] + vector_near[1] + vector_near[2]
     vectors = [
@@ -800,6 +799,357 @@
             vmem_limit_bytes=63 << 20, collective_id=1, has_side_effects=True
         ),
     )(keep.reshape(shape), give.reshape(shape), keep_x, came_x, keep_y, came_y, ffn_sum, near, *values)
+
+
+PLANES = 2
+
+
+def feed_kernel(half, cut, *refs):
+    (
+        gate_hbm, up_hbm, down_hbm, normed_hbm, cot_own_hbm, cot_peer_hbm, *rest
+    ) = refs
+    if half:
+        rest = rest[4:]
+    (
+        grad_own_hbm, grad_came_hbm, mixed_own_hbm, mixed_came_hbm,
+        keep_x_hbm, give_x_hbm, keep_y_hbm, give_y_hbm, share_ref,
+        weight, normed, cot, hidden, staged, blocks, up_blocks,
+        came_x, came_y, last_x, last_y, from_planes,
+        load_sems, store_sems, up_sems, send_sems, recv_sems, plane_send, plane_recv,
+    ) = rest
+    at = neighbours()
+    x, y, z = at["x"], at["y"], at["z"]
+    to_core, to_x, to_y = at["to_core"], at["to_x"], at["to_y"]
+    units = weight.shape[2]
+    rows = units // PLANES
+    share = rows // 4
+    sender = Sender(send_sems, recv_sems)
+    order = (0, 1) if half == 0 else (1, 0)
+
+    def load(place, source, target):
+        copy = pltpu.make_async_copy(source, target, load_sems.at[place])
+        copy.start()
+        return copy
+
+    columns = pl.ds(half * units, units)
+    loads = [
+        load(0, gate_hbm.at[:, columns], weight.at[0]),
+        load(1, normed_hbm, normed.at[0]),
+        load(2, up_hbm.at[:, columns], weight.at[1]),
+        load(3, down_hbm.at[:, columns], weight.at[2]),
+        load(4, cot_own_hbm, cot.at[0]),
+        load(5, cot_peer_hbm, cot.at[1]),
+    ]
+    meet([to_core, to_x, to_y, *at["to_plane"]])
+    exchange = sender.start(normed_hbm, normed.at[1], to_core)
+
+    def activate(side, low, size):
+        def step(block, carry):
+            cols = pl.ds(pl.multiple_of(block * 512, 512), 512)
+            span = slice(low, low + size)
+            value = normed[side, :, cols]
+            gate = dot(weight[0, :, span], value, TN)
+            up = dot(weight[1, :, span], value, TN)
+            grad = dot(weight[2, :, span], cot[side, :, cols], TN)
+            square = gate * gate
+            bend = jnp.tanh(GELU_C * gate * (1.0 + 0.044715 * square))
+            whole = 0.5 * (1.0 + bend)
+            gelu = gate * whole
+            slope = whole + 0.5 * gate * (1.0 - bend * bend) * (
+                GELU_C * (1.0 + 3 * 0.044715 * square)
+            )
+            hidden[0, side, span, cols] = (gelu * up).astype(BF16)
+            hidden[1, side, span, cols] = (grad * up * slope).astype(BF16)
+            hidden[2, side, span, cols] = (grad * gelu).astype(BF16)
+            return carry
+
+        lax.fori_loop(0, LMAX // 512, step, 0)
+
+    def weight_block(matrix, plane, target):
+        other = cot if matrix == 0 else normed
+        span = slice(plane * rows, (plane + 1) * rows)
+        for low, high in ((0, 768), (768, D)):
+            total = dot(hidden[matrix, 0, span], other[0, low:high], NT)
+            total = total + dot(hidden[matrix, 1, span], other[1, low:high], NT)
+            target[:, :, :, low:high] = total.astype(BF16).reshape(2, 2, share, high - low)
+
+    def first(b):
+        block = blocks.at[b]
+        return [
+            sender.start(block.at[:, 1 - x, :cut], came_x.at[b], to_x),
+            sender.start(block.at[1 - y, :, cut:], came_y.at[b], to_y),
+        ]
+
+    def second(b, copies):
+        arrived(copies)
+        block = blocks.at[b]
+        block[:, x, :cut] = plus(block[:, x, :cut], came_x[b]).astype(BF16)
+        block[y, :, cut:] = plus(block[y, :, cut:], came_y[b]).astype(BF16)
+        return [
+            sender.start(block.at[1 - y, x, :cut], last_x.at[b], to_y),
+            sender.start(block.at[y, 1 - x, cut:], last_y.at[b], to_x),
+        ]
+
+    def plane_of(b):
+        return half * PLANES + order[b // 2]
+
+    def inward(b, source_plane):
+        step = -1 if source_plane > plane_of(b) else 1
+        me = lax.axis_index("dp")
+        side = 0 if step < 0 else 1
+        return pltpu.make_async_remote_copy(
+            src_ref=blocks.at[b, y, x],
+            dst_ref=from_planes.at[b, side],
+            send_sem=plane_send.at[b],
+            recv_sem=plane_recv.at[b, side],
+            device_id=((source_plane + step) * 4 + me % 4, at["part"]),
+            device_id_type=MESH,
+        )
+
+    def third(b, copies):
+        arrived(copies)
+        block = blocks.at[b]
+        block[y, x, :cut] = plus(block[y, x, :cut], last_x[b]).astype(BF16)
+        block[y, x, cut:] = plus(block[y, x, cut:], last_y[b]).astype(BF16)
+        for end in (0, 3):
+            if end != plane_of(b):
+
+                @pl.when(z == end)
+                def _(end=end):
+                    inward(b, end).start()
+
+    def hop(b, distance):
+        for plane, side in ((3 - distance, 0), (distance, 1)):
+            outside = plane > plane_of(b) if side == 0 else plane < plane_of(b)
+            if outside:
+
+                @pl.when(z == plane)
+                def _(plane=plane, side=side):
+                    inward(b, plane + 1 if side == 0 else plane - 1).wait_recv()
+                    blocks[b, y, x] = plus(blocks[b, y, x], from_planes[b, side]).astype(BF16)
+                    inward(b, plane).start()
+
+    def final(b):
+        plane = plane_of(b)
+
+        @pl.when(z == plane)
+        def _():
+            got = []
+            for side, exists in ((0, plane < 3), (1, plane > 0)):
+                if exists:
+                    inward(b, plane + 1 if side == 0 else plane - 1).wait_recv()
+                    got.append(from_planes[b, side])
+            share_ref[b % 2] = plus(blocks[b, y, x], *got)
+
+    def finish_send(b):
+        for plane in range(4):
+            if plane != plane_of(b):
+
+                @pl.when(z == plane)
+                def _(plane=plane):
+                    inward(b, plane).wait_send()
+
+    up_copies = []
+
+    def up_block(plane):
+        weight_block(2, plane, up_blocks.at[plane])
+        block = up_blocks.at[plane]
+        to = half * PLANES + plane
+        for i, (source, target) in enumerate(
+            (
+                (block.at[:, x, :cut], keep_x_hbm),
+                (block.at[:, 1 - x, :cut], give_x_hbm),
+                (block.at[y, :, cut:], keep_y_hbm),
+                (block.at[1 - y, :, cut:], give_y_hbm),
+            )
+        ):
+            copy = pltpu.make_async_copy(source, target.at[to], up_sems.at[plane, i])
+            copy.start()
+            up_copies.append(copy)
+
+    def project_into(slot, side, pairs):
+        width = D // 4
+
+        def step(block, carry):
+            span = pl.ds(pl.multiple_of(block * width, 16), width)
+            total = dot(weight[pairs[0][0], span], hidden[pairs[0][1], side], NN)
+            for which, matrix in pairs[1:]:
+                total = total + dot(weight[which, span], hidden[matrix, side], NN)
+            staged[slot, span] = total.astype(BF16)
+            return carry
+
+        lax.fori_loop(0, 4, step, 0)
+
+    ahead_size = 512
+    tiles = ((0, ahead_size), (ahead_size, units - ahead_size))
+    if half:
+        tiles = ((units - ahead_size, ahead_size), (0, units - ahead_size))
+    for copy in loads[:5]:
+        copy.wait()
+    activate(0, *tiles[0])
+    loads[5].wait()
+    exchange.wait_recv()
+    activate(1, *tiles[0])
+    flying = {}
+    weight_block(0, order[0], blocks.at[0])
+    flying[0] = first(0)
+    weight_block(1, order[0], blocks.at[1])
+    flying[1] = first(1)
+    activate(0, *tiles[1])
+    flying[0] = second(0, flying[0])
+    activate(1, *tiles[1])
+    weight_block(0, order[1], blocks.at[2])
+    flying[1] = second(1, flying[1])
+    flying[2] = first(2)
+    third(0, flying[0])
+    weight_block(1, order[1], blocks.at[3])
+    flying[3] = first(3)
+    third(1, flying[1])
+    up_block(0)
+    hop(0, 1)
+    flying[2] = second(2, flying[2])
+    up_block(1)
+    hop(1, 1)
+    hop(0, 2)
+    back = ((0, 1), (1, 2))
+    ahead = ((2, 0),)
+    project_into(0, 1, back)
+    sent = [sender.start(staged.at[0], grad_came_hbm, to_core)]
+    flying[3] = second(3, flying[3])
+    hop(1, 2)
+    third(2, flying[2])
+    project_into(1, 1, ahead)
+    sent.append(sender.start(staged.at[1], mixed_came_hbm, to_core))
+    hop(2, 1)
+    final(0)
+    sent[0].wait_send()
+    project_into(0, 0, back)
+    store_one = pltpu.make_async_copy(staged.at[0], grad_own_hbm, store_sems.at[0])
+    store_one.start()
+    third(3, flying[3])
+    hop(2, 2)
+    final(1)
+    sent[1].wait_send()
+    project_into(1, 0, ahead)
+    store_two = pltpu.make_async_copy(staged.at[1], mixed_own_hbm, store_sems.at[1])
+    store_two.start()
+    hop(3, 1)
+    final(2)
+    hop(3, 2)
+    final(3)
+    for b in range(4):
+        finish_send(b)
+    for copy in sent:
+        copy.wait_recv()
+    for copy in sender.made:
+        if all(copy is not other for other in sent):
+            copy.wait_send()
+    for copy in up_copies + [store_one, store_two]:
+        copy.wait()
+
+
+def feed(half, cut, w_gate, w_up, w_down, normed, cot_own, cot_peer, pieces):
+    units = w_gate.shape[1] // 2
+    share = units // PLANES // 4
+    rest = share - cut
+    hbm = line(D, BF16)
+
+    def hold(*dims, dtype=BF16):
+        return pltpu.VMEM(dims, dtype)
+
+    def piece(rows):
+        return jax.ShapeDtypeStruct((4, 2, rows, D), BF16)
+
+    inputs = 6 + len(pieces)
+    copies = 24
+    return pl.pallas_call(
+        functools.partial(feed_kernel, half, cut),
+        name="feed_forward",
+        in_specs=[ANY] * inputs,
+        out_specs=[ANY] * 8 + [VMEM],
+        out_shape=[
+            hbm, hbm, hbm, hbm, piece(cut), piece(cut), piece(rest), piece(rest),
+            jax.ShapeDtypeStruct((2, share, D), F32),
+        ],
+        input_output_aliases={6 + i: 4 + i for i in range(len(pieces))},
+        scratch_shapes=[
+            hold(3, D, units), hold(2, D, LMAX), hold(2, D, LMAX), hold(3, 2, units, LMAX),
+            hold(2, D, LMAX), hold(4, 2, 2, share, D), hold(2, 2, 2, share, D),
+            hold(4, 2, cut, D), hold(4, 2, rest, D), hold(4, cut, D), hold(4, rest, D),
+            hold(4, 2, share, D),
+            pltpu.SemaphoreType.DMA((6,)),
+            pltpu.SemaphoreType.DMA((2,)),
+            pltpu.SemaphoreType.DMA((2, 4)),
+            pltpu.SemaphoreType.DMA((copies,)),
+            pltpu.SemaphoreType.DMA((copies,)),
+            pltpu.SemaphoreType.DMA((4,)),
+            pltpu.SemaphoreType.DMA((4, 2)),
+        ],
+        cost_estimate=pl.CostEstimate(
+            flops=18 * 2 * D * LMAX * units, bytes_accessed=60 << 20, transcendentals=0
+        ),
+        compiler_params=pltpu.CompilerParams(
+            vmem_limit_bytes=63 << 20, collective_id=2 + half, has_side_effects=True
+        ),
+    )(w_gate, w_up, w_down, normed, cot_own, cot_peer, *pieces)
+
+
+def after_feed_kernel(
+    own_one, own_two, came_one, came_two, mid_ref, cot_ref, columns_ref, scale_ref, weight_ref,
+    grad_mid_ref, grad_attn_ref, attended_ref, sums_ref,
+):
+    grad = plus(own_one[...], own_two[...], came_one[...], came_two[...])
+    mid, scale = mid_ref[...], scale_ref[...]
+    weighted = grad * columns_ref[:, 1:2]
+    inner = jnp.sum(weighted * mid, axis=0, keepdims=True)
+    grad_mid = (
+        cot_ref[...].astype(F32) + scale * weighted - mid * (scale * scale * scale * inner / D)
+    )
+    grad_mid_ref[...] = grad_mid
+    grad_attn = grad_mid.astype(BF16)
+    grad_attn_ref[...] = grad_attn
+    attended_ref[...] = dot(weight_ref[...], grad_attn, NN).astype(BF16)
+
+    @pl.when(pl.program_id(0) == 0)
+    def _():
+        sums_ref[...] = jnp.zeros_like(sums_ref)
+
+    sums_ref[...] += folded(grad * (mid * scale))
+
+
+def after_feed(parts, mid, cot, columns, scale, w_out):
+    inner = w_out.shape[0]
+    return call(
+        after_feed_kernel,
+        "norm_back",
+        2 * D * LMAX * inner,
+        D * LMAX * 26,
+        44,
+        grid=(LMAX // QBLOCK,),
+        in_specs=[ROWS] * 6 + [COLUMN, LINE, whole_spec(w_out)],
+        out_specs=[ROWS, ROWS, pl.BlockSpec((inner, QBLOCK), lambda i: (0, i)), SUMS],
+        out_shape=[
+            line(D), line(D, BF16), line(inner, BF16), jax.ShapeDtypeStruct((D, 128), F32),
+        ],
+    )(*parts, mid, cot, columns, scale, w_out)
+
+
+def add_mixed_kernel(one, two, three, four, mid_ref, out_ref):
+    out_ref[...] = plus(mid_ref[...], one[...], two[...], three[...], four[...]).astype(BF16)
+
+
+def add_mixed(parts, mid):
+    return call(
+        add_mixed_kernel,
+        "mixed_sum",
+        D * LMAX * 5,
+        D * LMAX * 14,
+        44,
+        grid=(LMAX // QBLOCK,),
+        in_specs=[ROWS] * 5,
+        out_specs=ROWS,
+        out_shape=line(D, BF16),
+    )(*parts, mid)
 
 
 STRIP = LMAX + LMAX - TILE
@@ -1118,44 +1468,6 @@
     )(*weights, *values)
 
 
-def split_grad_kernel(cut, bits_ref, a_own, a_peer, b_own, b_peer, *refs):
-    keep_x, give_x, keep_y, give_y, hold = refs
-    total = dot(a_own[...], b_own[...], NT) + dot(a_peer[...], b_peer[...], NT)
-    hold[...] = total.reshape(hold.shape).astype(BF16)
-    x, y = bits_ref[0], bits_ref[1]
-    for other in range(2):
-        keep_x[0, other] = hold[other, x, :cut]
-        give_x[0, other] = hold[other, 1 - x, :cut]
-        keep_y[0, other] = hold[y, other, cut:]
-        give_y[0, other] = hold[1 - y, other, cut:]
-
-
-def split_grad(cut, bits, a_own, a_peer, b_own, b_peer):
-    units = a_own.shape[0]
-    width = units // 4
-    share = width // 4
-    left = pl.BlockSpec((width, LMAX), lambda i: (i, 0))
-
-    def out(rows):
-        return pl.BlockSpec((1, 2, rows, D), lambda i: (i, 0, 0, 0))
-
-    def shape(rows):
-        return jax.ShapeDtypeStruct((4, 2, rows, D), BF16)
-
-    return call(
-        functools.partial(split_grad_kernel, cut),
-        "weight_grad",
-        4 * D * units * LMAX,
-        4 * D * LMAX + 4 * units * LMAX + 2 * units * D,
-        28,
-        grid=(4,),
-        in_specs=[SMEM, left, left, whole_spec(b_own), whole_spec(b_peer)],
-        out_specs=[out(cut), out(cut), out(share - cut), out(share - cut)],
-        out_shape=[shape(cut), shape(cut), shape(share - cut), shape(share - cut)],
-        scratch_shapes=[pltpu.VMEM((2, 2, share, D), BF16)],
-    )(bits, a_own, a_peer, b_own, b_peer)
-
-
 def fold_kernel(bit_ref, keep_ref, came_ref, keep_out, give_out):
     mine = bit_ref[0]
     for out, which in ((keep_out, mine), (give_out, 1 - mine)):
@@ -1189,56 +1501,6 @@
 
 def bit_of(bit):
     return (lax.axis_index("dp") >> bit) & 1
-
-
-def join_kernel(count, bit_ref, *refs):
-    keep_out, give_out = refs[4 * count :]
-    mine = bit_ref[0]
-    for i in range(count):
-        keep_x, keep_y, came_x, came_y = refs[4 * i : 4 * i + 4]
-        cut = keep_x.shape[2]
-        for out, which in ((keep_out, mine), (give_out, 1 - mine)):
-            total = keep_x[0, which].astype(F32) + came_x[0, which].astype(F32)
-            out[0, i, :cut] = total.astype(BF16)
-            total = keep_y[0, which].astype(F32) + came_y[0, which].astype(F32)
-            out[0, i, cut:] = total.astype(BF16)
-
-
-def join(bit, groups):
-    count = len(groups)
-    specs, args = [], []
-    for group in groups:
-        for array in group:
-            rows = array.shape[1]
-            specs.append(pl.BlockSpec((1, 2, rows, D), lambda i: (i, 0, 0, 0)))
-            args.append(array.reshape(2, 2, rows, D))
-    share = groups[0][0].shape[1] + groups[0][1].shape[1]
-    out = pl.BlockSpec((1, count, share, D), lambda i: (i, 0, 0, 0))
-    shape = jax.ShapeDtypeStruct((2, count, share, D), BF16)
-    return call(
-        functools.partial(join_kernel, count),
-        "join",
-        8 * count * share * D,
-        24 * count * share * D,
-        24,
-        grid=(2,),
-        in_specs=[SMEM] + specs,
-        out_specs=[out, out],
-        out_shape=[shape, shape],
-    )(bit.reshape(1), *args)
-
-
-def finish_groups(groups):
-    count = len(groups)
-    keep, give = join(bit_of(2), groups)
-    share = keep.shape[2]
-    came = across(give, 2)
-    keep, give = fold(
-        bit_of(3), keep.reshape(1, 2, count * share, D), came.reshape(1, 2, count * share, D)
-    )
-    came = across(give, 3)
-    keep, came = keep.reshape(count, share, D), came.reshape(count, share, D)
-    return [keep[i].astype(F32) + came[i].astype(F32) for i in range(count)]
 
 
 def stacked(values, came, mine, axis):
@@ -1369,73 +1631,55 @@
         part_ref, qkv, gate_rows, strip, own_cot, peer_cot, came_cot_own, came_cot_peer, heads
     )
     mid, normed_two, scale_two = middle_part(w_out, attended, state, columns)
-    normed_two_peer = swap(normed_two)
     w_down_t = w_ffn_out.T
-    hid_own, gg_own, gu_own = ffn(w_gate, w_up, w_down_t, normed_two, cot_own)
-    hid_peer, gg_peer, gu_peer = ffn(w_gate, w_up, w_down_t, normed_two_peer, cot_peer)
-
     share = w_gate.shape[1] // dev_count
-    split = bits == 4 and share % 16 == 0
-    if split:
+    if bits == 4 and share % 16 == 0:
         cut = (share // 2 + 15) // 16 * 16
-        my_bits = jnp.stack([bit_of(0), bit_of(1)])
-        make = functools.partial(split_grad, cut, my_bits)
-    else:
-        make = weight_grad
-
-    def first_step(pieces):
-        if not split:
-            return ()
-        keep_x, give_x, keep_y, give_y = pieces
-        return (
-            (bit_of(1), keep_x, across(give_x, 0)),
-            (bit_of(0), keep_y, across(give_y, 1)),
+        one = feed(0, cut, w_gate, w_up, w_down_t, normed_two, cot_own, cot_peer, ())
+        two = feed(1, cut, w_gate, w_up, w_down_t, normed_two, cot_own, cot_peer, one[4:8])
+        keep_x, give_x, keep_y, give_y = two[4:8]
+        up_x = (keep_x, across(give_x, 0))
+        up_y = (keep_y, across(give_y, 1))
+        grad_mid, grad_attn, grad_attended, sum_ffn = after_feed(
+            (one[0], two[0], one[1], two[1]), mid, cot_own, columns, scale_two, w_out
         )
-
-    def second_step(folded_pieces):
-        keep_x, give_x, keep_y, give_y = folded_pieces
-        return keep_x, keep_y, across(give_x, 1), across(give_y, 0)
-
-    def run(kernel, side, *args):
-        out = kernel(side, *args)
-        return out if side else (out, ())
-
-    part_down = make(hid_own, hid_peer, cot_own, cot_peer)
-    side_down = first_step(part_down)
-    part_gate = make(gg_own, gg_peer, normed_two, normed_two_peer)
-    side_gate = first_step(part_gate)
-    part_up = make(gu_own, gu_peer, normed_two, normed_two_peer)
-    side_up = first_step(part_up)
-    gg_peer, gu_peer, gg_own, gu_own, _ = lax.optimization_barrier(
-        (gg_peer, gu_peer, gg_own, gu_own, part_up)
-    )
-    back_peer, fold_down = run(project, side_down, (w_gate, w_up), (gg_peer, gu_peer), BF16)
-    grad_mid, grad_attn, grad_attended, sum_ffn = middle_back(
-        w_gate, w_up, gg_own, gu_own, swap(back_peer), mid, cot_own, columns, scale_two, w_out
-    )
-    (grad_q, grad_k, grad_v, sums, near), fold_gate = run(
-        attend_back, side_gate, qkv, prob, grad_attended, wide, heads
-    )
-    keep, give = head_grads(part_ref, grad_q, grad_k, grad_v, normed_one, attended, grad_attn)
-    back_args = (
-        grad_q, grad_k, grad_v, w_qkv, normed_one, state, grad_mid, scale_one, del_logit, sums, columns
-    )
-    if split:
-        grad_down, grad_gate = finish_groups([second_step(fold_down), second_step(fold_gate)])
-        (_, keep_x, came_x), (_, keep_y, came_y) = side_up
+        grad_q, grad_k, grad_v, sums, near = attend_back(
+            (), qkv, prob, grad_attended, wide, heads
+        )
+        keep, give = head_grads(part_ref, grad_q, grad_k, grad_v, normed_one, attended, grad_attn)
         totals, grad_up, small, state_own, state_came = tail(
-            keep, give, (keep_x, came_x), (keep_y, came_y), sum_ffn,
-            near.reshape(heads * BUCKETS, TILE), *back_args,
+            keep, give, up_x, up_y, sum_ffn, near.reshape(heads * BUCKETS, TILE),
+            grad_q, grad_k, grad_v, w_qkv, normed_one, state, grad_mid, scale_one, del_logit, sums,
+            columns,
         )
+        mixed_parts = (one[2], two[2], one[3], two[3])
+        mixed = home(add_mixed(mixed_parts, mid))
         total_q, total_v, total_k, total_out = totals.reshape(4, inner // 2, D).astype(F32)
         grad_tokens = spread(part_ref, slot, state_own, state_came).T
         grad_ln_ffn, grad_ln_attn, grad_w_delete = small[0], small[1], small[2]
         grad_table = small[3, : heads * BUCKETS].reshape(heads, BUCKETS).T
+        grad_down, grad_gate = jnp.where(bit_of(3) == 0, one[8], two[8])
     else:
+        normed_two_peer = swap(normed_two)
+        hid_own, gg_own, gu_own = ffn(w_gate, w_up, w_down_t, normed_two, cot_own)
+        hid_peer, gg_peer, gu_peer = ffn(w_gate, w_up, w_down_t, normed_two_peer, cot_peer)
+        order = tuple(range(bits))
+        grad_down = halve(weight_grad(hid_own, hid_peer, cot_own, cot_peer), order)
+        grad_gate = halve(weight_grad(gg_own, gg_peer, normed_two, normed_two_peer), order)
+        grad_up = halve(weight_grad(gu_own, gu_peer, normed_two, normed_two_peer), order)
+        back_peer = project((), (w_gate, w_up), (gg_peer, gu_peer), BF16)
+        grad_mid, grad_attn, grad_attended, sum_ffn = middle_back(
+            w_gate, w_up, gg_own, gu_own, swap(back_peer), mid, cot_own, columns, scale_two, w_out
+        )
+        grad_q, grad_k, grad_v, sums, near = attend_back(
+            (), qkv, prob, grad_attended, wide, heads
+        )
+        keep, give = head_grads(part_ref, grad_q, grad_k, grad_v, normed_one, attended, grad_attn)
         total_q, total_v, total_k, total_out = sum_everywhere(keep, swap(give))
-        order = tuple(range(bits))
-        grad_down, grad_gate, grad_up = (halve(v, order) for v in (part_down, part_gate, part_up))
-        grad_state, sum_attn, sum_delete = input_back((), *back_args)
+        grad_state, sum_attn, sum_delete = input_back(
+            (), grad_q, grad_k, grad_v, w_qkv, normed_one, state, grad_mid, scale_one, del_logit,
+            sums, columns,
+        )
         grad_tokens = home(grad_state)
         grad_table = jnp.sum(near, axis=2).T
         small = jnp.concatenate(
@@ -1446,15 +1690,14 @@
         grad_ln_ffn, grad_ln_attn = small[:D], small[D : 2 * D]
         grad_w_delete = small[2 * D : 3 * D]
         grad_table = small[3 * D :].reshape(BUCKETS, heads)
-
-    mixed_peer = project((), (w_down_t,), (hid_peer,), BF16)
-    mixed = mixed_part(w_down_t, hid_own, swap(mixed_peer), mid)
+        mixed_peer = project((), (w_down_t,), (hid_peer,), BF16)
+        mixed = home(mixed_part(w_down_t, hid_own, swap(mixed_peer), mid))
 
     def own_half(values):
         return lax.dynamic_slice_in_dim(values, part * half, half, 0)
 
     return (
-        home(mixed),
+        mixed,
         grad_tokens,
         own_half(grad_ln_attn),
         total_q.T,

time: 527 us -> 444 us (0.84)
  waiting for transfers between devices: 79.1 us -> 2.56 us
  starting transfers between devices: 18.9 us -> 5.33 us
  Pallas kernels: 400 us -> 411 us
    ppermute x12 -> x2, waiting for transfers between devices: 76.6 us -> 0.01 us  [across(): return lax.ppermute(values, 'dp', [(i, i ^ 1 << bit) for i in range(size)])]
    pallas_call x12 -> x5, Pallas kernels: 192 us -> 219 us  [the longest x2 178 us: feed(): pl.pallas_call(functools.partial(feed_kernel, half, cut), name='feed_forw...]
    pallas_call x1, Pallas kernels: 125 us -> 109 us  [tail(): pl.pallas_call(tail_kernel, name='tail', in_specs=[VMEM] * (8 + len(value...]
    ppermute x12 -> x2, starting transfers between devices: 16.5 us -> 3.79 us  [across(): return lax.ppermute(values, 'dp', [(i, i ^ 1 << bit) for i in range(size)])]
  transfers between devices with their start and end apart: 21 -> 8, of which waited for: 8 -> 1; matrix products, arithmetic and copies ran while one was open for 2% -> 3% of each run, Pallas kernels for 59% -> 45%
where the time goes in v2:
time: 444 us; the launch traced here: 437 us
  Pallas kernels  411 us (93%)
  local copies, waits for them, and re-layouts  16.8 us (4%)
  starting transfers between devices  5.33 us (1%)
    pallas_call x2, Pallas kernels, feed(): pl.pallas_call(functools.partial(feed_kernel, half, cut), name='feed_forw...  178 us
    pallas_call x1, Pallas kernels, tail(): pl.pallas_call(tail_kernel, name='tail', in_specs=[VMEM] * (8 + len(value...  109 us
    pallas_call x1, Pallas kernels, attend_back(): call(attend_back_kernel, 'attend_back', heads * 8 * LMAX * LMAX * HDIM *...  18.1 us
    pallas_call x1, Pallas kernels, attend(): call(attend_kernel, 'attend', heads * 4 * LMAX * LMAX * HDIM * 4, heads *...  16.4 us
    pallas_call x1, Pallas kernels, after_feed(): call(after_feed_kernel, 'norm_back', 2 * D * LMAX * inner, D * LMAX * 26,...  14.5 us
    pallas_call x2, Pallas kernels, spread(): call(spread_kernel, 'spread', 2 * width * 7168 * 256, width * 2048 * 4, 1...  13 us
    pallas_call x1, Pallas kernels, head_grads(): call(head_grad_kernel, 'head_grads', 8 * D * LMAX * inner, D * LMAX * 4 +...  11.1 us
    pallas_call x1, Pallas kernels, compact_join(): call(compact_join_kernel, 'compact_join', 2 * width * 2 * 4608 * 256, wid...  10.2 us
  transfers between devices with their start and end apart: 8, of which 1 were waited for; matrix products, arithmetic and copies ran while one was open for 3% of the time, Pallas kernels for 45%

profile of v2, /device:TPU:0, one launch (start us, length us, event | category | flops | bytes accessed | tf_op | source)
XLA Modules:
  0.0 437.3 jit_solution(8154209590838124888)
XLA Ops:
  0.7 3.7 places.1
  4.4 0.5 collective-permute-start
  4.8 6.8 %compact.1 = (bf16[736,1024]{1,0:T(8,128)(2,1)}, bf16[736,1024]{1,0:T(8,128)(2,1)}) custom-call(s32[1]{0:T(128)} %bitcast.part_ref, s32[1,2048]{1,0:T(1,128)} %get-tuple-element.70.slot_ref, bf16[736,2048]{1,0:T(8,128)(2,1)} %bitcast.46), custom_call_target="tpu_custom_call" | custom-call | flops 3472883712 | bytes 6029312 | tf_op jit(solution)/shard_map/compact/pallas_call | solution.py:221
  11.6 0.1 collective-permute-start.1
  11.7 0.0 collective-permute-done.came_ref
  11.7 0.0 copy-start.8
  11.7 1.4 copy-done.8
  13.1 0.0 copy-start.7
  13.1 0.0 copy-start.4
  13.1 0.0 copy-start.5
  13.1 10.2 %compact_join.1 = (bf16[736,1024]{1,0:T(8,128)(2,1)}, bf16[736,1024]{1,0:T(8,128)(2,1)}, bf16[1152,1472]{1,0:T(8,128)(2,1)}, bf16[384,1472]{1,0:T(8,128)(2,1)}) custom-call(s32[1]{0:T(128)} %bitcast.part_ref, s32[1,2048]{1,0:T(1,128)} %get-tuple-element.70.slot_ref, bf16[736,2048]{1,0:T(8,128)(2,1)} %bitcast.47, ...), custom_call_target="tpu_custom_call" | custom-call | flops 3472883712 | bytes 6029312 | tf_op jit(solution)/shard_map/compact_join/pallas_call | solution.py:198
  23.3 0.5 collective-permute-start.3
  23.8 0.1 collective-permute-start.4
  23.9 0.0 copy-done.7
  23.9 0.4 collective-permute-start.2
  24.3 0.0 copy-done.6
  24.3 0.0 copy-done.4
  24.4 0.0 copy-done.5
  24.4 1.2 copy.41.gain_ref.columns_ref
  25.6 2.5 collective-permute-done.2
  28.2 0.1 copy.42
  28.2 0.1 copy.43
  28.3 0.6 broadcast_select_fusion.1.table_ref
  28.9 5.4 %bias_strip.1.strip_ref = f32[6,1920,128]{2,1,0:T(8,128)} custom-call(f32[32,6]{1,0:T(8,128)} %broadcast_select_fusion.1.table_ref), custom_call_target="tpu_custom_call" | custom-call | flops 18000000 | bytes 5898240 | tf_op jit(solution)/shard_map/bias_strip/pallas_call | solution.py:1190
  34.4 0.0 collective-permute-done.1.came_ref
  34.4 1.1 copy-done.10
  35.5 8.7 %norm_project.1 = (bf16[1472,1024]{1,0:T(8,128)(2,1)}, bf16[1472,1024]{1,0:T(8,128)(2,1)}, bf16[1152,1024]{1,0:T(8,128)(2,1)}, bf16[16,1024]{1,0:T(8,128)(2,1)}, f32[1,1024]{1,0:T(1,128)}, /*index=5*/f32[1,1024]{1,0:T(1,128)}) custom-call(s32[1]{0:T(128)} %bitcast.part_ref, bf16[736,1024]{1,0:T(8,128)(2,1)} %get-tuple-element.73.own_ref, ...), custom_call_target="tpu_custom_call" | custom-call | flops 3472883712 | bytes 15073280 | tf_op jit(solution)/shard_map/norm_project/pallas_call | solution.py:318
  44.2 0.0 collective-permute-done.3.came_own_ref
  44.2 0.0 copy-start.9
  44.3 0.0 collective-permute-done.4.came_peer_ref
  44.3 1.1 copy-done.9
  45.4 16.4 %attend.1 = (bf16[6,1024,1024]{2,1,0:T(8,128)(2,1)}, bf16[384,1024]{1,0:T(8,128)(2,1)}, f32[384,1024]{1,0:T(8,128)}, bf16[1472,1024]{1,0:T(8,128)(2,1)}, bf16[1472,1024]{1,0:T(8,128)(2,1)}) custom-call(s32[1]{0:T(128)} %bitcast.part_ref, bf16[1152,1024]{1,0:T(8,128)(2,1)} %get-tuple-element.77.q_ref.k_ref.v_ref, ...), custom_call_target="tpu_custom_call" | custom-call | flops 6442450944 | bytes 12582912 | tf_op jit(solution)/shard_map/attend/pallas_call | solution.py:1252
  61.8 8.0 %attention_out_norm.1 = (f32[1472,1024]{1,0:T(8,128)}, bf16[1472,1024]{1,0:T(8,128)(2,1)}, f32[1,1024]{1,0:T(1,128)}) custom-call(bf16[384,1472]{1,0:T(8,128)(2,1)} %get-tuple-element.72.weight_ref, bf16[384,1024]{1,0:T(8,128)(2,1)} %get-tuple-element.81.attended_ref, bf16[1472,1024]{1,0:T(8,128)(2,1)} %get-tuple-element.82.state_ref, ...), custom_call_target="tpu_custom_call" | custom-call | flops 1157627904 | bytes 12058624 | tf_op jit(solution)/shard_map/attention_out_norm/pallas_call | solution.py:348
  69.8 86.9 %feed_forward.2 = (bf16[1472,1024]{1,0:T(8,128)(2,1)}, bf16[1472,1024]{1,0:T(8,128)(2,1)}, bf16[1472,1024]{1,0:T(8,128)(2,1)}, bf16[1472,1024]{1,0:T(8,128)(2,1)...) custom-call(bf16[1472,1792]{1,0:T(8,128)(2,1)} %refs_0_.3, ...), custom_call_target="tpu_custom_call" | custom-call | flops 48620371968 | bytes 62914560 | tf_op jit(solution)/shard_map/feed_forward/pallas_call | solution.py:1065
  156.7 90.9 %feed_forward.3 = (bf16[1472,1024]{1,0:T(8,128)(2,1)}, bf16[1472,1024]{1,0:T(8,128)(2,1)}, bf16[1472,1024]{1,0:T(8,128)(2,1)}, bf16[1472,1024]{1,0:T(8,128)(2,1)...) custom-call(bf16[1472,1792]{1,0:T(8,128)(2,1)} %refs_0_.3, ...), custom_call_target="tpu_custom_call", output_to_operand_aliasing={{4}: (6, {}), {5}: (7, {}), {6}: (8, {}), {7}: (9, {})} | custom-call | flops 48620371968 | bytes 62914560 | tf_op jit(solution)/shard_map/feed_forward/pallas_call | solution.py:1065
  247.6 2.3 collective-permute-start.6
  249.9 1.5 collective-permute-start.7
  251.4 8.5 %mixed_sum.1 = bf16[1472,1024]{1,0:T(8,128)(2,1)} custom-call(bf16[1472,1024]{1,0:T(8,128)(2,1)} %get-tuple-element.86.one, bf16[1472,1024]{1,0:T(8,128)(2,1)} %get-tuple-element.91.two, bf16[1472,1024]{1,0:T(8,128)(2,1)} %get-tuple-element.92.three, bf16[1472,1024]{1,0:T(8,128)(2,1)} %get-tuple-element.93.four, f32[1472,1024]{1,0:T(8,128)} %get-tuple-element.94.mid_ref), custom_call_target="tpu_custom_call" | custom-call | flops 7536640 | bytes 21102592 | tf_op jit(solution)/shard_map/mixed_sum/pallas_call | solution.py:1142
  259.9 3.7 constant_dynamic-slice_fusion
  263.7 0.0 collective-permute-start.5
  263.7 14.5 %norm_back.1 = (f32[1472,1024]{1,0:T(8,128)}, bf16[1472,1024]{1,0:T(8,128)(2,1)}, bf16[384,1024]{1,0:T(8,128)(2,1)}, f32[1472,128]{1,0:T(8,128)}) custom-call(bf16[1472,1024]{1,0:T(8,128)(2,1)} %get-tuple-element.96.own_one, bf16[1472,1024]{1,0:T(8,128)(2,1)} %get-tuple-element.97.own_two, bf16[1472,1024]{1,0:T(8,128)(2,1)} %get-tuple-element.98.came_one, ...), custom_call_target="tpu_custom_call" | custom-call | flops 1157627904 | bytes 39190528 | tf_op jit(solution)/shard_map/norm_back/pallas_call | solution.py:1122
  278.2 18.1 %attend_back.1 = (bf16[384,1024]{1,0:T(8,128)(2,1)}, bf16[384,1024]{1,0:T(8,128)(2,1)}, bf16[384,1024]{1,0:T(8,128)(2,1)}, f32[6,8,1024]{2,1,0:T(8,128)}, f32[6,32,128]{2,1,0:T(8,128)}) custom-call(bf16[1152,1024]{1,0:T(8,128)(2,1)} %get-tuple-element.77.q_ref.k_ref.v_ref, bf16[1152,1024]{1,0:T(8,128)(2,1)} %get-tuple-element.77.q_ref.k_ref.v_ref, ...), custom_call_target="tpu_custom_call" | custom-call | flops 12884901888 | bytes 12582912 | tf_op jit(solution)/shard_map/attend_back/pallas_call | solution.py:1354
  296.3 0.0 copy-start.1
  296.3 0.0 copy-start.2
  296.3 11.1 %head_grads.1 = (bf16[4,192,1472]{2,1,0:T(8,128)(2,1)}, bf16[4,192,1472]{2,1,0:T(8,128)(2,1)}) custom-call(s32[1]{0:T(128)} %bitcast.part_ref, bf16[384,1024]{1,0:T(8,128)(2,1)} %get-tuple-element.103.q_ref, bf16[384,1024]{1,0:T(8,128)(2,1)} %get-tuple-element.104.v_ref, bf16[384,1024]{1,0:T(8,128)(2,1)} %get-tuple-element.105.k_ref, ...), custom_call_target="tpu_custom_call" | custom-call | flops 4630511616 | bytes 18219008 | tf_op jit(solution)/shard_map/head_grads/pallas_call | solution.py:513
  307.4 0.0 copy-done.1
  307.4 0.0 copy-done.2
  307.4 0.2 broadcast_select_fusion
  307.6 1.2 slice_bitcast_fusion
  308.7 0.0 collective-permute-done.7.came_y
  308.7 0.0 collective-permute-done.6.came_x
  308.8 108.5 %tail.1 = (bf16[4,2,2,48,1472]{4,3,2,1,0:T(8,128)(2,1)}, f32[112,1472]{1,0:T(8,128)}, f32[8,1472]{1,0:T(8,128)}, bf16[736,1024]{1,0:T(8,128)(2,1)}, bf16[736,1024]{1,0:T(8,128)(2,1)}) custom-call(bf16[4,2,2,48,1472]{4,3,2,1,0:T(8,128)(2,1)} %bitcast.32, bf16[4,2,2,48,1472]{4,3,2,1,0:T(8,128)(2,1)} %bitcast.33, ...), custom_call_target="tpu_custom_call" | custom-call | flops 3472883712 | bytes 62914560 | tf_op jit(solution)/shard_map/tail/pallas_call | solution.py:772
  417.3 0.7 slice_reduce_fusion.1
  418.0 0.1 reshape_squeeze.3
  418.1 1.5 fusion.1
  419.6 0.7 dynamic-slice_reduce_fusion
  420.3 0.6 dynamic-slice_bitcast_fusion
  420.9 6.5 %spread.3 = bf16[736,2048]{1,0:T(8,128)(2,1)} custom-call(s32[1]{0:T(128)} %bitcast.part_ref, s32[1,2048]{1,0:T(1,128)} %get-tuple-element.70.slot_ref, bf16[736,1024]{1,0:T(8,128)(2,1)} %get-tuple-element.120.own_ref, bf16[736,1024]{1,0:T(8,128)(2,1)} %get-tuple-element.121.peer_ref), custom_call_target="tpu_custom_call" | custom-call | flops 2701131776 | bytes 6029312 | tf_op jit(solution)/shard_map/spread/pallas_call | solution.py:256
  427.4 0.0 copy-done
  427.4 2.4 fusion
  429.8 0.0 collective-permute-done.5.peer_ref
  429.8 6.5 %spread.2 = bf16[736,2048]{1,0:T(8,128)(2,1)} custom-call(s32[1]{0:T(128)} %bitcast.part_ref, s32[1,2048]{1,0:T(1,128)} %get-tuple-element.70.slot_ref, bf16[736,1024]{1,0:T(8,128)(2,1)} %get-tuple-element.128.own_ref, bf16[736,1024]{1,0:T(8,128)(2,1)} %collective-permute-done.5.peer_ref), custom_call_target="tpu_custom_call" | custom-call | flops 2701131776 | bytes 6029312 | tf_op jit(solution)/shard_map/spread/pallas_call | solution.py:256
  436.3 0.0 copy-done.3
  436.3 0.8 copy.52
  (9 shorter events, 0.1 us)
Async XLA Ops:
  4.4 7.3 %collective-permute-start = (bf16[4,192,1472]{2,1,0:T(8,128)(2,1)}, bf16[4,192,1472]{2,1,0:T(8,128)(2,1)S(1)}, u32[]{:S(2)}, u32[]{:S(2)}) collective-permute-start(bf16[4,192,1472]{2,1,0:T(8,128)(2,1)} %get-tuple-element.71.stack_ref), channel_id=1, source_target_pairs={{0,1},{1,0},{2,3},{3,2},{4,5},{5,4},{6,7},{7,6},{8,9},{9,8},{10,11... | collective-permute-start | bytes 6782984 | tf_op jit(solution)/shard_map/ppermute | solution.py:1575
  11.6 22.8 %collective-permute-start.1 = (bf16[736,1024]{1,0:T(8,128)(2,1)}, bf16[736,1024]{1,0:T(8,128)(2,1)S(1)}, u32[]{:S(2)}, u32[]{:S(2)}) collective-permute-start(bf16[736,1024]{1,0:T(8,128)(2,1)} %get-tuple-element.74), channel_id=1, source_target_pairs={{0,1},{1,0},{2,3},{3,2},{4,5},{5,4},{6,7},{7,6},{8,9},{9,8},{10,11... | collective-permute-start | bytes 4521992 | tf_op jit(solution)/shard_map/ppermute | solution.py:1575
  11.7 1.4 copy-start.8
  13.1 10.8 %copy-start.7 = (f32[32,3]{0,1:T(4,128)S(1)}, f32[32,3]{0,1:T(4,128)}, u32[]{:S(2)}) copy-start(f32[32,3]{0,1:T(4,128)} %param.24) | copy-start | bytes 1156
  13.1 11.3 %copy-start.6 = (bf16[1472]{0:T(1024)(128)(2,1)S(1)}, bf16[1472]{0:T(1024)(128)(2,1)}, u32[]{:S(2)}) copy-start(bf16[1472]{0:T(1024)(128)(2,1)} %param.25) | copy-start | bytes 8836
  13.1 11.3 %copy-start.4 = (f32[1472]{0:T(1024)S(1)}, f32[1472]{0:T(1024)}, u32[]{:S(2)}) copy-start(f32[1472]{0:T(1024)} %param.19) | copy-start | bytes 17668
  13.1 11.3 %copy-start.5 = (f32[1472]{0:T(1024)S(1)}, f32[1472]{0:T(1024)}, u32[]{:S(2)}) copy-start(f32[1472]{0:T(1024)} %param.26) | copy-start | bytes 17668
  23.3 20.9 %collective-permute-start.3 = (bf16[736,1024]{1,0:T(8,128)(2,1)}, bf16[736,1024]{1,0:T(8,128)(2,1)S(1)}, u32[]{:S(2)}, u32[]{:S(2)}) collective-permute-start(bf16[736,1024]{1,0:T(8,128)(2,1)} %get-tuple-element.80.peer_ref), channel_id=1, source_target_pairs={{0,1},{1,0},{2,3},{3,2},{4,5},{5,4},{6,7},{7,6},{8,9},{9,8},{10,11... | collective-permute-start | bytes 4521992 | tf_op jit(solution)/shard_map/ppermute | solution.py:1575
  23.8 20.4 %collective-permute-start.4 = (bf16[736,1024]{1,0:T(8,128)(2,1)}, bf16[736,1024]{1,0:T(8,128)(2,1)}, u32[]{:S(2)}, u32[]{:S(2)}) collective-permute-start(bf16[736,1024]{1,0:T(8,128)(2,1)} %get-tuple-element.79.own_ref), channel_id=1, source_target_pairs={{0,1},{1,0},{2,3},{3,2},{4,5},{5,4},{6,7},{7,6},{8,9},{9,8},{10,11... | collective-permute-start | bytes 4521992 | tf_op jit(solution)/shard_map/ppermute | solution.py:1575
  23.9 4.2 collective-permute-start.2
  34.4 1.1 copy-start.10
  44.2 1.1 copy-start.9
  247.6 61.1 %collective-permute-start.6 = (bf16[4,2,64,1472]{3,2,1,0:T(8,128)(2,1)}, bf16[4,2,64,1472]{3,2,1,0:T(8,128)(2,1)}, u32[]{:S(2)}, u32[]{:S(2)}) collective-permute-start(bf16[4,2,64,1472]{3,2,1,0:T(8,128)(2,1)} %get-tuple-element.111), channel_id=1, source_target_pairs={{0,2},{2,0},{4,6},{6,4},{8,10},{10,8},{12,14},{14,12},{16,18},{18,... | collective-permute-start | bytes 4521992 | tf_op jit(solution)/shard_map/ppermute | solution.py:1499
  249.9 58.8 %collective-permute-start.7 = (bf16[4,2,48,1472]{3,2,1,0:T(8,128)(2,1)}, bf16[4,2,48,1472]{3,2,1,0:T(8,128)(2,1)}, u32[]{:S(2)}, u32[]{:S(2)}) collective-permute-start(bf16[4,2,48,1472]{3,2,1,0:T(8,128)(2,1)} %get-tuple-element.113), channel_id=1, source_target_pairs={{0,4},{2,6},{4,0},{6,2},{8,12},{10,14},{12,8},{14,10},{16,20},{18,... | collective-permute-start | bytes 3391496 | tf_op jit(solution)/shard_map/ppermute | solution.py:1499
  263.7 166.1 %collective-permute-start.5 = (bf16[736,1024]{1,0:T(8,128)(2,1)}, bf16[736,1024]{1,0:T(8,128)(2,1)}, u32[]{:S(2)}, u32[]{:S(2)}) collective-permute-start(bf16[736,1024]{1,0:T(8,128)(2,1)} %get-tuple-element.127), channel_id=1, source_target_pairs={{0,1},{1,0},{2,3},{3,2},{4,5},{5,4},{6,7},{7,6},{8,9},{9,8},{10,11... | collective-permute-start | bytes 4521992 | tf_op jit(solution)/shard_map/ppermute | solution.py:1575
  296.3 11.1 %copy-start.1 = (f32[2,112,1472]{2,1,0:T(8,128)S(1)}, f32[2,112,1472]{2,1,0:T(8,128)}, u32[]{:S(2)}) copy-start(f32[2,112,1472]{2,1,0:T(8,128)} %get-tuple-element.124) | copy-start | bytes 3956740
  296.3 11.1 %copy-start.2 = (f32[2,112,1472]{2,1,0:T(8,128)S(1)}, f32[2,112,1472]{2,1,0:T(8,128)}, u32[]{:S(2)}) copy-start(f32[2,112,1472]{2,1,0:T(8,128)} %get-tuple-element.125) | copy-start | bytes 3956740
  420.9 6.5 %copy-start = (bf16[4,2,2,48,1472]{4,3,2,1,0:T(8,128)(2,1)S(1)}, bf16[4,2,2,48,1472]{4,3,2,1,0:T(8,128)(2,1)}, u32[]{:S(2)}) copy-start(bf16[4,2,2,48,1472]{4,3,2,1,0:T(8,128)(2,1)} %get-tuple-element.123) | copy-start | bytes 6782980
  429.8 6.5 %copy-start.3 = (f32[112,1472]{1,0:T(8,128)S(1)}, f32[112,1472]{1,0:T(8,128)}, u32[]{:S(2)}) copy-start(f32[112,1472]{1,0:T(8,128)} %get-tuple-element.126) | copy-start | bytes 1978372

commit v3 on v2

--- a/solution.py
+++ b/solution.py
@@ -79,7 +79,7 @@
         cost_estimate=pl.CostEstimate(
             flops=int(flops), bytes_accessed=int(nbytes), transcendentals=0
         ),
-        compiler_params=pltpu.CompilerParams(vmem_limit_bytes=56 << 20),
+        compiler_params=pltpu.CompilerParams(vmem_limit_bytes=limit << 20),
         **kw,
     )
     if not side:
@@ -320,7 +320,7 @@
         "norm_project",
         2 * D * LMAX * weights.shape[0],
         D * LMAX * 10,
-        24,
+        48,
         grid=(LMAX // QBLOCK,),
         in_specs=[SMEM, half, half, COLUMN, whole_spec(weights), whole_spec(count)],
         out_specs=[
@@ -350,7 +350,7 @@
         "attention_out_norm",
         2 * D * LMAX * inner,
         D * LMAX * 8,
-        24,
+        48,
         grid=(LMAX // QBLOCK,),
         in_specs=[
             whole_spec(weights),
@@ -395,7 +395,7 @@
         "norm_back",
         4 * D * LMAX * units,
         D * LMAX * 20 + 4 * D * units,
-        44,
+        48,
         grid=(LMAX // QBLOCK,),
         in_specs=[
             whole_spec(w_gate), whole_spec(w_up), unit_rows, unit_rows, ROWS, ROWS, ROWS, COLUMN,
@@ -455,7 +455,7 @@
         "project_norm_back",
         6 * D * LMAX * inner,
         D * LMAX * 12,
-        28,
+        48,
         side=side,
         grid=(LMAX // QBLOCK,),
         in_specs=[
@@ -486,7 +486,7 @@
         "mixed",
         2 * D * LMAX * units,
         D * LMAX * 8 + D * units * 2,
-        24,
+        48,
         grid=(D // width,),
         in_specs=[pl.BlockSpec((width, units), lambda i: (i, 0)), whole_spec(hid), rows, rows],
         out_specs=rows,
@@ -592,13 +592,52 @@
 
 def tail_kernel(
     keep_ref, give_ref, keep_x, came_x, keep_y, came_y, ffn_sum_ref, near_ref,
-    q_ref, k_ref, v_ref, weight_ref, normed_ref, state_ref, grad_mid_ref, scale_ref, logit_ref,
-    sums_ref, columns_ref,
-    out_ref, share_ref, vector_ref, own_ref, came_grad_ref,
+    scale_ref, logit_ref, sums_ref, columns_ref,
+    q_hbm, k_hbm, v_hbm, normed_hbm, state_hbm, grad_mid_hbm, mix_one, mix_two, mix_three, mix_four,
+    mid_hbm, weight_hbm,
+    out_ref, share_ref, vector_ref, own_ref, came_grad_ref, own_mixed_ref, came_mixed_ref,
     came_ref, total, from_x, from_y, sum_x, sum_y, last_x, last_y, plane_sum, from_planes,
     give_x, give_y, second_x, second_y, whole, from_whole,
-    vector, vector_core, vector_near, vector_far, grad_state, send_sems, recv_sems,
+    vector, vector_core, vector_near, vector_far, sent_grad, sent_mixed, block_hold,
+    head_hold, half_hold, wide_hold, weight_ref, load_sems, weight_sem, send_sems, recv_sems,
 ):
+    loads = {}
+
+    def load_block(block):
+        cols = slice(block * QBLOCK, (block + 1) * QBLOCK)
+        slot = block % 2
+        pairs = [
+            (source.at[:, cols], head_hold.at[slot, i])
+            for i, source in enumerate((q_hbm, k_hbm, v_hbm))
+        ]
+        pairs += [
+            (source.at[:, cols], half_hold.at[slot, i])
+            for i, source in enumerate((normed_hbm, state_hbm))
+        ]
+        pairs.append((grad_mid_hbm.at[:, cols], wide_hold.at[slot]))
+        start_loads(("grad", block), slot, pairs)
+
+    def load_mixed(block):
+        cols = slice(block * QBLOCK, (block + 1) * QBLOCK)
+        slot = block % 2
+        pairs = [
+            (source.at[:, cols], half_hold.at[slot, i])
+            for i, source in enumerate((mix_one, mix_two, mix_three, mix_four))
+        ]
+        pairs.append((mid_hbm.at[:, cols], wide_hold.at[slot]))
+        start_loads(("mixed", block), slot, pairs)
+
+    def start_loads(key, slot, pairs):
+        loads[key] = []
+        for i, (source, target) in enumerate(pairs):
+            copy = pltpu.make_async_copy(source, target, load_sems.at[slot, i])
+            copy.start()
+            loads[key].append(copy)
+
+    weight_load = pltpu.make_async_copy(weight_hbm, weight_ref, weight_sem)
+    weight_load.start()
+    load_block(0)
+    load_block(1)
     at = neighbours()
     x, y, z = at["x"], at["y"], at["z"]
     to_x, to_y = at["to_x"], at["to_y"]
@@ -675,19 +714,42 @@
     parts = []
     came_grads = []
 
+    def part_out(cols, values, out_ref, sent_ref, came_ref):
+        block_hold[...] = values
+        out_ref[:, cols] = block_hold[mine]
+        sent_ref[:, cols] = block_hold[other]
+        came_grads.append(
+            sender.start(sent_ref.at[:, cols], came_ref.at[:, cols], at["to_core"])
+        )
+
     def compute(block):
+        if block == 0:
+            weight_load.wait()
+        for copy in loads["grad", block]:
+            copy.wait()
         cols = slice(block * QBLOCK, (block + 1) * QBLOCK)
+        slot = block % 2
         grad, gain_part, delete_part = input_back_block(
-            q_ref[:, cols], k_ref[:, cols], v_ref[:, cols], weight_ref, normed_ref[:, cols],
-            state_ref[:, cols], grad_mid_ref[:, cols], scale_ref[:, cols], logit_ref[:, cols],
-            sums_ref[:, :, cols], columns_ref[...],
+            head_hold[slot, 0], head_hold[slot, 1], head_hold[slot, 2], weight_ref,
+            half_hold[slot, 0], half_hold[slot, 1], wide_hold[slot], scale_ref[:, cols],
+            logit_ref[:, cols], sums_ref[:, :, cols], columns_ref[...],
         )
-        grad_state[:, cols] = grad
-        own_ref[:, cols] = grad_state[mine, cols]
-        came_grads.append(
-            sender.start(grad_state.at[other, cols], came_grad_ref.at[:, cols], at["to_core"])
-        )
+        part_out(cols, grad, own_ref, sent_grad, came_grad_ref)
         parts.append((gain_part, delete_part))
+        if block < 2:
+            load_block(block + 2)
+        else:
+            load_mixed(block - 2)
+
+    def compute_mixed(block):
+        for copy in loads["mixed", block]:
+            copy.wait()
+        cols = slice(block * QBLOCK, (block + 1) * QBLOCK)
+        slot = block % 2
+        values = plus(wide_hold[slot], *[half_hold[slot, i] for i in range(4)]).astype(BF16)
+        part_out(cols, values, own_mixed_ref, sent_mixed, came_mixed_ref)
+        if block < 2:
+            load_mixed(block + 2)
 
     ones = jnp.ones((8, 128), F32)
 
@@ -696,6 +758,7 @@
             ones, values, NT, preferred_element_type=F32, precision=lax.Precision.HIGHEST
         )[:1]
 
+    cut = keep_x.shape[2]
     advance(0, 0)
     compute(0)
     advance(0, 1)
@@ -724,9 +787,9 @@
     vectors = [sender.start(vector, vector_core, at["to_core"])]
     advance(0, 5)
     advance(1, 4)
+    compute_mixed(0)
     advance(2, 3)
     arrived(seconds)
-    cut = keep_x.shape[2]
     whole[:, :cut] = plus(keep_x[:, y], came_x[:, y], second_x[...]).astype(BF16)
     whole[:, cut:] = plus(keep_y[:, x], came_y[:, x], second_y[...]).astype(BF16)
     wholes = [
@@ -740,7 +803,9 @@
         for k, device in enumerate((to_x, to_y, at["to_corner"]))
     ]
     advance(1, 5)
+    compute_mixed(1)
     advance(2, 4)
+    compute_mixed(2)
     arrived(vectors)
     vector_ref[...] = vector_core[...] + vector_near[0] + vector_near[1] + vector_near[2]
     vectors = [
@@ -748,6 +813,7 @@
         for k, device in enumerate(at["to_plane"])
     ]
     advance(2, 5)
+    compute_mixed(3)
     arrived(wholes)
     share_ref[...] = plus(whole[z], from_whole[0], from_whole[1], from_whole[2])
     for copies in flying:
@@ -758,13 +824,14 @@
     vector_ref[...] = vector_ref[...] + vector_far[0] + vector_far[1] + vector_far[2]
 
 
-def tail(keep, give, up_x, up_y, ffn_sum, near, *values):
+def tail(keep, give, up_x, up_y, ffn_sum, near, lines, far):
     rows = keep.shape[1] // 4
     (keep_x, came_x), (keep_y, came_y) = up_x, up_y
     cut, rest = keep_x.shape[2], keep_y.shape[2]
     share = cut + rest
     shape = (4, 2, 2, rows, D)
     copies = 80
+    heads = far[0].shape[0]
 
     def hold(*dims, dtype=BF16):
         return pltpu.VMEM(dims, dtype)
@@ -772,14 +839,13 @@
     return pl.pallas_call(
         tail_kernel,
         name="tail",
-        in_specs=[VMEM] * (8 + len(values)),
-        out_specs=[VMEM] * 5,
+        in_specs=[VMEM] * (8 + len(lines)) + [ANY] * len(far),
+        out_specs=[VMEM] * 7,
         out_shape=[
             jax.ShapeDtypeStruct(shape, BF16),
             jax.ShapeDtypeStruct((share, D), F32),
             jax.ShapeDtypeStruct((8, D), F32),
-            jax.ShapeDtypeStruct((D // 2, LMAX), BF16),
-            jax.ShapeDtypeStruct((D // 2, LMAX), BF16),
+            *[jax.ShapeDtypeStruct((D // 2, LMAX), BF16)] * 4,
         ],
         scratch_shapes=[
             hold(*shape), hold(*shape), hold(2, 2, rows, D), hold(2, 2, rows, D),
@@ -788,7 +854,11 @@
             hold(4, cut, D), hold(4, rest, D), hold(4, cut, D), hold(4, rest, D),
             hold(4, share, D), hold(3, share, D),
             hold(8, D, dtype=F32), hold(8, D, dtype=F32), hold(3, 8, D, dtype=F32),
-            hold(3, 8, D, dtype=F32), hold(D, LMAX),
+            hold(3, 8, D, dtype=F32), hold(D // 2, LMAX), hold(D // 2, LMAX), hold(D, QBLOCK),
+            hold(2, 3, heads, QBLOCK), hold(2, 4, D, QBLOCK), hold(2, D, QBLOCK, dtype=F32),
+            hold(3 * heads, D),
+            pltpu.SemaphoreType.DMA((2, 6)),
+            pltpu.SemaphoreType.DMA,
             pltpu.SemaphoreType.DMA((copies,)),
             pltpu.SemaphoreType.DMA((copies,)),
         ],
@@ -798,7 +868,7 @@
         compiler_params=pltpu.CompilerParams(
             vmem_limit_bytes=63 << 20, collective_id=1, has_side_effects=True
         ),
-    )(keep.reshape(shape), give.reshape(shape), keep_x, came_x, keep_y, came_y, ffn_sum, near, *values)
+    )(keep.reshape(shape), give.reshape(shape), keep_x, came_x, keep_y, came_y, ffn_sum, near, *lines, *far)
 
 
 PLANES = 2
@@ -1124,7 +1194,7 @@
         "norm_back",
         2 * D * LMAX * inner,
         D * LMAX * 26,
-        44,
+        48,
         grid=(LMAX // QBLOCK,),
         in_specs=[ROWS] * 6 + [COLUMN, LINE, whole_spec(w_out)],
         out_specs=[ROWS, ROWS, pl.BlockSpec((inner, QBLOCK), lambda i: (0, i)), SUMS],
@@ -1132,24 +1202,6 @@
             line(D), line(D, BF16), line(inner, BF16), jax.ShapeDtypeStruct((D, 128), F32),
         ],
     )(*parts, mid, cot, columns, scale, w_out)
-
-
-def add_mixed_kernel(one, two, three, four, mid_ref, out_ref):
-    out_ref[...] = plus(mid_ref[...], one[...], two[...], three[...], four[...]).astype(BF16)
-
-
-def add_mixed(parts, mid):
-    return call(
-        add_mixed_kernel,
-        "mixed_sum",
-        D * LMAX * 5,
-        D * LMAX * 14,
-        44,
-        grid=(LMAX // QBLOCK,),
-        in_specs=[ROWS] * 5,
-        out_specs=ROWS,
-        out_shape=line(D, BF16),
-    )(*parts, mid)
 
 
 STRIP = LMAX + LMAX - TILE
@@ -1254,7 +1306,7 @@
         "attend",
         heads * 4 * LMAX * LMAX * HDIM * 4,
         heads * LMAX * LMAX * 2,
-        36,
+        48,
         grid=(heads,),
         in_specs=[
             SMEM,
@@ -1356,7 +1408,7 @@
         "attend_back",
         heads * 8 * LMAX * LMAX * HDIM * 4,
         heads * LMAX * LMAX * 2,
-        28,
+        48,
         side=side,
         grid=(heads,),
         in_specs=[
@@ -1410,7 +1462,7 @@
         "ffn",
         6 * D * units * LMAX,
         3 * D * units * 2 + 2 * D * LMAX * 2 + 3 * units * LMAX * 2,
-        28,
+        48,
         grid=(units // width,),
         in_specs=[weight, weight, weight, whole, whole],
         out_specs=[out, out, out],
@@ -1433,7 +1485,7 @@
         "weight_grad",
         4 * D * units * LMAX,
         4 * D * LMAX + 4 * units * LMAX + 2 * units * D,
-        28,
+        48,
         grid=(units // width,),
         in_specs=[left, left, whole, whole],
         out_specs=pl.BlockSpec((width, D), lambda i: (i, 0)),
@@ -1459,7 +1511,7 @@
         "project",
         2 * count * D * units * LMAX,
         2 * count * (D * units + units * LMAX) + 4 * D * LMAX,
-        28,
+        48,
         side=side,
         grid=(D // width,),
         in_specs=[weight] * count + [whole] * count,
@@ -1486,7 +1538,7 @@
         "fold",
         4 * keep.size,
         6 * keep.size,
-        16,
+        48,
         grid=(steps,),
         in_specs=[SMEM, block, block],
         out_specs=[out, out],
@@ -1647,13 +1699,15 @@
             (), qkv, prob, grad_attended, wide, heads
         )
         keep, give = head_grads(part_ref, grad_q, grad_k, grad_v, normed_one, attended, grad_attn)
-        totals, grad_up, small, state_own, state_came = tail(
+        totals, grad_up, small, state_own, state_came, mixed_own, mixed_came = tail(
             keep, give, up_x, up_y, sum_ffn, near.reshape(heads * BUCKETS, TILE),
-            grad_q, grad_k, grad_v, w_qkv, normed_one, state, grad_mid, scale_one, del_logit, sums,
-            columns,
+            (scale_one, del_logit, sums, columns),
+            (
+                grad_q, grad_k, grad_v, normed_one, state, grad_mid, one[2], two[2], one[3], two[3],
+                mid, w_qkv,
+            ),
         )
-        mixed_parts = (one[2], two[2], one[3], two[3])
-        mixed = home(add_mixed(mixed_parts, mid))
+        mixed = spread(part_ref, slot, mixed_own, mixed_came).T
         total_q, total_v, total_k, total_out = totals.reshape(4, inner // 2, D).astype(F32)
         grad_tokens = spread(part_ref, slot, state_own, state_came).T
         grad_ln_ffn, grad_ln_attn, grad_w_delete = small[0], small[1], small[2]

time: 444 us -> 421 us (0.948)
  Pallas kernels: 411 us -> 376 us
  local copies, waits for them, and re-layouts: 16.8 us -> 31.7 us
    unnamed x23 -> x91, local copies, waits for them, and re-layouts: 4.51 us -> 22.3 us
    pallas_call x2 -> x1, Pallas kernels: 117 us -> 105 us  [tail(): pl.pallas_call(tail_kernel, name='tail', in_specs=[VMEM] * (8 + len(lines...]
    pallas_call x1, Pallas kernels: 11.1 us -> 5.25 us  [head_grads(): call(head_grad_kernel, 'head_grads', 8 * D * LMAX * inner, D * LMAX * 4 +...]
  transfers between devices with their start and end apart: 8 -> 7, of which waited for: 1 -> 1; matrix products, arithmetic and copies ran while one was open for 3% -> 0% of each run, Pallas kernels for 45% -> 14%
where the time goes in v3:
time: 421 us; the launch traced here: 417 us
  Pallas kernels  376 us (89%)
  local copies, waits for them, and re-layouts  31.7 us (8%)
  starting transfers between devices  4.86 us (1%)
    pallas_call x2, Pallas kernels, feed(): pl.pallas_call(functools.partial(feed_kernel, half, cut), name='feed_forw...  178 us
    pallas_call x1, Pallas kernels, tail(): pl.pallas_call(tail_kernel, name='tail', in_specs=[VMEM] * (8 + len(lines...  105 us
    unnamed x91, local copies, waits for them, and re-layouts  22.3 us
    pallas_call x1, Pallas kernels, attend_back(): call(attend_back_kernel, 'attend_back', heads * 8 * LMAX * LMAX * HDIM *...  17.3 us
    pallas_call x1, Pallas kernels, attend(): call(attend_kernel, 'attend', heads * 4 * LMAX * LMAX * HDIM * 4, heads *...  16.5 us
    pallas_call x1, Pallas kernels, after_feed(): call(after_feed_kernel, 'norm_back', 2 * D * LMAX * inner, D * LMAX * 26,...  12.9 us
    pallas_call x2, Pallas kernels, spread(): call(spread_kernel, 'spread', 2 * width * 7168 * 256, width * 2048 * 4, 1...  9.18 us
  transfers between devices with their start and end apart: 7, of which 1 were waited for; matrix products, arithmetic and copies ran while one was open for 0% of the time, Pallas kernels for 14%

profile of v3, /device:TPU:0, one launch (start us, length us, event | category | flops | bytes accessed | tf_op | source)
XLA Modules:
  0.0 416.6 jit_solution(16962197197203057537)
XLA Ops:
  0.7 1.1 copy-done.14
  1.7 1.1 copy-done.15
  2.8 1.1 copy-done.16
  3.9 1.1 copy-done.17
  4.9 0.7 copy-done.20
  5.6 0.7 copy-done.23
  6.3 1.3 places.1
  7.6 0.5 collective-permute-start.1
  8.1 1.9 copy-done.24
  10.0 4.9 %compact.1 = (bf16[736,1024]{1,0:T(8,128)(2,1)S(1)}, bf16[736,1024]{1,0:T(8,128)(2,1)}) custom-call(s32[1]{0:T(128)} %bitcast.part_ref, s32[1,2048]{1,0:T(1,128)S(1)} %get-tuple-element.72.slot_ref, bf16[736,2048]{1,0:T(8,128)(2,1)S(1)} %bitcast.39), custom_call_target="tpu_custom_call" | custom-call | flops 3472883712 | bytes 6029312 | tf_op jit(solution)/shard_map/compact/pallas_call | solution.py:221
  14.8 1.1 copy-done.36
  16.0 0.1 collective-permute-start
  16.0 0.0 collective-permute-done.1.came_ref
  16.0 0.0 copy-start.44
  16.0 0.0 copy-start.43
  16.1 0.0 copy-start.41
  16.1 0.0 copy-start.42
  16.1 8.0 %compact_join.1 = (bf16[736,1024]{1,0:T(8,128)(2,1)}, bf16[736,1024]{1,0:T(8,128)(2,1)}, bf16[1152,1472]{1,0:T(8,128)(2,1)S(1)}, bf16[384,1472]{1,0:T(8,128)(2,1)S(1)}) custom-call(s32[1]{0:T(128)} %bitcast.part_ref, s32[1,2048]{1,0:T(1,128)S(1)} %get-tuple-element.72.slot_ref, bf16[736,2048]{1,0:T(8,128)(2,1)S(1)} %bitcast.40, ...), custom_call_target="tpu_custom_call" | custom-call | flops 3472883712 | bytes 6029312 | tf_op jit(solution)/shard_map/compact_join/pallas_call | solution.py:198
  24.1 1.7 copy-done.4
  25.8 0.5 collective-permute-start.3
  26.3 0.1 collective-permute-start.4
  26.4 0.5 collective-permute-start.2
  26.9 0.3 copy.41.gain_ref.columns_ref
  27.2 2.0 collective-permute-done.2
  29.3 0.1 copy.42
  29.3 0.1 copy.43
  29.4 2.4 bias_strip.1.strip_ref
  31.9 2.5 copy-done.1
  34.3 0.0 collective-permute-done.came_ref
  34.3 8.1 %norm_project.1 = (bf16[1472,1024]{1,0:T(8,128)(2,1)}, bf16[1472,1024]{1,0:T(8,128)(2,1)}, bf16[1152,1024]{1,0:T(8,128)(2,1)S(1)}, bf16[16,1024]{1,0:T(8,128)(2,...) custom-call(s32[1]{0:T(128)} %bitcast.part_ref, bf16[736,1024]{1,0:T(8,128)(2,1)S(1)} %copy-done.37, ...), custom_call_target="tpu_custom_call" | custom-call | flops 3472883712 | bytes 15073280 | tf_op jit(solution)/shard_map/norm_project/pallas_call | solution.py:318
  42.4 0.6 copy-done.22
  43.0 1.4 copy-done.34
  44.5 16.5 %attend.1 = (bf16[6,1024,1024]{2,1,0:T(8,128)(2,1)}, bf16[384,1024]{1,0:T(8,128)(2,1)S(1)}, f32[384,1024]{1,0:T(8,128)}, bf16[1472,1024]{1,0:T(8,128)(2,1)}, bf16[1472,1024]{1,0:T(8,128)(2,1)}) custom-call(s32[1]{0:T(128)} %bitcast.part_ref, bf16[1152,1024]{1,0:T(8,128)(2,1)} %copy-done.34, bf16[1152,1024]{1,0:T(8,128)(2,1)} %copy-done.34, ...), custom_call_target="tpu_custom_call" | custom-call | flops 6442450944 | bytes 12582912 | tf_op jit(solution)/shard_map/attend/pallas_call | solution.py:1304
  61.0 0.0 copy-start.8
  61.0 7.1 %attention_out_norm.1 = (f32[1472,1024]{1,0:T(8,128)}, bf16[1472,1024]{1,0:T(8,128)(2,1)S(1)}, f32[1,1024]{1,0:T(1,128)S(1)}) custom-call(bf16[384,1472]{1,0:T(8,128)(2,1)S(1)} %get-tuple-element.83.weight_ref, bf16[384,1024]{1,0:T(8,128)(2,1)S(1)} %get-tuple-element.84.attended_ref, bf16[1472,1024]{1,0:T(8,128)(2,1)} %get-tuple-element.85.state_ref.state_hbm, ...), custom_call_target="tpu_custom_call" | custom-call | flops 1157627904 | bytes 12058624 | tf_op jit(solution)/shard_map/attention_out_norm/pallas_call | solution.py:348
  68.1 1.7 copy-done.27
  69.7 87.0 %feed_forward.2 = (bf16[1472,1024]{1,0:T(8,128)(2,1)}, bf16[1472,1024]{1,0:T(8,128)(2,1)}, bf16[1472,1024]{1,0:T(8,128)(2,1)}, bf16[1472,1024]{1,0:T(8,128)(2,1)...) custom-call(bf16[1472,1792]{1,0:T(8,128)(2,1)} %refs_0_.3, ...), custom_call_target="tpu_custom_call" | custom-call | flops 48620371968 | bytes 62914560 | tf_op jit(solution)/shard_map/feed_forward/pallas_call | solution.py:1135
  156.8 91.2 %feed_forward.3 = (bf16[1472,1024]{1,0:T(8,128)(2,1)}, bf16[1472,1024]{1,0:T(8,128)(2,1)}, bf16[1472,1024]{1,0:T(8,128)(2,1)}, bf16[1472,1024]{1,0:T(8,128)(2,1)...) custom-call(bf16[1472,1792]{1,0:T(8,128)(2,1)} %refs_0_.3, ...), custom_call_target="tpu_custom_call", output_to_operand_aliasing={{4}: (6, {}), {5}: (7, {}), {6}: (8, {}), {7}: (9, {})} | custom-call | flops 48620371968 | bytes 62914560 | tf_op jit(solution)/shard_map/feed_forward/pallas_call | solution.py:1135
  248.0 1.8 collective-permute-start.5
  249.8 1.5 collective-permute-start.6
  251.3 1.3 copy-done.3
  252.6 12.9 %norm_back.1 = (f32[1472,1024]{1,0:T(8,128)}, bf16[1472,1024]{1,0:T(8,128)(2,1)}, bf16[384,1024]{1,0:T(8,128)(2,1)S(1)}, f32[1472,128]{1,0:T(8,128)S(1)}) custom-call(bf16[1472,1024]{1,0:T(8,128)(2,1)} %get-tuple-element.89.own_one, bf16[1472,1024]{1,0:T(8,128)(2,1)} %get-tuple-element.94.own_two, bf16[1472,1024]{1,0:T(8,128)(2,1)} %get-tuple-element.95.came_one, ...), custom_call_target="tpu_custom_call" | custom-call | flops 1157627904 | bytes 39190528 | tf_op jit(solution)/shard_map/norm_back/pallas_call | solution.py:1192
  265.5 0.9 copy-done.13
  266.4 17.3 %attend_back.1 = (bf16[384,1024]{1,0:T(8,128)(2,1)S(1)}, bf16[384,1024]{1,0:T(8,128)(2,1)S(1)}, bf16[384,1024]{1,0:T(8,128)(2,1)S(1)}, f32[6,8,1024]{2,1,0:T(8,128)S(1)}, f32[6,32,128]{2,1,0:T(8,128)S(1)}) custom-call(bf16[1152,1024]{1,0:T(8,128)(2,1)} %copy-done.34, bf16[1152,1024]{1,0:T(8,128)(2,1)} %copy-done.34, bf16[1152,1024]{1,0:T(8,128)(2,1)} %copy-done.34, ...), custom_call_target="tpu_custom_call" | custom-call | flops 12884901888 | bytes 12582912 | tf_op jit(solution)/shard_map/attend_back/pallas_call | solution.py:1406
  283.7 0.0 copy-start.10
  283.7 0.0 copy-start.11
  283.7 0.0 copy-start.12
  283.7 0.0 copy-start.18
  283.8 5.2 %head_grads.1 = (bf16[4,192,1472]{2,1,0:T(8,128)(2,1)S(1)}, bf16[4,192,1472]{2,1,0:T(8,128)(2,1)S(1)}) custom-call(s32[1]{0:T(128)} %bitcast.part_ref, bf16[384,1024]{1,0:T(8,128)(2,1)S(1)} %get-tuple-element.101.q_ref.q_hbm, bf16[384,1024]{1,0:T(8,128)(2,1)S(1)} %get-tuple-element.102.v_ref.v_hbm, bf16[384,1024]{1,0:T(8,128)(2,1)S(1)} %get-tuple-element.103.k_ref.k_hbm, ...), custom_call_target="tpu_custom_call" | custom-call | flops 4630511616 | bytes 18219008 | tf_op jit(solution)/shard_map/head_grads/pallas_call | solution.py:513
  289.1 1.5 copy-done.7
  290.6 0.2 broadcast_select_fusion
  290.8 1.2 copy-done.6
  292.0 1.2 slice_bitcast_fusion
  293.2 0.0 collective-permute-done.6.came_y
  293.2 105.4 %tail.1 = (bf16[4,2,2,48,1472]{4,3,2,1,0:T(8,128)(2,1)}, f32[112,1472]{1,0:T(8,128)}, f32[8,1472]{1,0:T(8,128)}, bf16[736,1024]{1,0:T(8,128)(2,1)}, bf16[736,102...) custom-call(bf16[4,2,2,48,1472]{4,3,2,1,0:T(8,128)(2,1)} %bitcast.32, ...), custom_call_target="tpu_custom_call" | custom-call | flops 3472883712 | bytes 62914560 | tf_op jit(solution)/shard_map/tail/pallas_call | solution.py:839
  398.6 1.5 fusion.1
  400.1 0.7 slice_reduce_fusion.1
  400.8 4.2 fusion
  405.0 0.1 reshape_squeeze.3
  405.1 4.6 %spread.3 = bf16[736,2048]{1,0:T(8,128)(2,1)} custom-call(s32[1]{0:T(128)} %bitcast.part_ref, s32[1,2048]{1,0:T(1,128)S(1)} %copy-done.33, bf16[736,1024]{1,0:T(8,128)(2,1)S(1)} %copy-done.30, bf16[736,1024]{1,0:T(8,128)(2,1)S(1)} %copy-done.31), custom_call_target="tpu_custom_call" | custom-call | flops 2701131776 | bytes 6029312 | tf_op jit(solution)/shard_map/spread/pallas_call | solution.py:256
  409.7 4.6 %spread.2 = bf16[736,2048]{1,0:T(8,128)(2,1)} custom-call(s32[1]{0:T(128)} %bitcast.part_ref, s32[1,2048]{1,0:T(1,128)S(1)} %copy-done.33, bf16[736,1024]{1,0:T(8,128)(2,1)S(1)} %copy-done.28, bf16[736,1024]{1,0:T(8,128)(2,1)S(1)} %copy-done.29), custom_call_target="tpu_custom_call" | custom-call | flops 2701131776 | bytes 6029312 | tf_op jit(solution)/shard_map/spread/pallas_call | solution.py:256
  414.3 0.6 dynamic-slice_bitcast_fusion
  414.9 0.7 dynamic-slice_reduce_fusion
  415.6 0.8 copy.52
  (73 shorter events, 0.2 us)
Async XLA Ops:
  0.7 1.1 copy-start.14
  1.7 1.1 copy-start.15
  2.8 1.1 copy-start.16
  3.8 1.1 copy-start.17
  4.9 0.7 copy-start.20
  5.6 0.7 copy-start.23
  7.6 8.4 %copy-start.32 = (s32[1,2048]{1,0:T(1,128)}, s32[1,2048]{1,0:T(1,128)S(1)}, u32[]{:S(2)}) copy-start(s32[1,2048]{1,0:T(1,128)S(1)} %get-tuple-element.72.slot_ref) | copy-start | bytes 24580
  7.6 8.4 %collective-permute-start.1 = (bf16[4,192,1472]{2,1,0:T(8,128)(2,1)S(1)}, bf16[4,192,1472]{2,1,0:T(8,128)(2,1)S(1)}, u32[]{:S(2)}, u32[]{:S(2)}) collective-permute-start(bf16[4,192,1472]{2,1,0:T(8,128)(2,1)S(1)} %get-tuple-element.75.stack_ref), channel_id=1, source_target_pairs={{0,1},{1,0},{2,3},{3,2},{4,5},{5,4},{6,7},{7,6},{8,9},{9,8},{10,11... | collective-permute-start | bytes 6782984 | tf_op jit(solution)/shard_map/ppermute | solution.py:1627
  8.1 1.9 copy-start.24
  10.0 6.1 %copy-start.25 = (bf16[2048,736]{0,1:T(8,128)(2,1)S(1)}, bf16[2048,736]{0,1:T(8,128)(2,1)}, u32[]{:S(2)}) copy-start(bf16[2048,736]{0,1:T(8,128)(2,1)} %param.16) | copy-start | bytes 9043972
  14.8 1.1 copy-start.36
  16.0 18.4 %collective-permute-start = (bf16[736,1024]{1,0:T(8,128)(2,1)}, bf16[736,1024]{1,0:T(8,128)(2,1)}, u32[]{:S(2)}, u32[]{:S(2)}) collective-permute-start(bf16[736,1024]{1,0:T(8,128)(2,1)} %get-tuple-element.74), channel_id=1, source_target_pairs={{0,1},{1,0},{2,3},{3,2},{4,5},{5,4},{6,7},{7,6},{8,9},{9,8},{10,11... | collective-permute-start | bytes 4521992 | tf_op jit(solution)/shard_map/ppermute | solution.py:1627
  16.0 10.3 %copy-start.44 = (f32[32,3]{0,1:T(4,128)S(1)}, f32[32,3]{0,1:T(4,128)}, u32[]{:S(2)}) copy-start(f32[32,3]{0,1:T(4,128)} %param.24) | copy-start | bytes 1156
  16.0 10.8 %copy-start.43 = (bf16[1472]{0:T(1024)(128)(2,1)S(1)}, bf16[1472]{0:T(1024)(128)(2,1)}, u32[]{:S(2)}) copy-start(bf16[1472]{0:T(1024)(128)(2,1)} %param.25) | copy-start | bytes 8836
  16.1 10.8 %copy-start.41 = (f32[1472]{0:T(1024)S(1)}, f32[1472]{0:T(1024)}, u32[]{:S(2)}) copy-start(f32[1472]{0:T(1024)} %param.19) | copy-start | bytes 17668
  16.1 10.8 %copy-start.42 = (f32[1472]{0:T(1024)S(1)}, f32[1472]{0:T(1024)}, u32[]{:S(2)}) copy-start(f32[1472]{0:T(1024)} %param.26) | copy-start | bytes 17668
  24.1 1.7 copy-start.4
  25.8 35.1 %copy-start.2 = (bf16[384,1472]{1,0:T(8,128)(2,1)}, bf16[384,1472]{1,0:T(8,128)(2,1)S(1)}, u32[]{:S(2)}) copy-start(bf16[384,1472]{1,0:T(8,128)(2,1)S(1)} %get-tuple-element.83.weight_ref) | copy-start | bytes 3391492
  25.8 18.6 %collective-permute-start.3 = (bf16[736,1024]{1,0:T(8,128)(2,1)}, bf16[736,1024]{1,0:T(8,128)(2,1)}, u32[]{:S(2)}, u32[]{:S(2)}) collective-permute-start(bf16[736,1024]{1,0:T(8,128)(2,1)} %get-tuple-element.81.peer_ref), channel_id=1, source_target_pairs={{0,1},{1,0},{2,3},{3,2},{4,5},{5,4},{6,7},{7,6},{8,9},{9,8},{10,11... | collective-permute-start | bytes 4521992 | tf_op jit(solution)/shard_map/ppermute | solution.py:1627
  26.3 18.2 %collective-permute-start.4 = (bf16[736,1024]{1,0:T(8,128)(2,1)}, bf16[736,1024]{1,0:T(8,128)(2,1)}, u32[]{:S(2)}, u32[]{:S(2)}) collective-permute-start(bf16[736,1024]{1,0:T(8,128)(2,1)} %get-tuple-element.80.own_ref), channel_id=1, source_target_pairs={{0,1},{1,0},{2,3},{3,2},{4,5},{5,4},{6,7},{7,6},{8,9},{9,8},{10,11... | collective-permute-start | bytes 4521992 | tf_op jit(solution)/shard_map/ppermute | solution.py:1627
  26.4 2.9 collective-permute-start.2
  27.2 224.1 %copy-start = (f32[1472,3]{1,0:T(8,128)}, f32[1472,3]{1,0:T(8,128)S(1)}, u32[]{:S(2)}) copy-start(f32[1472,3]{1,0:T(8,128)S(1)} %copy.41.gain_ref.columns_ref) | copy-start | bytes 52996
  29.4 4.9 %copy-start.37 = (bf16[736,1024]{1,0:T(8,128)(2,1)S(1)}, bf16[736,1024]{1,0:T(8,128)(2,1)}, u32[]{:S(2)}) copy-start(bf16[736,1024]{1,0:T(8,128)(2,1)} %copy-done.36) | copy-start | bytes 4521988
  31.9 2.5 copy-start.1
  42.4 0.6 copy-start.22
  43.0 1.4 copy-start.34
  44.5 16.5 %copy-start.21 = (f32[1,1024]{1,0:T(1,128)}, f32[1,1024]{1,0:T(1,128)S(1)}, u32[]{:S(2)}) copy-start(f32[1,1024]{1,0:T(1,128)S(1)} %get-tuple-element.115.logit_ref) | copy-start | bytes 12292
  61.0 7.1 %copy-start.8 = (bf16[384,1024]{1,0:T(8,128)(2,1)}, bf16[384,1024]{1,0:T(8,128)(2,1)S(1)}, u32[]{:S(2)}) copy-start(bf16[384,1024]{1,0:T(8,128)(2,1)S(1)} %get-tuple-element.84.attended_ref) | copy-start | bytes 2359300
  68.1 1.7 copy-start.27
  248.0 45.2 %collective-permute-start.5 = (bf16[4,2,64,1472]{3,2,1,0:T(8,128)(2,1)}, bf16[4,2,64,1472]{3,2,1,0:T(8,128)(2,1)}, u32[]{:S(2)}, u32[]{:S(2)}) collective-permute-start(bf16[4,2,64,1472]{3,2,1,0:T(8,128)(2,1)} %get-tuple-element.109), channel_id=1, source_target_pairs={{0,2},{2,0},{4,6},{6,4},{8,10},{10,8},{12,14},{14,12},{16,18},{18,... | collective-permute-start | bytes 4521992 | tf_op jit(solution)/shard_map/ppermute | solution.py:1551
  249.8 43.4 %collective-permute-start.6 = (bf16[4,2,48,1472]{3,2,1,0:T(8,128)(2,1)}, bf16[4,2,48,1472]{3,2,1,0:T(8,128)(2,1)}, u32[]{:S(2)}, u32[]{:S(2)}) collective-permute-start(bf16[4,2,48,1472]{3,2,1,0:T(8,128)(2,1)} %get-tuple-element.111), channel_id=1, source_target_pairs={{0,4},{2,6},{4,0},{6,2},{8,12},{10,14},{12,8},{14,10},{16,20},{18,... | collective-permute-start | bytes 3391496 | tf_op jit(solution)/shard_map/ppermute | solution.py:1551
  251.3 1.3 copy-start.3
  252.6 13.8 %copy-start.35 = (f32[384,1024]{1,0:T(8,128)S(1)}, f32[384,1024]{1,0:T(8,128)}, u32[]{:S(2)}) copy-start(f32[384,1024]{1,0:T(8,128)} %get-tuple-element.100.wide_ref) | copy-start | bytes 4718596
  265.5 0.9 copy-start.13
  266.4 17.3 %copy-start.5 = (bf16[1472,1024]{1,0:T(8,128)(2,1)S(1)}, bf16[1472,1024]{1,0:T(8,128)(2,1)}, u32[]{:S(2)}) copy-start(bf16[1472,1024]{1,0:T(8,128)(2,1)} %get-tuple-element.104.normed_ref.normed_hbm) | copy-start | bytes 9043972
  266.4 17.3 %copy-start.9 = (bf16[384,1024]{1,0:T(8,128)(2,1)S(1)}, bf16[384,1024]{1,0:T(8,128)(2,1)}, u32[]{:S(2)}) copy-start(bf16[384,1024]{1,0:T(8,128)(2,1)} %copy-done.8) | copy-start | bytes 2359300
  266.4 17.4 %copy-start.26 = (bf16[1472,1024]{1,0:T(8,128)(2,1)S(1)}, bf16[1472,1024]{1,0:T(8,128)(2,1)}, u32[]{:S(2)}) copy-start(bf16[1472,1024]{1,0:T(8,128)(2,1)} %get-tuple-element.105.back_ref) | copy-start | bytes 9043972
  283.7 5.4 %copy-start.10 = (bf16[384,1024]{1,0:T(8,128)(2,1)}, bf16[384,1024]{1,0:T(8,128)(2,1)S(1)}, u32[]{:S(2)}) copy-start(bf16[384,1024]{1,0:T(8,128)(2,1)S(1)} %get-tuple-element.101.q_ref.q_hbm) | copy-start | bytes 2359300
  283.7 5.4 %copy-start.11 = (bf16[384,1024]{1,0:T(8,128)(2,1)}, bf16[384,1024]{1,0:T(8,128)(2,1)S(1)}, u32[]{:S(2)}) copy-start(bf16[384,1024]{1,0:T(8,128)(2,1)S(1)} %get-tuple-element.103.k_ref.k_hbm) | copy-start | bytes 2359300
  283.7 5.4 %copy-start.12 = (bf16[384,1024]{1,0:T(8,128)(2,1)}, bf16[384,1024]{1,0:T(8,128)(2,1)S(1)}, u32[]{:S(2)}) copy-start(bf16[384,1024]{1,0:T(8,128)(2,1)S(1)} %get-tuple-element.102.v_ref.v_hbm) | copy-start | bytes 2359300
  283.7 5.4 %copy-start.18 = (f32[6,8,1024]{2,1,0:T(8,128)}, f32[6,8,1024]{2,1,0:T(8,128)S(1)}, u32[]{:S(2)}) copy-start(f32[6,8,1024]{2,1,0:T(8,128)S(1)} %get-tuple-element.116.sums_ref) | copy-start | bytes 589828
  283.7 5.4 %copy-start.19 = (f32[6,32,128]{2,1,0:T(8,128)}, f32[6,32,128]{2,1,0:T(8,128)S(1)}, u32[]{:S(2)}) copy-start(f32[6,32,128]{2,1,0:T(8,128)S(1)} %get-tuple-element.113) | copy-start | bytes 294916
  283.8 6.8 %copy-start.38 = (f32[2,112,1472]{2,1,0:T(8,128)S(1)}, f32[2,112,1472]{2,1,0:T(8,128)}, u32[]{:S(2)}) copy-start(f32[2,112,1472]{2,1,0:T(8,128)} %get-tuple-element.128) | copy-start | bytes 3956740
  283.8 6.8 %copy-start.39 = (f32[2,112,1472]{2,1,0:T(8,128)S(1)}, f32[2,112,1472]{2,1,0:T(8,128)}, u32[]{:S(2)}) copy-start(f32[2,112,1472]{2,1,0:T(8,128)} %get-tuple-element.129) | copy-start | bytes 3956740
  289.1 1.5 copy-start.7
  290.6 1.4 copy-start.6
  400.8 4.3 %copy-start.30 = (bf16[736,1024]{1,0:T(8,128)(2,1)S(1)}, bf16[736,1024]{1,0:T(8,128)(2,1)}, u32[]{:S(2)}) copy-start(bf16[736,1024]{1,0:T(8,128)(2,1)} %get-tuple-element.124.own_ref) | copy-start | bytes 4521988
  400.8 4.3 %copy-start.31 = (bf16[736,1024]{1,0:T(8,128)(2,1)S(1)}, bf16[736,1024]{1,0:T(8,128)(2,1)}, u32[]{:S(2)}) copy-start(bf16[736,1024]{1,0:T(8,128)(2,1)} %get-tuple-element.125.peer_ref) | copy-start | bytes 4521988
  400.8 4.2 %copy-start.33 = (s32[1,2048]{1,0:T(1,128)S(1)}, s32[1,2048]{1,0:T(1,128)}, u32[]{:S(2)}) copy-start(s32[1,2048]{1,0:T(1,128)} %copy-done.32) | copy-start | bytes 24580
  405.1 4.6 %copy-start.28 = (bf16[736,1024]{1,0:T(8,128)(2,1)S(1)}, bf16[736,1024]{1,0:T(8,128)(2,1)}, u32[]{:S(2)}) copy-start(bf16[736,1024]{1,0:T(8,128)(2,1)} %get-tuple-element.122.own_ref) | copy-start | bytes 4521988
  405.1 4.6 %copy-start.29 = (bf16[736,1024]{1,0:T(8,128)(2,1)S(1)}, bf16[736,1024]{1,0:T(8,128)(2,1)}, u32[]{:S(2)}) copy-start(bf16[736,1024]{1,0:T(8,128)(2,1)} %get-tuple-element.123.peer_ref) | copy-start | bytes 4521988
  409.7 5.8 %copy-start.40 = (f32[112,1472]{1,0:T(8,128)S(1)}, f32[112,1472]{1,0:T(8,128)}, u32[]{:S(2)}) copy-start(f32[112,1472]{1,0:T(8,128)} %get-tuple-element.130) | copy-start | bytes 1978372

commit v4 on v3

--- a/solution.py
+++ b/solution.py
@@ -597,7 +597,7 @@
     mid_hbm, weight_hbm,
     out_ref, share_ref, vector_ref, own_ref, came_grad_ref, own_mixed_ref, came_mixed_ref,
     came_ref, total, from_x, from_y, sum_x, sum_y, last_x, last_y, plane_sum, from_planes,
-    give_x, give_y, second_x, second_y, whole, from_whole,
+    whole, from_whole,
     vector, vector_core, vector_near, vector_far, sent_grad, sent_mixed, block_hold,
     head_hold, half_hold, wide_hold, weight_ref, load_sems, weight_sem, send_sems, recv_sems,
 ):
@@ -650,8 +650,13 @@
         sender.start(give_ref.at[:, :, :, c], came_ref.at[:, :, :, c], at["to_core"])
         for c in chunks
     ]
-    give_x[...] = plus(keep_x[:, 1 - y], came_x[:, 1 - y]).astype(BF16)
-    give_y[...] = plus(keep_y[:, 1 - x], came_y[:, 1 - x]).astype(BF16)
+    cut = keep_x.shape[1]
+    whole[:, :cut] = plus(keep_x[...], came_x[...]).astype(BF16)
+    whole[:, cut:] = plus(keep_y[...], came_y[...]).astype(BF16)
+    wholes = [
+        sender.start(whole.at[p], from_whole.at[k], device)
+        for k, (p, device) in enumerate(zip(at["planes"], at["to_plane"]))
+    ]
 
     def first(c):
         arrived([cores[c]])
@@ -758,7 +763,6 @@
             ones, values, NT, preferred_element_type=F32, precision=lax.Precision.HIGHEST
         )[:1]
 
-    cut = keep_x.shape[2]
     advance(0, 0)
     compute(0)
     advance(0, 1)
@@ -771,10 +775,6 @@
     advance(0, 3)
     advance(1, 2)
     advance(2, 1)
-    seconds = [
-        sender.start(give_x, second_x, to_y),
-        sender.start(give_y, second_y, to_x),
-    ]
     compute(3)
     advance(0, 4)
     advance(1, 3)
@@ -789,13 +789,6 @@
     advance(1, 4)
     compute_mixed(0)
     advance(2, 3)
-    arrived(seconds)
-    whole[:, :cut] = plus(keep_x[:, y], came_x[:, y], second_x[...]).astype(BF16)
-    whole[:, cut:] = plus(keep_y[:, x], came_y[:, x], second_y[...]).astype(BF16)
-    wholes = [
-        sender.start(whole.at[p], from_whole.at[k], device)
-        for k, (p, device) in enumerate(zip(at["planes"], at["to_plane"]))
-    ]
     arrived(vectors)
     vector_core[...] = vector_core[...] + vector[...]
     vectors = [
@@ -827,7 +820,7 @@
 def tail(keep, give, up_x, up_y, ffn_sum, near, lines, far):
     rows = keep.shape[1] // 4
     (keep_x, came_x), (keep_y, came_y) = up_x, up_y
-    cut, rest = keep_x.shape[2], keep_y.shape[2]
+    cut, rest = keep_x.shape[1], keep_y.shape[1]
     share = cut + rest
     shape = (4, 2, 2, rows, D)
     copies = 80
@@ -851,7 +844,6 @@
             hold(*shape), hold(*shape), hold(2, 2, rows, D), hold(2, 2, rows, D),
             hold(2, 2, rows, D), hold(2, 2, rows, D), hold(2, rows, D), hold(2, rows, D),
             hold(4, rows, D), hold(3, rows, D),
-            hold(4, cut, D), hold(4, rest, D), hold(4, cut, D), hold(4, rest, D),
             hold(4, share, D), hold(3, share, D),
             hold(8, D, dtype=F32), hold(8, D, dtype=F32), hold(3, 8, D, dtype=F32),
             hold(3, 8, D, dtype=F32), hold(D // 2, LMAX), hold(D // 2, LMAX), hold(D, QBLOCK),
@@ -1698,6 +1690,11 @@
         grad_q, grad_k, grad_v, sums, near = attend_back(
             (), qkv, prob, grad_attended, wide, heads
         )
+        up_x, up_y, grad_q = lax.optimization_barrier((up_x, up_y, grad_q))
+        keep_x, give_x = fold(bit_of(1), *up_x)
+        keep_y, give_y = fold(bit_of(0), *up_y)
+        up_x = (keep_x, across(give_x, 1))
+        up_y = (keep_y, across(give_y, 0))
         keep, give = head_grads(part_ref, grad_q, grad_k, grad_v, normed_one, attended, grad_attn)
         totals, grad_up, small, state_own, state_came, mixed_own, mixed_came = tail(
             keep, give, up_x, up_y, sum_ffn, near.reshape(heads * BUCKETS, TILE),

time: 421 us -> 418 us (level)
  Pallas kernels: 376 us -> 360 us
  waiting for transfers between devices: 2.05 us -> 9.57 us
    pallas_call x1, Pallas kernels: 105 us -> 88.2 us  [tail(): pl.pallas_call(tail_kernel, name='tail', in_specs=[VMEM] * (8 + len(lines...]
    ppermute x2 -> x4, waiting for transfers between devices: 0.01 us -> 7.53 us  [across(): return lax.ppermute(values, 'dp', [(i, i ^ 1 << bit) for i in range(size)])]
    unnamed x91 -> x99, local copies, waits for them, and re-layouts: 22.3 us -> 25.6 us
  transfers between devices with their start and end apart: 7 -> 9, of which waited for: 1 -> 3; matrix products, arithmetic and copies ran while one was open for 0% -> 1% of each run, Pallas kernels for 14% -> 14%
where the time goes in v4:
time: 418 us; the launch traced here: 414 us
  Pallas kernels  360 us (86%)
  local copies, waits for them, and re-layouts  35.1 us (8%)
  waiting for transfers between devices  9.57 us (2%)
  starting transfers between devices  5.7 us (1%)
    pallas_call x2, Pallas kernels, feed(): pl.pallas_call(functools.partial(feed_kernel, half, cut), name='feed_forw...  178 us
    pallas_call x1, Pallas kernels, tail(): pl.pallas_call(tail_kernel, name='tail', in_specs=[VMEM] * (8 + len(lines...  88.2 us
    unnamed x99, local copies, waits for them, and re-layouts  25.6 us
    pallas_call x1, Pallas kernels, attend_back(): call(attend_back_kernel, 'attend_back', heads * 8 * LMAX * LMAX * HDIM *...  17 us
    pallas_call x1, Pallas kernels, attend(): call(attend_kernel, 'attend', heads * 4 * LMAX * LMAX * HDIM * 4, heads *...  16.5 us
    pallas_call x1, Pallas kernels, after_feed(): call(after_feed_kernel, 'norm_back', 2 * D * LMAX * inner, D * LMAX * 26,...  12.9 us
    pallas_call x2, Pallas kernels, spread(): call(spread_kernel, 'spread', 2 * width * 7168 * 256, width * 2048 * 4, 1...  9.15 us
  transfers between devices with their start and end apart: 9, of which 3 were waited for; matrix products, arithmetic and copies ran while one was open for 1% of the time, Pallas kernels for 14%

profile of v4, /device:TPU:0, one launch (start us, length us, event | category | flops | bytes accessed | tf_op | source)
XLA Modules:
  0.0 414.4 jit_solution(9333969364512471662)
XLA Ops:
  0.7 1.1 copy-done.17
  1.7 1.1 copy-done.18
  2.8 1.1 copy-done.19
  3.9 1.1 copy-done.20
  4.9 0.7 copy-done.24
  5.6 0.7 copy-done.27
  6.3 1.3 places.1
  7.6 0.5 collective-permute-start
  8.1 1.9 copy-done.28
  10.0 4.9 %compact.1 = (bf16[736,1024]{1,0:T(8,128)(2,1)S(1)}, bf16[736,1024]{1,0:T(8,128)(2,1)}) custom-call(s32[1]{0:T(128)} %bitcast.part_ref, s32[1,2048]{1,0:T(1,128)S(1)} %get-tuple-element.81.slot_ref, bf16[736,2048]{1,0:T(8,128)(2,1)S(1)} %bitcast.41), custom_call_target="tpu_custom_call" | custom-call | flops 3472883712 | bytes 6029312 | tf_op jit(solution)/shard_map/compact/pallas_call | solution.py:221
  14.8 1.1 copy-done.40
  16.0 0.1 collective-permute-start.1
  16.0 0.0 copy-start.48
  16.1 8.0 %compact_join.1 = (bf16[736,1024]{1,0:T(8,128)(2,1)}, bf16[736,1024]{1,0:T(8,128)(2,1)}, bf16[1152,1472]{1,0:T(8,128)(2,1)S(1)}, bf16[384,1472]{1,0:T(8,128)(2,1)S(1)}) custom-call(s32[1]{0:T(128)} %bitcast.part_ref, s32[1,2048]{1,0:T(1,128)S(1)} %get-tuple-element.81.slot_ref, bf16[736,2048]{1,0:T(8,128)(2,1)S(1)} %bitcast.42, ...), custom_call_target="tpu_custom_call" | custom-call | flops 3472883712 | bytes 6029312 | tf_op jit(solution)/shard_map/compact_join/pallas_call | solution.py:198
  24.1 1.7 copy-done.4
  25.8 0.5 collective-permute-start.3
  26.3 0.1 collective-permute-start.4
  26.4 0.5 collective-permute-start.2
  26.9 0.3 copy.41.gain_ref.columns_ref
  27.2 2.0 collective-permute-done.2
  29.3 0.1 copy.42
  29.3 0.1 copy.43
  29.4 2.4 bias_strip.1.strip_ref
  31.9 2.5 copy-done.1
  34.3 8.1 %norm_project.1 = (bf16[1472,1024]{1,0:T(8,128)(2,1)}, bf16[1472,1024]{1,0:T(8,128)(2,1)}, bf16[1152,1024]{1,0:T(8,128)(2,1)S(1)}, bf16[16,1024]{1,0:T(8,128)(2,...) custom-call(s32[1]{0:T(128)} %bitcast.part_ref, bf16[736,1024]{1,0:T(8,128)(2,1)S(1)} %copy-done.41, ...), custom_call_target="tpu_custom_call" | custom-call | flops 3472883712 | bytes 15073280 | tf_op jit(solution)/shard_map/norm_project/pallas_call | solution.py:318
  42.4 0.6 copy-done.26
  43.0 1.4 copy-done.38
  44.5 16.5 %attend.1 = (bf16[6,1024,1024]{2,1,0:T(8,128)(2,1)}, bf16[384,1024]{1,0:T(8,128)(2,1)S(1)}, f32[384,1024]{1,0:T(8,128)}, bf16[1472,1024]{1,0:T(8,128)(2,1)}, bf16[1472,1024]{1,0:T(8,128)(2,1)}) custom-call(s32[1]{0:T(128)} %bitcast.part_ref, bf16[1152,1024]{1,0:T(8,128)(2,1)} %copy-done.38, bf16[1152,1024]{1,0:T(8,128)(2,1)} %copy-done.38, ...), custom_call_target="tpu_custom_call" | custom-call | flops 6442450944 | bytes 12582912 | tf_op jit(solution)/shard_map/attend/pallas_call | solution.py:1296
  61.0 7.1 %attention_out_norm.1 = (f32[1472,1024]{1,0:T(8,128)}, bf16[1472,1024]{1,0:T(8,128)(2,1)S(1)}, f32[1,1024]{1,0:T(1,128)S(1)}) custom-call(bf16[384,1472]{1,0:T(8,128)(2,1)S(1)} %get-tuple-element.83.weight_ref, bf16[384,1024]{1,0:T(8,128)(2,1)S(1)} %get-tuple-element.92.attended_ref, bf16[1472,1024]{1,0:T(8,128)(2,1)} %get-tuple-element.93.state_ref.state_hbm, ...), custom_call_target="tpu_custom_call" | custom-call | flops 1157627904 | bytes 12058624 | tf_op jit(solution)/shard_map/attention_out_norm/pallas_call | solution.py:348
  68.1 1.7 copy-done.31
  69.8 87.0 %feed_forward.2 = (bf16[1472,1024]{1,0:T(8,128)(2,1)}, bf16[1472,1024]{1,0:T(8,128)(2,1)}, bf16[1472,1024]{1,0:T(8,128)(2,1)}, bf16[1472,1024]{1,0:T(8,128)(2,1)...) custom-call(bf16[1472,1792]{1,0:T(8,128)(2,1)} %refs_0_.3, ...), custom_call_target="tpu_custom_call" | custom-call | flops 48620371968 | bytes 62914560 | tf_op jit(solution)/shard_map/feed_forward/pallas_call | solution.py:1127
  156.8 91.2 %feed_forward.3 = (bf16[1472,1024]{1,0:T(8,128)(2,1)}, bf16[1472,1024]{1,0:T(8,128)(2,1)}, bf16[1472,1024]{1,0:T(8,128)(2,1)}, bf16[1472,1024]{1,0:T(8,128)(2,1)...) custom-call(bf16[1472,1792]{1,0:T(8,128)(2,1)} %refs_0_.3, ...), custom_call_target="tpu_custom_call", output_to_operand_aliasing={{4}: (6, {}), {5}: (7, {}), {6}: (8, {}), {7}: (9, {})} | custom-call | flops 48620371968 | bytes 62914560 | tf_op jit(solution)/shard_map/feed_forward/pallas_call | solution.py:1127
  248.0 1.8 collective-permute-start.5
  249.9 1.6 collective-permute-start.6
  251.4 2.7 broadcast_select_fusion
  254.1 12.9 %norm_back.1 = (f32[1472,1024]{1,0:T(8,128)}, bf16[1472,1024]{1,0:T(8,128)(2,1)}, bf16[384,1024]{1,0:T(8,128)(2,1)S(1)}, f32[1472,128]{1,0:T(8,128)S(1)}) custom-call(bf16[1472,1024]{1,0:T(8,128)(2,1)} %get-tuple-element.106.own_one, bf16[1472,1024]{1,0:T(8,128)(2,1)} %get-tuple-element.107.own_two, bf16[1472,1024]{1,0:T(8,128)(2,1)} %get-tuple-element.108.came_one, ...), custom_call_target="tpu_custom_call" | custom-call | flops 1157627904 | bytes 39190528 | tf_op jit(solution)/shard_map/norm_back/pallas_call | solution.py:1184
  267.0 0.9 copy-done.16
  267.9 17.0 %attend_back.1 = (bf16[384,1024]{1,0:T(8,128)(2,1)S(1)}, bf16[384,1024]{1,0:T(8,128)(2,1)S(1)}, bf16[384,1024]{1,0:T(8,128)(2,1)S(1)}, f32[6,8,1024]{2,1,0:T(8,128)S(1)}, f32[6,32,128]{2,1,0:T(8,128)S(1)}) custom-call(bf16[1152,1024]{1,0:T(8,128)(2,1)} %copy-done.38, bf16[1152,1024]{1,0:T(8,128)(2,1)} %copy-done.38, bf16[1152,1024]{1,0:T(8,128)(2,1)} %copy-done.38, ...), custom_call_target="tpu_custom_call" | custom-call | flops 12884901888 | bytes 12582912 | tf_op jit(solution)/shard_map/attend_back/pallas_call | solution.py:1398
  285.0 0.7 copy-done.22
  285.6 0.6 copy-done.23
  286.3 0.3 fold.3
  286.7 0.8 copy-done.21
  287.5 0.2 collective-permute-start.8
  287.7 1.0 copy-done.8
  288.8 0.6 fold.2
  289.4 0.5 collective-permute-start.7
  289.9 1.2 slice_bitcast_fusion
  291.1 0.4 copy-done.11
  291.5 5.2 %head_grads.1 = (bf16[4,192,1472]{2,1,0:T(8,128)(2,1)S(1)}, bf16[4,192,1472]{2,1,0:T(8,128)(2,1)S(1)}) custom-call(s32[1]{0:T(128)} %bitcast.part_ref, bf16[384,1024]{1,0:T(8,128)(2,1)S(1)} %get-tuple-element.115.q_ref.q_hbm, bf16[384,1024]{1,0:T(8,128)(2,1)S(1)} %get-tuple-element.116.v_ref.v_hbm, bf16[384,1024]{1,0:T(8,128)(2,1)S(1)} %get-tuple-element.117.k_ref.k_hbm, ...), custom_call_target="tpu_custom_call" | custom-call | flops 4630511616 | bytes 18219008 | tf_op jit(solution)/shard_map/head_grads/pallas_call | solution.py:513
  296.8 1.4 copy-done.6
  298.2 1.5 copy-done.7
  299.7 1.4 collective-permute-done.8.came_y
  301.1 6.1 %collective-permute-done.7.came_x = bf16[4,64,1472]{2,1,0:T(8,128)(2,1)S(1)} collective-permute-done((bf16[4,64,1472]{2,1,0:T(8,128)(2,1)S(1)}, bf16[4,64,1472]{2,1,0:T(8,128)(2,1)S(1)}, u32[]{:S(2)}, u32[]{:S(2)}) %collective-permute-start.7) | collective-permute-done | bytes 753696 | tf_op jit(solution)/shard_map/ppermute | solution.py:1543
  307.2 0.9 copy-done.43
  308.1 88.2 %tail.1 = (bf16[4,2,2,48,1472]{4,3,2,1,0:T(8,128)(2,1)}, f32[112,1472]{1,0:T(8,128)}, f32[8,1472]{1,0:T(8,128)}, bf16[736,1024]{1,0:T(8,128)(2,1)}, bf16[736,102...) custom-call(bf16[4,2,2,48,1472]{4,3,2,1,0:T(8,128)(2,1)} %bitcast.34, ...), custom_call_target="tpu_custom_call" | custom-call | flops 3472883712 | bytes 62914560 | tf_op jit(solution)/shard_map/tail/pallas_call | solution.py:832
  396.3 1.7 fusion.1
  398.0 0.7 slice_reduce_fusion.1
  398.7 4.2 %fusion = (f32[1,2,2,48,1472]{4,3,2,1,0:T(8,128)}, f32[1,2,2,48,1472]{4,3,2,1,0:T(8,128)}, f32[1,2,2,48,1472]{4,3,2,1,0:T(8,128)}, f32[1,2,2,48,1472]{4,3,2,1,0:T(8,128)}) fusion(bf16[4,2,2,48,1472]{4,3,2,1,0:T(8,128)(2,1)} %get-tuple-element.145), kind=kLoop, calls=%fused_computation.12 | loop fusion | bytes 9043968 | tf_op jit(solution)/shard_map/unstack | solution.py:1708
  402.8 0.1 reshape_squeeze.3
  403.0 4.6 %spread.3 = bf16[736,2048]{1,0:T(8,128)(2,1)} custom-call(s32[1]{0:T(128)} %bitcast.part_ref, s32[1,2048]{1,0:T(1,128)S(1)} %copy-done.37, bf16[736,1024]{1,0:T(8,128)(2,1)S(1)} %copy-done.34, bf16[736,1024]{1,0:T(8,128)(2,1)S(1)} %copy-done.35), custom_call_target="tpu_custom_call" | custom-call | flops 2701131776 | bytes 6029312 | tf_op jit(solution)/shard_map/spread/pallas_call | solution.py:256
  407.6 4.6 %spread.2 = bf16[736,2048]{1,0:T(8,128)(2,1)} custom-call(s32[1]{0:T(128)} %bitcast.part_ref, s32[1,2048]{1,0:T(1,128)S(1)} %copy-done.37, bf16[736,1024]{1,0:T(8,128)(2,1)S(1)} %copy-done.32, bf16[736,1024]{1,0:T(8,128)(2,1)S(1)} %copy-done.33), custom_call_target="tpu_custom_call" | custom-call | flops 2701131776 | bytes 6029312 | tf_op jit(solution)/shard_map/spread/pallas_call | solution.py:256
  412.1 0.6 dynamic-slice_bitcast_fusion
  412.7 0.7 dynamic-slice_reduce_fusion
  413.4 0.8 copy.52
  (87 shorter events, 0.2 us)
Async XLA Ops:
  0.7 1.1 copy-start.17
  1.7 1.1 copy-start.18
  2.8 1.1 copy-start.19
  3.8 1.1 copy-start.20
  4.9 0.7 copy-start.24
  5.6 0.7 copy-start.27
  7.6 8.4 %copy-start.36 = (s32[1,2048]{1,0:T(1,128)}, s32[1,2048]{1,0:T(1,128)S(1)}, u32[]{:S(2)}) copy-start(s32[1,2048]{1,0:T(1,128)S(1)} %get-tuple-element.81.slot_ref) | copy-start | bytes 24580
  7.6 8.4 %collective-permute-start = (bf16[4,192,1472]{2,1,0:T(8,128)(2,1)S(1)}, bf16[4,192,1472]{2,1,0:T(8,128)(2,1)S(1)}, u32[]{:S(2)}, u32[]{:S(2)}) collective-permute-start(bf16[4,192,1472]{2,1,0:T(8,128)(2,1)S(1)} %get-tuple-element.82.stack_ref), channel_id=1, source_target_pairs={{0,1},{1,0},{2,3},{3,2},{4,5},{5,4},{6,7},{7,6},{8,9},{9,8},{10,11... | collective-permute-start | bytes 6782984 | tf_op jit(solution)/shard_map/ppermute | solution.py:1619
  8.1 1.9 copy-start.28
  10.0 6.1 %copy-start.29 = (bf16[2048,736]{0,1:T(8,128)(2,1)S(1)}, bf16[2048,736]{0,1:T(8,128)(2,1)}, u32[]{:S(2)}) copy-start(bf16[2048,736]{0,1:T(8,128)(2,1)} %param.16) | copy-start | bytes 9043972
  14.8 1.1 copy-start.40
  16.0 18.4 %collective-permute-start.1 = (bf16[736,1024]{1,0:T(8,128)(2,1)}, bf16[736,1024]{1,0:T(8,128)(2,1)}, u32[]{:S(2)}, u32[]{:S(2)}) collective-permute-start(bf16[736,1024]{1,0:T(8,128)(2,1)} %get-tuple-element.85), channel_id=1, source_target_pairs={{0,1},{1,0},{2,3},{3,2},{4,5},{5,4},{6,7},{7,6},{8,9},{9,8},{10,11... | collective-permute-start | bytes 4521992 | tf_op jit(solution)/shard_map/ppermute | solution.py:1619
  16.0 10.3 %copy-start.48 = (f32[32,3]{0,1:T(4,128)S(1)}, f32[32,3]{0,1:T(4,128)}, u32[]{:S(2)}) copy-start(f32[32,3]{0,1:T(4,128)} %param.24) | copy-start | bytes 1156
  16.0 10.8 %copy-start.47 = (bf16[1472]{0:T(1024)(128)(2,1)S(1)}, bf16[1472]{0:T(1024)(128)(2,1)}, u32[]{:S(2)}) copy-start(bf16[1472]{0:T(1024)(128)(2,1)} %param.25) | copy-start | bytes 8836
  16.1 10.8 %copy-start.45 = (f32[1472]{0:T(1024)S(1)}, f32[1472]{0:T(1024)}, u32[]{:S(2)}) copy-start(f32[1472]{0:T(1024)} %param.19) | copy-start | bytes 17668
  16.1 10.8 %copy-start.46 = (f32[1472]{0:T(1024)S(1)}, f32[1472]{0:T(1024)}, u32[]{:S(2)}) copy-start(f32[1472]{0:T(1024)} %param.26) | copy-start | bytes 17668
  24.1 1.7 copy-start.4
  25.8 35.1 %copy-start.2 = (bf16[384,1472]{1,0:T(8,128)(2,1)}, bf16[384,1472]{1,0:T(8,128)(2,1)S(1)}, u32[]{:S(2)}) copy-start(bf16[384,1472]{1,0:T(8,128)(2,1)S(1)} %get-tuple-element.83.weight_ref) | copy-start | bytes 3391492
  25.8 18.6 %collective-permute-start.3 = (bf16[736,1024]{1,0:T(8,128)(2,1)}, bf16[736,1024]{1,0:T(8,128)(2,1)}, u32[]{:S(2)}, u32[]{:S(2)}) collective-permute-start(bf16[736,1024]{1,0:T(8,128)(2,1)} %get-tuple-element.91.peer_ref), channel_id=1, source_target_pairs={{0,1},{1,0},{2,3},{3,2},{4,5},{5,4},{6,7},{7,6},{8,9},{9,8},{10,11... | collective-permute-start | bytes 4521992 | tf_op jit(solution)/shard_map/ppermute | solution.py:1619
  26.3 18.2 %collective-permute-start.4 = (bf16[736,1024]{1,0:T(8,128)(2,1)}, bf16[736,1024]{1,0:T(8,128)(2,1)}, u32[]{:S(2)}, u32[]{:S(2)}) collective-permute-start(bf16[736,1024]{1,0:T(8,128)(2,1)} %get-tuple-element.90.own_ref), channel_id=1, source_target_pairs={{0,1},{1,0},{2,3},{3,2},{4,5},{5,4},{6,7},{7,6},{8,9},{9,8},{10,11... | collective-permute-start | bytes 4521992 | tf_op jit(solution)/shard_map/ppermute | solution.py:1619
  26.4 2.9 collective-permute-start.2
  27.2 226.9 %copy-start = (f32[1472,3]{1,0:T(8,128)}, f32[1472,3]{1,0:T(8,128)S(1)}, u32[]{:S(2)}) copy-start(f32[1472,3]{1,0:T(8,128)S(1)} %copy.41.gain_ref.columns_ref) | copy-start | bytes 52996
  29.4 4.9 %copy-start.41 = (bf16[736,1024]{1,0:T(8,128)(2,1)S(1)}, bf16[736,1024]{1,0:T(8,128)(2,1)}, u32[]{:S(2)}) copy-start(bf16[736,1024]{1,0:T(8,128)(2,1)} %copy-done.40) | copy-start | bytes 4521988
  31.9 2.5 copy-start.1
  42.4 0.6 copy-start.26
  43.0 1.4 copy-start.38
  44.5 16.5 %copy-start.25 = (f32[1,1024]{1,0:T(1,128)}, f32[1,1024]{1,0:T(1,128)S(1)}, u32[]{:S(2)}) copy-start(f32[1,1024]{1,0:T(1,128)S(1)} %get-tuple-element.133.logit_ref) | copy-start | bytes 12292
  61.0 7.1 %copy-start.10 = (bf16[384,1024]{1,0:T(8,128)(2,1)}, bf16[384,1024]{1,0:T(8,128)(2,1)S(1)}, u32[]{:S(2)}) copy-start(bf16[384,1024]{1,0:T(8,128)(2,1)S(1)} %get-tuple-element.92.attended_ref) | copy-start | bytes 2359300
  68.1 1.7 copy-start.31
  248.0 38.3 %collective-permute-start.5 = (bf16[4,2,64,1472]{3,2,1,0:T(8,128)(2,1)}, bf16[4,2,64,1472]{3,2,1,0:T(8,128)(2,1)S(1)}, u32[]{:S(2)}, u32[]{:S(2)}) collective-permute-start(bf16[4,2,64,1472]{3,2,1,0:T(8,128)(2,1)} %get-tuple-element.102), channel_id=1, source_target_pairs={{0,2},{2,0},{4,6},{6,4},{8,10},{10,8},{12,14},{14,12},{16,18},{18,... | collective-permute-start | bytes 4521992 | tf_op jit(solution)/shard_map/ppermute | solution.py:1543
  249.9 36.4 %collective-permute-start.6 = (bf16[4,2,48,1472]{3,2,1,0:T(8,128)(2,1)}, bf16[4,2,48,1472]{3,2,1,0:T(8,128)(2,1)S(1)}, u32[]{:S(2)}, u32[]{:S(2)}) collective-permute-start(bf16[4,2,48,1472]{3,2,1,0:T(8,128)(2,1)} %get-tuple-element.104), channel_id=1, source_target_pairs={{0,4},{2,6},{4,0},{6,2},{8,12},{10,14},{12,8},{14,10},{16,20},{18,... | collective-permute-start | bytes 3391496 | tf_op jit(solution)/shard_map/ppermute | solution.py:1543
  251.4 2.7 copy-start.3
  254.1 13.8 %copy-start.39 = (f32[384,1024]{1,0:T(8,128)S(1)}, f32[384,1024]{1,0:T(8,128)}, u32[]{:S(2)}) copy-start(f32[384,1024]{1,0:T(8,128)} %get-tuple-element.113.wide_ref) | copy-start | bytes 4718596
  267.0 0.9 copy-start.16
  267.9 18.4 %copy-start.9 = (bf16[4,2,48,1472]{3,2,1,0:T(8,128)(2,1)S(1)}, bf16[4,2,48,1472]{3,2,1,0:T(8,128)(2,1)}, u32[]{:S(2)}) copy-start(bf16[4,2,48,1472]{3,2,1,0:T(8,128)(2,1)} %get-tuple-element.126.keep_ref) | copy-start | bytes 3391492
  267.9 23.2 %copy-start.30 = (bf16[1472,1024]{1,0:T(8,128)(2,1)S(1)}, bf16[1472,1024]{1,0:T(8,128)(2,1)}, u32[]{:S(2)}) copy-start(bf16[1472,1024]{1,0:T(8,128)(2,1)} %get-tuple-element.119.back_ref) | copy-start | bytes 9043972
  285.0 0.7 copy-start.22
  285.6 0.6 copy-start.23
  286.3 4.8 %copy-start.12 = (bf16[384,1024]{1,0:T(8,128)(2,1)}, bf16[384,1024]{1,0:T(8,128)(2,1)S(1)}, u32[]{:S(2)}) copy-start(bf16[384,1024]{1,0:T(8,128)(2,1)S(1)} %get-tuple-element.115.q_ref.q_hbm) | copy-start | bytes 2359300
  286.3 4.8 %copy-start.13 = (bf16[384,1024]{1,0:T(8,128)(2,1)}, bf16[384,1024]{1,0:T(8,128)(2,1)S(1)}, u32[]{:S(2)}) copy-start(bf16[384,1024]{1,0:T(8,128)(2,1)S(1)} %get-tuple-element.117.k_ref.k_hbm) | copy-start | bytes 2359300
  286.3 4.8 %copy-start.14 = (bf16[384,1024]{1,0:T(8,128)(2,1)}, bf16[384,1024]{1,0:T(8,128)(2,1)S(1)}, u32[]{:S(2)}) copy-start(bf16[384,1024]{1,0:T(8,128)(2,1)S(1)} %get-tuple-element.116.v_ref.v_hbm) | copy-start | bytes 2359300
  286.3 2.5 copy-start.8
  286.3 3.6 copy-start.42
  286.7 0.8 copy-start.21
  287.5 13.6 %collective-permute-start.8 = (bf16[4,48,1472]{2,1,0:T(8,128)(2,1)S(1)}, bf16[4,48,1472]{2,1,0:T(8,128)(2,1)}, u32[]{:S(2)}, u32[]{:S(2)}) collective-permute-start(bf16[4,48,1472]{2,1,0:T(8,128)(2,1)S(1)} %get-tuple-element.129), channel_id=1, source_target_pairs={{0,2},{2,0},{4,6},{6,4},{8,10},{10,8},{12,14},{14,12},{16,18},{18,... | collective-permute-start | bytes 1695752 | tf_op jit(solution)/shard_map/ppermute | solution.py:1543
  288.8 2.4 copy-start.5
  289.4 7.4 %copy-start.15 = (bf16[4,64,1472]{2,1,0:T(8,128)(2,1)}, bf16[4,64,1472]{2,1,0:T(8,128)(2,1)S(1)}, u32[]{:S(2)}) copy-start(bf16[4,64,1472]{2,1,0:T(8,128)(2,1)S(1)} %get-tuple-element.124.keep_x) | copy-start | bytes 2260996
  289.4 2.1 copy-start.11
  289.4 17.8 %collective-permute-start.7 = (bf16[4,64,1472]{2,1,0:T(8,128)(2,1)S(1)}, bf16[4,64,1472]{2,1,0:T(8,128)(2,1)S(1)}, u32[]{:S(2)}, u32[]{:S(2)}) collective-permute-start(bf16[4,64,1472]{2,1,0:T(8,128)(2,1)S(1)} %get-tuple-element.125), channel_id=1, source_target_pairs={{0,4},{2,6},{4,0},{6,2},{8,12},{10,14},{12,8},{14,10},{16,20},{18,... | collective-permute-start | bytes 2261000 | tf_op jit(solution)/shard_map/ppermute | solution.py:1543
  296.8 1.4 copy-start.6
  298.2 1.5 copy-start.7
  307.2 0.9 copy-start.43
  398.7 4.3 %copy-start.34 = (bf16[736,1024]{1,0:T(8,128)(2,1)S(1)}, bf16[736,1024]{1,0:T(8,128)(2,1)}, u32[]{:S(2)}) copy-start(bf16[736,1024]{1,0:T(8,128)(2,1)} %get-tuple-element.142.own_ref) | copy-start | bytes 4521988
  398.7 4.3 %copy-start.35 = (bf16[736,1024]{1,0:T(8,128)(2,1)S(1)}, bf16[736,1024]{1,0:T(8,128)(2,1)}, u32[]{:S(2)}) copy-start(bf16[736,1024]{1,0:T(8,128)(2,1)} %get-tuple-element.143.peer_ref) | copy-start | bytes 4521988
  398.7 4.2 %copy-start.37 = (s32[1,2048]{1,0:T(1,128)S(1)}, s32[1,2048]{1,0:T(1,128)}, u32[]{:S(2)}) copy-start(s32[1,2048]{1,0:T(1,128)} %copy-done.36) | copy-start | bytes 24580
  402.9 4.6 %copy-start.32 = (bf16[736,1024]{1,0:T(8,128)(2,1)S(1)}, bf16[736,1024]{1,0:T(8,128)(2,1)}, u32[]{:S(2)}) copy-start(bf16[736,1024]{1,0:T(8,128)(2,1)} %get-tuple-element.140.own_ref) | copy-start | bytes 4521988
  402.9 4.6 %copy-start.33 = (bf16[736,1024]{1,0:T(8,128)(2,1)S(1)}, bf16[736,1024]{1,0:T(8,128)(2,1)}, u32[]{:S(2)}) copy-start(bf16[736,1024]{1,0:T(8,128)(2,1)} %get-tuple-element.141.peer_ref) | copy-start | bytes 4521988
  407.6 5.8 %copy-start.44 = (f32[112,1472]{1,0:T(8,128)S(1)}, f32[112,1472]{1,0:T(8,128)}, u32[]{:S(2)}) copy-start(f32[112,1472]{1,0:T(8,128)} %get-tuple-element.148) | copy-start | bytes 1978372
